TPU v7x, 128 devices: a whole 4x4x4 slice. The times are simulated.
128 devices in a mesh: row: 8 (over x, core), col: 16 (over z, y).
Axes of the slice: x: 4, y: 4, z: 4, core: 2. Of those that a mesh axis runs over, the one named last changes fastest.
Arguments:
- values: bfloat16 [1024, 60416], P('col', 'row'), as said below
- pattern: int32 [944, 16], P(None, 'col'), may hold values from 0 to 943, as said below
Outputs:
- squared: bfloat16 [1024, 60416], P('col', 'row')
- updated: bfloat16 [1024, 60416], P('col', 'row')
Inputs may be any that keep to these rules, and one draw needn't show every extreme that they name: pattern[r, g] lies in the group g * 59 to (g + 1) * 59 - 1; pattern[r, r // 59] = r; the pattern is symmetric: pattern[pattern[r, g], r // 59] = r. values define a symmetric matrix: the block stored for block row r in group g is exactly the transpose of the block stored for block row pattern[r, g] in group r // 59.
All inputs are finite; a program needn't handle non-finite values.
Results may differ from a plain program's by a relative error of at most 0.0047.
Values may be sent and summed in bfloat16 or wider, within the bound.
No kernel may reach another device: no remote copies, remote signals or barrier semaphores. Data moves between devices by JAX's collectives and lax.ppermute only.
A program may use at most 320 MiB of HBM per device.

v0:
```python
import math

import jax
import jax.numpy as jnp
from jax import lax
from jax.experimental import pallas as pl
from jax.experimental.pallas import tpu as pltpu
from jax.sharding import PartitionSpec as P

TURNS = (0, -1, 1, 2)
CORES = 2
SIDE = 4
DIGIT = 32
CHUNK = 12
STEP = 6
WEIGHT = 48
ROWS = 16
MIB = 1024 * 1024


def pair_columns(values, links, spans, halves):
    block = values.shape[0]
    lanes = 2 * block

    def body(flat_ref, links_ref, whole_ref, *half_refs):
        for (start, size), ref in zip(halves, half_refs):
            for m in range(start, start + size):
                first = flat_ref[:, m * block : (m + 1) * block]
                second = flat_ref[:, (spans + m) * block : (spans + m + 1) * block]
                both = jnp.concatenate([first, second], axis=1)
                whole_ref[m] = both
                ref[m - start] = both
        row = lax.broadcasted_iota(jnp.int32, (block, lanes), 0)
        numbers = jnp.broadcast_to(links_ref[...], (block, lanes))
        digits = jnp.where(row == 0, numbers // DIGIT, numbers % DIGIT)
        half_refs[0][halves[0][1]] = digits.astype(jnp.float32).astype(values.dtype)

    sizes = [spans, halves[0][1] + 1, halves[1][1]]
    padded = jnp.pad(links, (0, lanes - links.shape[0])).reshape(1, lanes)
    return pl.pallas_call(
        body,
        out_shape=[jax.ShapeDtypeStruct((size, block, lanes), values.dtype) for size in sizes],
        compiler_params=pltpu.CompilerParams(vmem_limit_bytes=16 * MIB),
    )(values, padded)


def join_columns(pick, flat_ref, spans, block):
    for m in range(spans):
        both = pick(m)
        flat_ref[:, m * block : (m + 1) * block] = both[:, :block]
        flat_ref[:, (spans + m) * block : (spans + m + 1) * block] = both[:, block:]


def sent_row(array, turn, swap):
    chips = lax.axis_size("row") // CORES
    order = [
        (x * CORES + c, ((x - turn) % chips) * CORES + (c + swap) % CORES)
        for x in range(chips)
        for c in range(CORES)
    ]
    return lax.ppermute(array, "row", order)


def sent_col(array, turn, axis):
    step = (turn, 0) if axis == 0 else (0, turn)
    order = [
        (z * SIDE + y, ((z - step[0]) % SIDE) * SIDE + (y - step[1]) % SIDE)
        for z in range(SIDE)
        for y in range(SIDE)
    ]
    return lax.ppermute(array, "col", order)


def ring(array, sent, nearest=None):
    size = array.shape[0]
    half = (size + 1) // 2
    behind, ahead = nearest or (sent(array, -1), sent(array, 1))
    low = sent(lax.slice_in_dim(ahead, 0, half, axis=0), 1)
    high = sent(lax.slice_in_dim(behind, half, size, axis=0), -1)
    return [(array, 0, 0), (behind, 1, 0), (ahead, 2, 0), (low, 3, 0), (high, 3, half)]


def col_ring(array, axis):
    return ring(array, lambda x, turn: sent_col(x, turn, axis))


def row_slab(array, strips):
    behind, ahead, swapped = sent_row(array, -1, 0), sent_row(array, 1, 0), sent_row(array, 0, 1)
    nearest = lax.optimization_barrier((behind, ahead, swapped))
    near = ring(array, lambda x, turn: sent_row(x, turn, 0), nearest[:2])
    slab = []
    for piece, turn, begin in near:
        end, at, ranges = begin + piece.shape[0], 0, []
        for start, size in strips:
            low, high = max(at, begin), min(at + size, end)
            if low < high:
                ranges.append((low - begin, start + low - at, high - low))
            at += size
        slab.append((piece, turn * CORES, ranges))
        other = nearest[2] if turn == 0 else sent_row(piece, 0, 1)
        slab.append((other, turn * CORES + 1, ranges))
    return slab


def swapped_slab(chips):
    size = chips[0].shape[0]
    swapped = sent_row(jnp.concatenate(chips, axis=0), 0, 1)
    slab = []
    for step, x in enumerate(chips):
        place = CORES * TURNS.index((step + 1) % SIDE - 1)
        slab += [(x, place, [(0, 0, size)]), (swapped, place + 1, [(step * size, 0, size)])]
    return slab


def slab_copies(refs, slab, rows_ref, left_ref, sems):
    copies = []
    for ref, (_, place, ranges) in zip(refs, slab):
        for offset, start, size in ranges:
            source = ref.at[pl.ds(offset, size)]
            target = left_ref.at[rows_ref[place], pl.ds(start, size)]
            copies.append(pltpu.make_async_copy(source, target, sems.at[len(copies)]))
    return copies


def pieces_of(size, strip):
    edges = list(range(STEP if strip == 0 else 0, size, CHUNK))
    edges = sorted({0, *edges, size})
    return [(a, b - a) for a, b in zip(edges[:-1], edges[1:])]


def panel_copies(refs, panels, starts, strips, more, groups_ref, right_ref, sems):
    runs, used = [], 0
    for strip, (refs_here, (pieces, axis), at, (member, size)) in enumerate(zip(refs, panels, starts, strips)):
        stride = size + (more if strip == 0 else 0)
        for a, some in pieces_of(size, strip):
            copies = []
            for ref, (array, second, begin) in zip(refs_here, pieces):
                for first in range(SIDE):
                    offset = first * stride - begin
                    if 0 <= offset < array.shape[0]:
                        slot = first * SIDE + second if axis == 0 else second * SIDE + first
                        source = ref.at[pl.ds(offset + a, some)]
                        target = right_ref.at[groups_ref[slot], pl.ds(at + a, some)]
                        copies.append(pltpu.make_async_copy(source, target, sems.at[used]))
                        used += 1
            runs.append((copies, member + a, at + a, some))
    return runs


def panel_moves(strips):
    return SIDE * SIDE * sum(len(pieces_of(size, i)) for i, (_, size) in enumerate(strips))


def block_sums(table_ref, left_ref, right_ref, spans, finish):
    positions = left_ref.shape[0]
    groups, _, block, lanes = right_ref.shape
    low = lax.broadcasted_iota(jnp.int32, (block, lanes), 1) < block

    def strip_of(member, e):
        row = e * spans + member
        return jnp.concatenate(
            [
                jnp.where(low, left_ref[j, table_ref[2 * j, row]], left_ref[j, table_ref[2 * j + 1, row]])
                for j in range(positions)
            ],
            axis=1,
        )

    def members(first, at, number):
        rows = [strip_of(first + u, e) for u in range(number) for e in range(2)]
        columns = [right_ref[:, at + u].reshape(groups * block, lanes) for u in range(number)]
        sums = jnp.dot(
            jnp.concatenate(rows, axis=0),
            jnp.concatenate(columns, axis=1),
            preferred_element_type=jnp.float32,
        )
        for u in range(number):
            across = slice(u * lanes, (u + 1) * lanes)
            top = 2 * u * block
            upper, lower = sums[top : top + block, across], sums[top + block : top + 2 * block, across]
            finish(first + u, at + u, jnp.where(low, upper, lower))

    def run(first, at, size):
        def step(t, carry):
            for u in range(0, STEP, 2):
                members(first + STEP * t + u, at + STEP * t + u, 2)
            return carry

        lax.fori_loop(0, size // STEP, step, 0)
        for u in range(size // STEP * STEP, size - 1, 2):
            members(first + u, at + u, 2)
        if size % 2:
            members(first + size - 1, at + size - 1, 1)

    return run


def first_product(table, expected, rows_at, groups_at, slab, panels, strips, spans, scale):
    positions = SIDE * CORES
    groups = 2 * positions
    block, lanes = slab[0][0].shape[-2:]
    starts = [sum(size for _, size in strips[:i]) for i in range(len(strips))]
    count = sum(size for _, size in strips)
    make = table is None
    left_moves = sum(len(ranges) for _, _, ranges in slab)

    def body(rows_ref, groups_ref, *refs):
        refs = list(refs)
        if make:
            expected_ref = refs.pop(0)
        else:
            table_ref = refs.pop(0)
        slab_refs = [refs.pop(0) for _ in slab]
        piece_refs = [[refs.pop(0) for _ in pieces] for pieces, _ in panels]
        done_ref = refs.pop(0)
        if make:
            table_out, left_ref, left_sem, right_ref, right_sem, table_ref, extra_ref, extra_sem, table_sem = refs
        else:
            left_ref, left_sem, right_ref, right_sem = refs

        runs = panel_copies(piece_refs, panels, starts, strips, int(make), groups_ref, right_ref, right_sem)
        extra_copies = []
        if make:
            (pieces, axis), size = panels[0], strips[0][1]
            for ref, (array, second, begin) in zip(piece_refs[0], pieces):
                for first in range(SIDE):
                    offset = first * (size + 1) - begin
                    if 0 <= offset < array.shape[0]:
                        slot = first * SIDE + second if axis == 0 else second * SIDE + first
                        source = ref.at[offset + size, pl.ds(0, ROWS)]
                        target = extra_ref.at[groups_ref[slot]]
                        sem = extra_sem.at[len(extra_copies)]
                        extra_copies.append(pltpu.make_async_copy(source, target, sem))
        left_copies = slab_copies(slab_refs, slab, rows_ref, left_ref, left_sem)
        for copy in extra_copies + left_copies + runs[0][0]:
            copy.start()
        left_ref[:, spans] = jnp.zeros((positions, block, lanes), left_ref.dtype)
        if make:
            for copy in extra_copies:
                copy.wait()
            row = lax.broadcasted_iota(jnp.int32, (groups, ROWS, lanes), 1)
            weights = jnp.where(row == 0, DIGIT, jnp.where(row == 1, 1, 0)).astype(jnp.float32)
            links = jnp.sum(extra_ref[...].astype(jnp.float32) * weights, axis=1).astype(jnp.int32)
            wanted = expected_ref[...]
            first_of = spans * lax.broadcasted_iota(jnp.int32, (groups, lanes), 0)
            table_out[...] = jnp.where(links == wanted, wanted - first_of, spans)
            copy = pltpu.make_async_copy(table_out, table_ref, table_sem)
            copy.start()
            copy.wait()
        for copy in left_copies:
            copy.wait()
        for copies, _, _, _ in runs[1:]:
            for copy in copies:
                copy.start()

        def finish(member, at, sums):
            done_ref[at] = (sums * scale).astype(done_ref.dtype)

        run = block_sums(table_ref, left_ref, right_ref, spans, finish)
        for copies, first, at, size in runs:
            for copy in copies:
                copy.wait()
            run(first, at, size)

    anywhere = pl.BlockSpec(memory_space=pl.ANY)
    in_vmem = pl.BlockSpec(memory_space=pltpu.VMEM)
    in_smem = pl.BlockSpec(memory_space=pltpu.SMEM)
    operands = [array for array, _, _ in slab] + [x for pieces, _ in panels for x, _, _ in pieces]
    flops = WEIGHT * count * block * lanes * groups * block
    cost = pl.CostEstimate(flops=flops, bytes_accessed=2 * sum(x.size for x in operands), transcendentals=0)
    in_specs = [in_smem, in_smem, in_vmem if make else in_smem] + [anywhere] * len(operands)
    out_shape = [jax.ShapeDtypeStruct((count, block, lanes), jnp.bfloat16)]
    scratch = [
        pltpu.VMEM((positions, spans + 1, block, lanes), jnp.bfloat16),
        pltpu.SemaphoreType.DMA((left_moves,)),
        pltpu.VMEM((groups, count, block, lanes), jnp.bfloat16),
        pltpu.SemaphoreType.DMA((panel_moves(strips),)),
    ]
    if make:
        out_shape.append(jax.ShapeDtypeStruct((groups, lanes), jnp.int32))
        scratch += [
            pltpu.SMEM((groups, lanes), jnp.int32),
            pltpu.VMEM((groups, ROWS, lanes), jnp.bfloat16),
            pltpu.SemaphoreType.DMA((groups,)),
            pltpu.SemaphoreType.DMA,
        ]
    out = pl.pallas_call(
        body,
        in_specs=in_specs,
        out_specs=[in_vmem] * len(out_shape),
        out_shape=out_shape,
        scratch_shapes=scratch,
        compiler_params=pltpu.CompilerParams(vmem_limit_bytes=60 * MIB),
        cost_estimate=cost,
    )(rows_at, groups_at, expected if make else table, *operands)
    return out if make else (*out, table)


def second_product(table, rows_at, groups_at, slab, panels, strips, spans, scale, square, own):
    positions = SIDE * CORES
    groups = 2 * positions
    block, lanes = own.shape[-2:]
    left_moves = sum(len(ranges) for _, _, ranges in slab)
    members, flat_strips = {}, []
    for part, part_strips in enumerate(strips):
        inside = 0
        for first, size in part_strips:
            at = sum(size for _, size in flat_strips)
            members.update({first + m: (part, inside + m, at + m) for m in range(size)})
            flat_strips.append((first, size))
            inside += size
    starts = [sum(size for _, size in flat_strips[:i]) for i in range(len(flat_strips))]

    def body(table_ref, rows_ref, groups_ref, *refs):
        refs = list(refs)
        slab_refs = [refs.pop(0) for _ in slab]
        piece_refs = [[refs.pop(0) for _ in pieces] for pieces, _ in panels]
        square_refs = [refs.pop(0) for _ in square]
        own_ref, square_ref, flat_ref, left_ref, left_sem, right_ref, right_sem, done_ref = refs
        left_copies = slab_copies(slab_refs, slab, rows_ref, left_ref, left_sem)
        runs = panel_copies(piece_refs, panels, starts, flat_strips, 1, groups_ref, right_ref, right_sem)
        for copy in left_copies + runs[0][0]:
            copy.start()
        left_ref[:, spans] = jnp.zeros((positions, block, lanes), left_ref.dtype)
        join_columns(lambda m: square_refs[members[m][0]][members[m][1]], square_ref, spans, block)
        for copy in left_copies:
            copy.wait()
        for copies, _, _, _ in runs[1:]:
            for copy in copies:
                copy.start()

        def finish(member, at, sums):
            own_part = 1.5 * own_ref[member].astype(jnp.float32)
            done_ref[at] = (own_part - (0.5 * scale) * sums).astype(done_ref.dtype)

        run = block_sums(table_ref, left_ref, right_ref, spans, finish)
        for copies, first, at, size in runs:
            for copy in copies:
                copy.wait()
            run(first, at, size)
        join_columns(lambda m: done_ref[members[m][2]], flat_ref, spans, block)

    anywhere = pl.BlockSpec(memory_space=pl.ANY)
    in_vmem = pl.BlockSpec(memory_space=pltpu.VMEM)
    in_smem = pl.BlockSpec(memory_space=pltpu.SMEM)
    operands = [array for array, _, _ in slab] + [x for pieces, _ in panels for x, _, _ in pieces]
    flops = WEIGHT * spans * block * lanes * groups * block
    cost = pl.CostEstimate(flops=flops, bytes_accessed=2 * sum(x.size for x in operands), transcendentals=0)
    flat = jax.ShapeDtypeStruct((block, spans * lanes), jnp.bfloat16)
    return pl.pallas_call(
        body,
        in_specs=[in_smem] * 3 + [anywhere] * len(operands) + [in_vmem] * (len(square) + 1),
        out_specs=[in_vmem] * 2,
        out_shape=[flat] * 2,
        scratch_shapes=[
            pltpu.VMEM((positions, spans + 1, block, lanes), jnp.bfloat16),
            pltpu.SemaphoreType.DMA((left_moves,)),
            pltpu.VMEM((groups, spans, block, lanes), jnp.bfloat16),
            pltpu.SemaphoreType.DMA((panel_moves(flat_strips),)),
            pltpu.VMEM((spans, block, lanes), jnp.bfloat16),
        ],
        compiler_params=pltpu.CompilerParams(vmem_limit_bytes=60 * MIB),
        cost_estimate=cost,
    )(table, rows_at, groups_at, *operands, *square, own)


def per_device(values, pattern):
    block = values.shape[0]
    rows_here = values.shape[1] // block
    groups = lax.axis_size("col")
    spans = pattern.shape[0] // groups
    mine, group = lax.axis_index("row"), lax.axis_index("col")
    z, y = group // SIDE, group % SIDE
    column = pattern[:, 0]
    scale = 1.0 / math.sqrt(groups * block)

    split = (spans + 1) // 2
    halves = [(0, split), (split, spans - split)]
    own_links = lax.dynamic_slice_in_dim(column, mine * rows_here, rows_here, 0)
    own, *pieces = pair_columns(values, own_links, spans, halves)
    lines = []
    for axis, piece in enumerate(pieces):
        *three, (low, _, _), (high, _, _) = col_ring(piece, axis)
        lines.append([x for x, _, _ in three] + [jnp.concatenate([low, high], axis=0)])
    on_1 = sent_row(own, 1, 0)
    lines, on_1 = lax.optimization_barrier((lines, on_1))
    on_2 = sent_row(on_1, 1, 0)
    on_3 = sent_row(on_2, 1, 0)

    chip, core = mine // CORES, mine % CORES
    rows_at = [((chip + t) % SIDE) * CORES + (core + swap) % CORES for t in TURNS for swap in range(CORES)]
    groups_at = [((z + t) % SIDE) * SIDE + (y + u) % SIDE for t in TURNS for u in TURNS]
    rows_at = jnp.stack(rows_at).astype(jnp.int32)
    groups_at = jnp.stack(groups_at).astype(jnp.int32)
    member = jnp.arange(spans, dtype=jnp.int32)
    found = column.reshape(groups, spans, 1) == own_links[None, None, :]
    expected = jnp.sum(jnp.where(found, member[None, :, None], 0), axis=1)
    expected = expected + spans * jnp.arange(groups, dtype=jnp.int32)[:, None]
    expected = jnp.pad(expected, ((0, 0), (0, 2 * block - rows_here)), constant_values=-1)

    planes = [col_ring(jnp.concatenate(line, axis=0), 1 - axis) for axis, line in enumerate(lines)]
    nearest = [x for plane in planes for x, place, _ in plane if place in (1, 2)]
    chips, _ = lax.optimization_barrier(((own, on_1, on_2, on_3), nearest))
    first_slab = swapped_slab(chips)
    panels = [(plane, axis) for axis, plane in enumerate(planes)]
    square, table = first_product(
        None, expected, rows_at, groups_at, first_slab, panels, halves, spans, scale
    )
    second_slab = row_slab(square, halves)
    squares, all_strips = [square], [halves]
    where = (table, rows_at, groups_at)
    return tuple(second_product(*where, second_slab, panels, all_strips, spans, scale, squares, own))


def solution(mesh):
    in_specs = (P("col", "row"), P(None, "col"))
    out_specs = (P("col", "row"), P("col", "row"))
    return jax.shard_map(
        per_device, mesh=mesh, in_specs=in_specs, out_specs=out_specs, check_vma=False
    )
```

profile of v0, /device:TPU:1, one launch (start us, length us, event | category | flops | bytes accessed | tf_op | source)
XLA Modules:
  0.0 188.3 jit_solution(8018908182347029248)
XLA Ops:
  0.6 0.8 dynamic-slice_bitcast_fusion
  1.4 1.2 copy-done
  2.6 0.4 shard_map.41
  3.0 3.6 %collective-permute-start.5 = (bf16[29,64,128]{2,1,0:T(8,128)(2,1)S(1)}, bf16[29,64,128]{2,1,0:T(8,128)(2,1)S(1)}, u32[]{:S(2)}, u32[]{:S(2)}) collective-permute-start(bf16[29,64,128]{2,1,0:T(8,128)(2,1)S(1)} %get-tuple-element.31), channel_id=1, source_target_pairs={{0,3},{1,0},{2,1},{3,2},{4,7},{5,4},{6,5},{7,6},{8,11},{9,8},{10,9... | collective-permute-start | bytes 1425416 | tf_op jit(solution)/shard_map/ppermute | solution.py:71
  6.6 2.5 %collective-permute-start.8 = (bf16[59,64,128]{2,1,0:T(8,128)(2,1)S(1)}, bf16[59,64,128]{2,1,0:T(8,128)(2,1)S(1)}, u32[]{:S(2)}, u32[]{:S(2)}) collective-permute-start(bf16[59,64,128]{2,1,0:T(8,128)(2,1)S(1)} %get-tuple-element.35.refs_1_.refs_21_), channel_id=1, source_target_pairs={{0,96},{16,112},{32,0},{48,16},{64,32},{80,48},{96,64},{112,80},{1... | collective-permute-start | bytes 2899976 | tf_op jit(solution)/shard_map/ppermute | solution.py:61
  9.1 3.8 %collective-permute-start.1 = (bf16[31,64,128]{2,1,0:T(8,128)(2,1)S(1)}, bf16[31,64,128]{2,1,0:T(8,128)(2,1)S(1)}, u32[]{:S(2)}, u32[]{:S(2)}) collective-permute-start(bf16[31,64,128]{2,1,0:T(8,128)(2,1)S(1)} %get-tuple-element.27), channel_id=1, source_target_pairs={{0,12},{1,13},{2,14},{3,15},{4,0},{5,1},{6,2},{7,3},{8,4},{9,5},{1... | collective-permute-start | bytes 1523720 | tf_op jit(solution)/shard_map/ppermute | solution.py:71
  12.9 3.3 %collective-permute-done.5 = bf16[29,64,128]{2,1,0:T(8,128)(2,1)S(1)} collective-permute-done((bf16[29,64,128]{2,1,0:T(8,128)(2,1)S(1)}, bf16[29,64,128]{2,1,0:T(8,128)(2,1)S(1)}, u32[]{:S(2)}, u32[]{:S(2)}) %collective-permute-start.5) | collective-permute-done | bytes 475168 | tf_op jit(solution)/shard_map/ppermute | solution.py:71
  16.2 3.5 %collective-permute-start.6 = (bf16[15,64,128]{2,1,0:T(8,128)(2,1)S(1)}, bf16[15,64,128]{2,1,0:T(8,128)(2,1)S(1)}, u32[]{:S(2)}, u32[]{:S(2)}) collective-permute-start(bf16[15,64,128]{2,1,0:T(8,128)(2,1)S(1)} %slice.42), channel_id=1, source_target_pairs={{0,3},{1,0},{2,1},{3,2},{4,7},{5,4},{6,5},{7,6},{8,11},{9,8},{10,9... | collective-permute-start | bytes 737288 | tf_op jit(solution)/shard_map/ppermute | solution.py:71
  19.7 1.8 collective-permute-done.4
  21.5 0.1 collective-permute-start.7
  21.6 0.9 collective-permute-done.1
  22.5 3.5 %collective-permute-start.2 = (bf16[16,64,128]{2,1,0:T(8,128)(2,1)S(1)}, bf16[16,64,128]{2,1,0:T(8,128)(2,1)S(1)}, u32[]{:S(2)}, u32[]{:S(2)}) collective-permute-start(bf16[16,64,128]{2,1,0:T(8,128)(2,1)S(1)} %slice.40), channel_id=1, source_target_pairs={{0,12},{1,13},{2,14},{3,15},{4,0},{5,1},{6,2},{7,3},{8,4},{9,5},{1... | collective-permute-start | bytes 786440 | tf_op jit(solution)/shard_map/ppermute | solution.py:71
  26.0 0.1 collective-permute-start.3
  26.1 1.6 collective-permute-done.7
  27.7 4.6 %collective-permute-done.3 = bf16[15,64,128]{2,1,0:T(8,128)(2,1)S(1)} collective-permute-done((bf16[15,64,128]{2,1,0:T(8,128)(2,1)S(1)}, bf16[15,64,128]{2,1,0:T(8,128)(2,1)S(1)}, u32[]{:S(2)}, u32[]{:S(2)}) %collective-permute-start.3) | collective-permute-done | bytes 245792 | tf_op jit(solution)/shard_map/ppermute | solution.py:71
  32.5 0.1 constant_dynamic-update-slice_fusion.2
  32.6 0.1 constant_dynamic-update-slice_fusion.1
  32.6 0.1 constant_dynamic-update-slice_fusion.refs_9_.refs_10_
  32.7 0.1 collective-permute-start.11
  32.8 2.7 %collective-permute-start.12 = (bf16[124,64,128]{2,1,0:T(8,128)(2,1)S(1)}, bf16[124,64,128]{2,1,0:T(8,128)(2,1)S(1)}, u32[]{:S(2)}, u32[]{:S(2)}) collective-permute-start(bf16[124,64,128]{2,1,0:T(8,128)(2,1)S(1)} %constant_dynamic-update-slice_fusion.refs_9_.refs_10_), channel_id=1, source_target_pairs={{0,3},{1,0},{2,1},{3,2},{4,7},{5,4},{6,5},{7,6},{8,11},{9,8},{10,9... | collective-permute-start | bytes 6094856 | tf_op jit(solution)/shard_map/ppermute | solution.py:71
  35.5 0.9 collective-permute-start.9
  36.5 0.1 constant_dynamic-update-slice_fusion.5
  36.6 0.7 collective-permute-start.13
  37.3 2.2 %collective-permute-start.14 = (bf16[116,64,128]{2,1,0:T(8,128)(2,1)S(1)}, bf16[116,64,128]{2,1,0:T(8,128)(2,1)S(1)}, u32[]{:S(2)}, u32[]{:S(2)}) collective-permute-start(bf16[116,64,128]{2,1,0:T(8,128)(2,1)S(1)} %constant_dynamic-update-slice_fusion.4.refs_14_.refs_15_), channel_id=1, source_target_pairs={{0,12},{1,13},{2,14},{3,15},{4,0},{5,1},{6,2},{7,3},{8,4},{9,5},{1... | collective-permute-start | bytes 5701640 | tf_op jit(solution)/shard_map/ppermute | solution.py:71
  39.5 14.8 %collective-permute-done.9.refs_5_ = bf16[59,64,128]{2,1,0:T(8,128)(2,1)S(1)} collective-permute-done((bf16[59,64,128]{2,1,0:T(8,128)(2,1)S(1)}, bf16[59,64,128]{2,1,0:T(8,128)(2,1)S(1)}, u32[]{:S(2)}, u32[]{:S(2)}) %collective-permute-start.9) | collective-permute-done | bytes 966688 | tf_op jit(solution)/shard_map/ppermute | solution.py:61
  54.3 2.4 %collective-permute-start.10 = (bf16[59,64,128]{2,1,0:T(8,128)(2,1)S(1)}, bf16[59,64,128]{2,1,0:T(8,128)(2,1)S(1)}, u32[]{:S(2)}, u32[]{:S(2)}) collective-permute-start(bf16[59,64,128]{2,1,0:T(8,128)(2,1)S(1)} %collective-permute-done.9.refs_5_), channel_id=1, source_target_pairs={{0,96},{16,112},{32,0},{48,16},{64,32},{80,48},{96,64},{112,80},{1... | collective-permute-start | bytes 2899976 | tf_op jit(solution)/shard_map/ppermute | solution.py:61
  56.7 20.2 %collective-permute-done.13.refs_15_.refs_16_ = bf16[116,64,128]{2,1,0:T(8,128)(2,1)S(1)} collective-permute-done((bf16[116,64,128]{2,1,0:T(8,128)(2,1)S(1)}, bf16[116,64,128]{2,1,0:T(8,128)(2,1)S(1)}, u32[]{:S(2)}, u32[]{:S(2)}) %collective-permute-start.13) | collective-permute-done | bytes 1900576 | tf_op jit(solution)/shard_map/ppermute | solution.py:71
  76.9 0.2 collective-permute-done.14.refs_16_.refs_17_
  77.1 2.6 %pad_maximum_fusion = bf16[236,64,128]{2,1,0:T(8,128)(2,1)} fusion(bf16[59,64,128]{2,1,0:T(8,128)(2,1)S(1)} %collective-permute-done.10.refs_7_, bf16[59,64,128]{2,1,0:T(8,128)(2,1)S(1)} %collective-permute-done.9.refs_5_, bf16[59,64,128]{2,1,0:T(8,128)(2,1)S(1)} %collective-permute-done.8.refs_3_, bf16[59,64,128]{2,1,0:T(8,128)(2,1)S(1)} %get-tuple-element.35.refs_1_.refs_21_), kind=kLoop, calls=%fused_computation | loop fusion | flops 5799936 | bytes 7733248 | tf_op jit(solution)/shard_map/concatenate | solution.py:107
  79.7 4.7 %collective-permute-start.15 = (bf16[236,64,128]{2,1,0:T(8,128)(2,1)}, bf16[236,64,128]{2,1,0:T(8,128)(2,1)}, u32[]{:S(2)}, u32[]{:S(2)}) collective-permute-start(bf16[236,64,128]{2,1,0:T(8,128)(2,1)} %pad_maximum_fusion), channel_id=1, source_target_pairs={{0,16},{16,0},{32,48},{48,32},{64,80},{80,64},{96,112},{112,96},{1... | collective-permute-start | bytes 11599880 | tf_op jit(solution)/shard_map/ppermute | solution.py:61
  84.5 0.1 slice.44
  84.5 1.6 collective-permute-start.16
  86.1 0.1 slice.45
  86.2 0.1 collective-permute-start.17
  86.4 2.7 %collective-permute-start.18 = (bf16[58,64,128]{2,1,0:T(8,128)(2,1)S(1)}, bf16[58,64,128]{2,1,0:T(8,128)(2,1)}, u32[]{:S(2)}, u32[]{:S(2)}) collective-permute-start(bf16[58,64,128]{2,1,0:T(8,128)(2,1)S(1)} %slice.46), channel_id=1, source_target_pairs={{0,12},{1,13},{2,14},{3,15},{4,0},{5,1},{6,2},{7,3},{8,4},{9,5},{1... | collective-permute-start | bytes 2850824 | tf_op jit(solution)/shard_map/ppermute | solution.py:71
  89.1 1.0 slice.47
  90.1 0.5 broadcast.35
  90.6 0.6 reduce.3
  91.1 0.1 eq.68
  91.2 0.1 copy.4
  91.3 0.2 select_reduce_fusion
  91.5 0.1 broadcast_add_fusion
  91.6 0.6 pad.8.refs_0_
  92.2 0.6 stack.86.rows_ref
  92.8 0.7 stack.103.groups_ref
  93.5 14.5 %collective-permute-done.18.refs_17_.refs_18_ = bf16[58,64,128]{2,1,0:T(8,128)(2,1)} collective-permute-done((bf16[58,64,128]{2,1,0:T(8,128)(2,1)S(1)}, bf16[58,64,128]{2,1,0:T(8,128)(2,1)}, u32[]{:S(2)}, u32[]{:S(2)}) %collective-permute-start.18) | collective-permute-done | bytes 950304 | tf_op jit(solution)/shard_map/ppermute | solution.py:71
  108.0 4.4 %collective-permute-done.19.refs_18_.refs_19_ = bf16[58,64,128]{2,1,0:T(8,128)(2,1)} collective-permute-done((bf16[58,64,128]{2,1,0:T(8,128)(2,1)}, bf16[58,64,128]{2,1,0:T(8,128)(2,1)}, u32[]{:S(2)}, u32[]{:S(2)}) %collective-permute-start.19) | collective-permute-done | bytes 950304 | tf_op jit(solution)/shard_map/ppermute | solution.py:71
  112.4 14.5 %shard_map.42 = (bf16[59,64,128]{2,1,0:T(8,128)(2,1)}, s32[16,128]{1,0:T(8,128)}) custom-call(s32[8]{0:T(128)} %stack.86.rows_ref, s32[16]{0:T(128)} %stack.103.groups_ref, s32[16,128]{1,0:T(8,128)} %pad.8.refs_0_, bf16[59,64,128]{2,1,0:T(8,128)(2,1)} %copy-done.1, bf16[236,64,128]{2,1,0:T(8,128)(2,1)} %collective-permute-done.15.refs_2_.refs_4_.refs_6_.refs_8_, ...), custom_call_target="tpu_custom_call" | custom-call | flops 23756537856 | bytes 35061760 | tf_op jit(solution)/shard_map/pallas_call | solution.py:287
  126.9 0.5 collective-permute-start.20
  127.4 2.2 %collective-permute-start.21 = (bf16[59,64,128]{2,1,0:T(8,128)(2,1)}, bf16[59,64,128]{2,1,0:T(8,128)(2,1)S(1)}, u32[]{:S(2)}, u32[]{:S(2)}) collective-permute-start(bf16[59,64,128]{2,1,0:T(8,128)(2,1)} %get-tuple-element.40.refs_0_.refs_20_), channel_id=1, source_target_pairs={{0,96},{16,112},{32,0},{48,16},{64,32},{80,48},{96,64},{112,80},{1... | collective-permute-start | bytes 2899976 | tf_op jit(solution)/shard_map/ppermute | solution.py:61
  129.6 3.2 %collective-permute-start.22 = (bf16[59,64,128]{2,1,0:T(8,128)(2,1)}, bf16[59,64,128]{2,1,0:T(8,128)(2,1)S(1)}, u32[]{:S(2)}, u32[]{:S(2)}) collective-permute-start(bf16[59,64,128]{2,1,0:T(8,128)(2,1)} %get-tuple-element.40.refs_0_.refs_20_), channel_id=1, source_target_pairs={{0,16},{16,0},{32,48},{48,32},{64,80},{80,64},{96,112},{112,96},{1... | collective-permute-start | bytes 2899976 | tf_op jit(solution)/shard_map/ppermute | solution.py:61
  132.9 15.7 %collective-permute-done.20.refs_2_ = bf16[59,64,128]{2,1,0:T(8,128)(2,1)S(1)} collective-permute-done((bf16[59,64,128]{2,1,0:T(8,128)(2,1)}, bf16[59,64,128]{2,1,0:T(8,128)(2,1)S(1)}, u32[]{:S(2)}, u32[]{:S(2)}) %collective-permute-start.20) | collective-permute-done | bytes 966688 | tf_op jit(solution)/shard_map/ppermute | solution.py:61
  148.6 2.4 %collective-permute-start.25 = (bf16[30,64,128]{2,1,0:T(8,128)(2,1)S(1)}, bf16[30,64,128]{2,1,0:T(8,128)(2,1)S(1)}, u32[]{:S(2)}, u32[]{:S(2)}) collective-permute-start(bf16[30,64,128]{2,1,0:T(8,128)(2,1)S(1)} %slice.38), channel_id=1, source_target_pairs={{0,96},{16,112},{32,0},{48,16},{64,32},{80,48},{96,64},{112,80},{1... | collective-permute-start | bytes 1474568 | tf_op jit(solution)/shard_map/ppermute | solution.py:61
  151.1 4.2 %collective-permute-start.23 = (bf16[59,64,128]{2,1,0:T(8,128)(2,1)S(1)}, bf16[59,64,128]{2,1,0:T(8,128)(2,1)S(1)}, u32[]{:S(2)}, u32[]{:S(2)}) collective-permute-start(bf16[59,64,128]{2,1,0:T(8,128)(2,1)S(1)} %collective-permute-done.20.refs_2_), channel_id=1, source_target_pairs={{0,16},{16,0},{32,48},{48,32},{64,80},{80,64},{96,112},{112,96},{1... | collective-permute-start | bytes 2899976 | tf_op jit(solution)/shard_map/ppermute | solution.py:61
  155.3 0.1 collective-permute-start.27
  155.4 2.4 %collective-permute-done.25.refs_6_ = bf16[30,64,128]{2,1,0:T(8,128)(2,1)S(1)} collective-permute-done((bf16[30,64,128]{2,1,0:T(8,128)(2,1)S(1)}, bf16[30,64,128]{2,1,0:T(8,128)(2,1)S(1)}, u32[]{:S(2)}, u32[]{:S(2)}) %collective-permute-start.25) | collective-permute-done | bytes 491552 | tf_op jit(solution)/shard_map/ppermute | solution.py:61
  157.8 4.7 %collective-permute-start.26 = (bf16[30,64,128]{2,1,0:T(8,128)(2,1)S(1)}, bf16[30,64,128]{2,1,0:T(8,128)(2,1)S(1)}, u32[]{:S(2)}, u32[]{:S(2)}) collective-permute-start(bf16[30,64,128]{2,1,0:T(8,128)(2,1)S(1)} %collective-permute-done.25.refs_6_), channel_id=1, source_target_pairs={{0,16},{16,0},{32,48},{48,32},{64,80},{80,64},{96,112},{112,96},{1... | collective-permute-start | bytes 1474568 | tf_op jit(solution)/shard_map/ppermute | solution.py:61
  162.5 6.0 %collective-permute-done.27.refs_8_ = bf16[29,64,128]{2,1,0:T(8,128)(2,1)S(1)} collective-permute-done((bf16[29,64,128]{2,1,0:T(8,128)(2,1)S(1)}, bf16[29,64,128]{2,1,0:T(8,128)(2,1)S(1)}, u32[]{:S(2)}, u32[]{:S(2)}) %collective-permute-start.27) | collective-permute-done | bytes 475168 | tf_op jit(solution)/shard_map/ppermute | solution.py:61
  168.5 1.4 collective-permute-start.28
  169.9 1.5 collective-permute-done.28.refs_9_
  171.3 0.9 copy-done.16
  172.3 0.1 copy-done.20
  172.4 0.8 copy-done.18
  173.2 15.0 %shard_map.43 = (bf16[64,7552]{1,0:T(8,128)(2,1)}, bf16[64,7552]{1,0:T(8,128)(2,1)}) custom-call(s32[16,128]{1,0:T(8,128)} %get-tuple-element.39.table_ref, s32[8]{0:T(128)} %stack.86.rows_ref, s32[16]{0:T(128)} %stack.103.groups_ref, bf16[59,64,128]{2,1,0:T(8,128)(2,1)} %get-tuple-element.40.refs_0_.refs_20_, bf16[59,64,128]{2,1,0:T(8,128)(2,1)} %copy-done.14, ...), custom_call_target="tpu_custom_call" | custom-call | flops 23756537856 | bytes 23461888 | tf_op jit(solution)/shard_map/pallas_call | solution.py:350
  (72 shorter events, 0.6 us)
Async XLA Ops:
  1.4 1.2 copy-start
  3.0 74.1 %copy-start.1 = (bf16[59,64,128]{2,1,0:T(8,128)(2,1)}, bf16[59,64,128]{2,1,0:T(8,128)(2,1)S(1)}, u32[]{:S(2)}) copy-start(bf16[59,64,128]{2,1,0:T(8,128)(2,1)S(1)} %get-tuple-element.35.refs_1_.refs_21_) | copy-start | bytes 2899972
  3.0 13.2 %collective-permute-start.5 = (bf16[29,64,128]{2,1,0:T(8,128)(2,1)S(1)}, bf16[29,64,128]{2,1,0:T(8,128)(2,1)S(1)}, u32[]{:S(2)}, u32[]{:S(2)}) collective-permute-start(bf16[29,64,128]{2,1,0:T(8,128)(2,1)S(1)} %get-tuple-element.31), channel_id=1, source_target_pairs={{0,3},{1,0},{2,1},{3,2},{4,7},{5,4},{6,5},{7,6},{8,11},{9,8},{10,9... | collective-permute-start | bytes 1425416 | tf_op jit(solution)/shard_map/ppermute | solution.py:71
  6.6 25.8 %collective-permute-start.8 = (bf16[59,64,128]{2,1,0:T(8,128)(2,1)S(1)}, bf16[59,64,128]{2,1,0:T(8,128)(2,1)S(1)}, u32[]{:S(2)}, u32[]{:S(2)}) collective-permute-start(bf16[59,64,128]{2,1,0:T(8,128)(2,1)S(1)} %get-tuple-element.35.refs_1_.refs_21_), channel_id=1, source_target_pairs={{0,96},{16,112},{32,0},{48,16},{64,32},{80,48},{96,64},{112,80},{1... | collective-permute-start | bytes 2899976 | tf_op jit(solution)/shard_map/ppermute | solution.py:61
  9.1 12.3 %collective-permute-start.4 = (bf16[29,64,128]{2,1,0:T(8,128)(2,1)S(1)}, bf16[29,64,128]{2,1,0:T(8,128)(2,1)S(1)}, u32[]{:S(2)}, u32[]{:S(2)}) collective-permute-start(bf16[29,64,128]{2,1,0:T(8,128)(2,1)S(1)} %get-tuple-element.31), channel_id=1, source_target_pairs={{0,1},{1,2},{2,3},{3,0},{4,5},{5,6},{6,7},{7,4},{8,9},{9,10},{10,1... | collective-permute-start | bytes 1425416 | tf_op jit(solution)/shard_map/ppermute | solution.py:71
  9.1 13.4 %collective-permute-start.1 = (bf16[31,64,128]{2,1,0:T(8,128)(2,1)S(1)}, bf16[31,64,128]{2,1,0:T(8,128)(2,1)S(1)}, u32[]{:S(2)}, u32[]{:S(2)}) collective-permute-start(bf16[31,64,128]{2,1,0:T(8,128)(2,1)S(1)} %get-tuple-element.27), channel_id=1, source_target_pairs={{0,12},{1,13},{2,14},{3,15},{4,0},{5,1},{6,2},{7,3},{8,4},{9,5},{1... | collective-permute-start | bytes 1523720 | tf_op jit(solution)/shard_map/ppermute | solution.py:71
  12.9 13.1 %collective-permute-start = (bf16[31,64,128]{2,1,0:T(8,128)(2,1)S(1)}, bf16[31,64,128]{2,1,0:T(8,128)(2,1)S(1)}, u32[]{:S(2)}, u32[]{:S(2)}) collective-permute-start(bf16[31,64,128]{2,1,0:T(8,128)(2,1)S(1)} %get-tuple-element.27), channel_id=1, source_target_pairs={{0,4},{1,5},{2,6},{3,7},{4,8},{5,9},{6,10},{7,11},{8,12},{9,13},{1... | collective-permute-start | bytes 1523720 | tf_op jit(solution)/shard_map/ppermute | solution.py:71
  16.2 11.5 %collective-permute-start.6 = (bf16[15,64,128]{2,1,0:T(8,128)(2,1)S(1)}, bf16[15,64,128]{2,1,0:T(8,128)(2,1)S(1)}, u32[]{:S(2)}, u32[]{:S(2)}) collective-permute-start(bf16[15,64,128]{2,1,0:T(8,128)(2,1)S(1)} %slice.42), channel_id=1, source_target_pairs={{0,3},{1,0},{2,1},{3,2},{4,7},{5,4},{6,5},{7,6},{8,11},{9,8},{10,9... | collective-permute-start | bytes 737288 | tf_op jit(solution)/shard_map/ppermute | solution.py:71
  21.5 6.2 %collective-permute-start.7 = (bf16[14,64,128]{2,1,0:T(8,128)(2,1)S(1)}, bf16[14,64,128]{2,1,0:T(8,128)(2,1)S(1)}, u32[]{:S(2)}, u32[]{:S(2)}) collective-permute-start(bf16[14,64,128]{2,1,0:T(8,128)(2,1)S(1)} %slice.43), channel_id=1, source_target_pairs={{0,1},{1,2},{2,3},{3,0},{4,5},{5,6},{6,7},{7,4},{8,9},{9,10},{10,1... | collective-permute-start | bytes 688136 | tf_op jit(solution)/shard_map/ppermute | solution.py:71
  22.5 9.8 %collective-permute-start.2 = (bf16[16,64,128]{2,1,0:T(8,128)(2,1)S(1)}, bf16[16,64,128]{2,1,0:T(8,128)(2,1)S(1)}, u32[]{:S(2)}, u32[]{:S(2)}) collective-permute-start(bf16[16,64,128]{2,1,0:T(8,128)(2,1)S(1)} %slice.40), channel_id=1, source_target_pairs={{0,12},{1,13},{2,14},{3,15},{4,0},{5,1},{6,2},{7,3},{8,4},{9,5},{1... | collective-permute-start | bytes 786440 | tf_op jit(solution)/shard_map/ppermute | solution.py:71
  26.0 6.3 %collective-permute-start.3 = (bf16[15,64,128]{2,1,0:T(8,128)(2,1)S(1)}, bf16[15,64,128]{2,1,0:T(8,128)(2,1)S(1)}, u32[]{:S(2)}, u32[]{:S(2)}) collective-permute-start(bf16[15,64,128]{2,1,0:T(8,128)(2,1)S(1)} %slice.41), channel_id=1, source_target_pairs={{0,4},{1,5},{2,6},{3,7},{4,8},{5,9},{6,10},{7,11},{8,12},{9,13},{1... | collective-permute-start | bytes 737288 | tf_op jit(solution)/shard_map/ppermute | solution.py:71
  32.4 44.7 %copy-start.2 = (bf16[59,64,128]{2,1,0:T(8,128)(2,1)}, bf16[59,64,128]{2,1,0:T(8,128)(2,1)S(1)}, u32[]{:S(2)}) copy-start(bf16[59,64,128]{2,1,0:T(8,128)(2,1)S(1)} %collective-permute-done.8.refs_3_) | copy-start | bytes 2899972
  32.7 44.3 %copy-start.11 = (bf16[124,64,128]{2,1,0:T(8,128)(2,1)}, bf16[124,64,128]{2,1,0:T(8,128)(2,1)S(1)}, u32[]{:S(2)}) copy-start(bf16[124,64,128]{2,1,0:T(8,128)(2,1)S(1)} %constant_dynamic-update-slice_fusion.refs_9_.refs_10_) | copy-start | bytes 6094852
  32.7 44.3 %collective-permute-start.11 = (bf16[124,64,128]{2,1,0:T(8,128)(2,1)S(1)}, bf16[124,64,128]{2,1,0:T(8,128)(2,1)S(1)}, u32[]{:S(2)}, u32[]{:S(2)}) collective-permute-start(bf16[124,64,128]{2,1,0:T(8,128)(2,1)S(1)} %constant_dynamic-update-slice_fusion.refs_9_.refs_10_), channel_id=1, source_target_pairs={{0,1},{1,2},{2,3},{3,0},{4,5},{5,6},{6,7},{7,4},{8,9},{9,10},{10,1... | collective-permute-start | bytes 6094856 | tf_op jit(solution)/shard_map/ppermute | solution.py:71
  32.8 44.3 %collective-permute-start.12 = (bf16[124,64,128]{2,1,0:T(8,128)(2,1)S(1)}, bf16[124,64,128]{2,1,0:T(8,128)(2,1)S(1)}, u32[]{:S(2)}, u32[]{:S(2)}) collective-permute-start(bf16[124,64,128]{2,1,0:T(8,128)(2,1)S(1)} %constant_dynamic-update-slice_fusion.refs_9_.refs_10_), channel_id=1, source_target_pairs={{0,3},{1,0},{2,1},{3,2},{4,7},{5,4},{6,5},{7,6},{8,11},{9,8},{10,9... | collective-permute-start | bytes 6094856 | tf_op jit(solution)/shard_map/ppermute | solution.py:71
  35.5 18.8 %collective-permute-start.9 = (bf16[59,64,128]{2,1,0:T(8,128)(2,1)S(1)}, bf16[59,64,128]{2,1,0:T(8,128)(2,1)S(1)}, u32[]{:S(2)}, u32[]{:S(2)}) collective-permute-start(bf16[59,64,128]{2,1,0:T(8,128)(2,1)S(1)} %collective-permute-done.8.refs_3_), channel_id=1, source_target_pairs={{0,96},{16,112},{32,0},{48,16},{64,32},{80,48},{96,64},{112,80},{1... | collective-permute-start | bytes 2899976 | tf_op jit(solution)/shard_map/ppermute | solution.py:61
  36.6 40.4 %copy-start.12 = (bf16[116,64,128]{2,1,0:T(8,128)(2,1)}, bf16[116,64,128]{2,1,0:T(8,128)(2,1)S(1)}, u32[]{:S(2)}) copy-start(bf16[116,64,128]{2,1,0:T(8,128)(2,1)S(1)} %constant_dynamic-update-slice_fusion.4.refs_14_.refs_15_) | copy-start | bytes 5701636
  36.6 40.2 %collective-permute-start.13 = (bf16[116,64,128]{2,1,0:T(8,128)(2,1)S(1)}, bf16[116,64,128]{2,1,0:T(8,128)(2,1)S(1)}, u32[]{:S(2)}, u32[]{:S(2)}) collective-permute-start(bf16[116,64,128]{2,1,0:T(8,128)(2,1)S(1)} %constant_dynamic-update-slice_fusion.4.refs_14_.refs_15_), channel_id=1, source_target_pairs={{0,4},{1,5},{2,6},{3,7},{4,8},{5,9},{6,10},{7,11},{8,12},{9,13},{1... | collective-permute-start | bytes 5701640 | tf_op jit(solution)/shard_map/ppermute | solution.py:71
  37.3 39.7 %collective-permute-start.14 = (bf16[116,64,128]{2,1,0:T(8,128)(2,1)S(1)}, bf16[116,64,128]{2,1,0:T(8,128)(2,1)S(1)}, u32[]{:S(2)}, u32[]{:S(2)}) collective-permute-start(bf16[116,64,128]{2,1,0:T(8,128)(2,1)S(1)} %constant_dynamic-update-slice_fusion.4.refs_14_.refs_15_), channel_id=1, source_target_pairs={{0,12},{1,13},{2,14},{3,15},{4,0},{5,1},{6,2},{7,3},{8,4},{9,5},{1... | collective-permute-start | bytes 5701640 | tf_op jit(solution)/shard_map/ppermute | solution.py:71
  54.3 25.4 %copy-start.3 = (bf16[59,64,128]{2,1,0:T(8,128)(2,1)}, bf16[59,64,128]{2,1,0:T(8,128)(2,1)S(1)}, u32[]{:S(2)}) copy-start(bf16[59,64,128]{2,1,0:T(8,128)(2,1)S(1)} %collective-permute-done.9.refs_5_) | copy-start | bytes 2899972
  54.3 22.7 %collective-permute-start.10 = (bf16[59,64,128]{2,1,0:T(8,128)(2,1)S(1)}, bf16[59,64,128]{2,1,0:T(8,128)(2,1)S(1)}, u32[]{:S(2)}, u32[]{:S(2)}) collective-permute-start(bf16[59,64,128]{2,1,0:T(8,128)(2,1)S(1)} %collective-permute-done.9.refs_5_), channel_id=1, source_target_pairs={{0,96},{16,112},{32,0},{48,16},{64,32},{80,48},{96,64},{112,80},{1... | collective-permute-start | bytes 2899976 | tf_op jit(solution)/shard_map/ppermute | solution.py:61
  76.9 12.2 %copy-start.7 = (bf16[116,64,128]{2,1,0:T(8,128)(2,1)}, bf16[116,64,128]{2,1,0:T(8,128)(2,1)S(1)}, u32[]{:S(2)}) copy-start(bf16[116,64,128]{2,1,0:T(8,128)(2,1)S(1)} %collective-permute-done.13.refs_15_.refs_16_) | copy-start | bytes 5701636
  77.0 9.3 %copy-start.8 = (bf16[116,64,128]{2,1,0:T(8,128)(2,1)}, bf16[116,64,128]{2,1,0:T(8,128)(2,1)S(1)}, u32[]{:S(2)}) copy-start(bf16[116,64,128]{2,1,0:T(8,128)(2,1)S(1)} %collective-permute-done.14.refs_16_.refs_17_) | copy-start | bytes 5701636
  77.0 2.7 %copy-start.4 = (bf16[59,64,128]{2,1,0:T(8,128)(2,1)}, bf16[59,64,128]{2,1,0:T(8,128)(2,1)S(1)}, u32[]{:S(2)}) copy-start(bf16[59,64,128]{2,1,0:T(8,128)(2,1)S(1)} %collective-permute-done.10.refs_7_) | copy-start | bytes 2899972
  77.1 9.1 %copy-start.5 = (bf16[124,64,128]{2,1,0:T(8,128)(2,1)}, bf16[124,64,128]{2,1,0:T(8,128)(2,1)S(1)}, u32[]{:S(2)}) copy-start(bf16[124,64,128]{2,1,0:T(8,128)(2,1)S(1)} %collective-permute-done.11.refs_10_.refs_11_) | copy-start | bytes 6094852
  77.1 7.4 %copy-start.6 = (bf16[124,64,128]{2,1,0:T(8,128)(2,1)}, bf16[124,64,128]{2,1,0:T(8,128)(2,1)S(1)}, u32[]{:S(2)}) copy-start(bf16[124,64,128]{2,1,0:T(8,128)(2,1)S(1)} %collective-permute-done.12.refs_11_.refs_12_) | copy-start | bytes 6094852
  79.7 32.7 %collective-permute-start.15 = (bf16[236,64,128]{2,1,0:T(8,128)(2,1)}, bf16[236,64,128]{2,1,0:T(8,128)(2,1)}, u32[]{:S(2)}, u32[]{:S(2)}) collective-permute-start(bf16[236,64,128]{2,1,0:T(8,128)(2,1)} %pad_maximum_fusion), channel_id=1, source_target_pairs={{0,16},{16,0},{32,48},{48,32},{64,80},{80,64},{96,112},{112,96},{1... | collective-permute-start | bytes 11599880 | tf_op jit(solution)/shard_map/ppermute | solution.py:61
  84.5 27.9 %collective-permute-start.16 = (bf16[62,64,128]{2,1,0:T(8,128)(2,1)S(1)}, bf16[62,64,128]{2,1,0:T(8,128)(2,1)}, u32[]{:S(2)}, u32[]{:S(2)}) collective-permute-start(bf16[62,64,128]{2,1,0:T(8,128)(2,1)S(1)} %slice.44), channel_id=1, source_target_pairs={{0,3},{1,0},{2,1},{3,2},{4,7},{5,4},{6,5},{7,6},{8,11},{9,8},{10,9... | collective-permute-start | bytes 3047432 | tf_op jit(solution)/shard_map/ppermute | solution.py:71
  86.2 4.4 %copy-start.13 = (s32[944,1]{0,1:T(1,128)S(1)}, s32[944,1]{0,1:T(1,128)}, u32[]{:S(2)}) copy-start(s32[944,1]{0,1:T(1,128)} %param.3) | copy-start | bytes 11332
  86.2 26.2 %collective-permute-start.17 = (bf16[62,64,128]{2,1,0:T(8,128)(2,1)S(1)}, bf16[62,64,128]{2,1,0:T(8,128)(2,1)}, u32[]{:S(2)}, u32[]{:S(2)}) collective-permute-start(bf16[62,64,128]{2,1,0:T(8,128)(2,1)S(1)} %slice.45), channel_id=1, source_target_pairs={{0,1},{1,2},{2,3},{3,0},{4,5},{5,6},{6,7},{7,4},{8,9},{9,10},{10,1... | collective-permute-start | bytes 3047432 | tf_op jit(solution)/shard_map/ppermute | solution.py:71
  86.4 21.6 %collective-permute-start.18 = (bf16[58,64,128]{2,1,0:T(8,128)(2,1)S(1)}, bf16[58,64,128]{2,1,0:T(8,128)(2,1)}, u32[]{:S(2)}, u32[]{:S(2)}) collective-permute-start(bf16[58,64,128]{2,1,0:T(8,128)(2,1)S(1)} %slice.46), channel_id=1, source_target_pairs={{0,12},{1,13},{2,14},{3,15},{4,0},{5,1},{6,2},{7,3},{8,4},{9,5},{1... | collective-permute-start | bytes 2850824 | tf_op jit(solution)/shard_map/ppermute | solution.py:71
  90.1 22.3 %collective-permute-start.19 = (bf16[58,64,128]{2,1,0:T(8,128)(2,1)}, bf16[58,64,128]{2,1,0:T(8,128)(2,1)}, u32[]{:S(2)}, u32[]{:S(2)}) collective-permute-start(bf16[58,64,128]{2,1,0:T(8,128)(2,1)} %slice.47), channel_id=1, source_target_pairs={{0,4},{1,5},{2,6},{3,7},{4,8},{5,9},{6,10},{7,11},{8,12},{9,13},{1... | collective-permute-start | bytes 2850824 | tf_op jit(solution)/shard_map/ppermute | solution.py:71
  126.9 21.7 %collective-permute-start.20 = (bf16[59,64,128]{2,1,0:T(8,128)(2,1)}, bf16[59,64,128]{2,1,0:T(8,128)(2,1)S(1)}, u32[]{:S(2)}, u32[]{:S(2)}) collective-permute-start(bf16[59,64,128]{2,1,0:T(8,128)(2,1)} %get-tuple-element.40.refs_0_.refs_20_), channel_id=1, source_target_pairs={{0,32},{16,48},{32,64},{48,80},{64,96},{80,112},{96,0},{112,16},{1... | collective-permute-start | bytes 2899976 | tf_op jit(solution)/shard_map/ppermute | solution.py:61
  127.4 21.2 %collective-permute-start.21 = (bf16[59,64,128]{2,1,0:T(8,128)(2,1)}, bf16[59,64,128]{2,1,0:T(8,128)(2,1)S(1)}, u32[]{:S(2)}, u32[]{:S(2)}) collective-permute-start(bf16[59,64,128]{2,1,0:T(8,128)(2,1)} %get-tuple-element.40.refs_0_.refs_20_), channel_id=1, source_target_pairs={{0,96},{16,112},{32,0},{48,16},{64,32},{80,48},{96,64},{112,80},{1... | collective-permute-start | bytes 2899976 | tf_op jit(solution)/shard_map/ppermute | solution.py:61
  129.6 19.0 %collective-permute-start.22 = (bf16[59,64,128]{2,1,0:T(8,128)(2,1)}, bf16[59,64,128]{2,1,0:T(8,128)(2,1)S(1)}, u32[]{:S(2)}, u32[]{:S(2)}) collective-permute-start(bf16[59,64,128]{2,1,0:T(8,128)(2,1)} %get-tuple-element.40.refs_0_.refs_20_), channel_id=1, source_target_pairs={{0,16},{16,0},{32,48},{48,32},{64,80},{80,64},{96,112},{112,96},{1... | collective-permute-start | bytes 2899976 | tf_op jit(solution)/shard_map/ppermute | solution.py:61
  148.6 24.6 %copy-start.10 = (bf16[59,64,128]{2,1,0:T(8,128)(2,1)}, bf16[59,64,128]{2,1,0:T(8,128)(2,1)S(1)}, u32[]{:S(2)}) copy-start(bf16[59,64,128]{2,1,0:T(8,128)(2,1)S(1)} %collective-permute-done.20.refs_2_) | copy-start | bytes 2899972
  148.6 24.6 %copy-start.9 = (bf16[59,64,128]{2,1,0:T(8,128)(2,1)}, bf16[59,64,128]{2,1,0:T(8,128)(2,1)S(1)}, u32[]{:S(2)}) copy-start(bf16[59,64,128]{2,1,0:T(8,128)(2,1)S(1)} %collective-permute-done.21.refs_4_) | copy-start | bytes 2899972
  148.6 24.6 %copy-start.14 = (bf16[59,64,128]{2,1,0:T(8,128)(2,1)}, bf16[59,64,128]{2,1,0:T(8,128)(2,1)S(1)}, u32[]{:S(2)}) copy-start(bf16[59,64,128]{2,1,0:T(8,128)(2,1)S(1)} %collective-permute-done.22.refs_1_) | copy-start | bytes 2899972
  148.6 9.2 %collective-permute-start.25 = (bf16[30,64,128]{2,1,0:T(8,128)(2,1)S(1)}, bf16[30,64,128]{2,1,0:T(8,128)(2,1)S(1)}, u32[]{:S(2)}, u32[]{:S(2)}) collective-permute-start(bf16[30,64,128]{2,1,0:T(8,128)(2,1)S(1)} %slice.38), channel_id=1, source_target_pairs={{0,96},{16,112},{32,0},{48,16},{64,32},{80,48},{96,64},{112,80},{1... | collective-permute-start | bytes 1474568 | tf_op jit(solution)/shard_map/ppermute | solution.py:61
  151.1 20.2 %collective-permute-start.23 = (bf16[59,64,128]{2,1,0:T(8,128)(2,1)S(1)}, bf16[59,64,128]{2,1,0:T(8,128)(2,1)S(1)}, u32[]{:S(2)}, u32[]{:S(2)}) collective-permute-start(bf16[59,64,128]{2,1,0:T(8,128)(2,1)S(1)} %collective-permute-done.20.refs_2_), channel_id=1, source_target_pairs={{0,16},{16,0},{32,48},{48,32},{64,80},{80,64},{96,112},{112,96},{1... | collective-permute-start | bytes 2899976 | tf_op jit(solution)/shard_map/ppermute | solution.py:61
  155.2 16.1 %collective-permute-start.24 = (bf16[59,64,128]{2,1,0:T(8,128)(2,1)S(1)}, bf16[59,64,128]{2,1,0:T(8,128)(2,1)S(1)}, u32[]{:S(2)}, u32[]{:S(2)}) collective-permute-start(bf16[59,64,128]{2,1,0:T(8,128)(2,1)S(1)} %collective-permute-done.21.refs_4_), channel_id=1, source_target_pairs={{0,16},{16,0},{32,48},{48,32},{64,80},{80,64},{96,112},{112,96},{1... | collective-permute-start | bytes 2899976 | tf_op jit(solution)/shard_map/ppermute | solution.py:61
  155.3 13.2 %collective-permute-start.27 = (bf16[29,64,128]{2,1,0:T(8,128)(2,1)S(1)}, bf16[29,64,128]{2,1,0:T(8,128)(2,1)S(1)}, u32[]{:S(2)}, u32[]{:S(2)}) collective-permute-start(bf16[29,64,128]{2,1,0:T(8,128)(2,1)S(1)} %slice.39), channel_id=1, source_target_pairs={{0,32},{16,48},{32,64},{48,80},{64,96},{80,112},{96,0},{112,16},{1... | collective-permute-start | bytes 1425416 | tf_op jit(solution)/shard_map/ppermute | solution.py:61
  157.8 14.5 %copy-start.17 = (bf16[30,64,128]{2,1,0:T(8,128)(2,1)}, bf16[30,64,128]{2,1,0:T(8,128)(2,1)S(1)}, u32[]{:S(2)}) copy-start(bf16[30,64,128]{2,1,0:T(8,128)(2,1)S(1)} %collective-permute-done.25.refs_6_) | copy-start | bytes 1474564
  157.8 14.5 %collective-permute-start.26 = (bf16[30,64,128]{2,1,0:T(8,128)(2,1)S(1)}, bf16[30,64,128]{2,1,0:T(8,128)(2,1)S(1)}, u32[]{:S(2)}, u32[]{:S(2)}) collective-permute-start(bf16[30,64,128]{2,1,0:T(8,128)(2,1)S(1)} %collective-permute-done.25.refs_6_), channel_id=1, source_target_pairs={{0,16},{16,0},{32,48},{48,32},{64,80},{80,64},{96,112},{112,96},{1... | collective-permute-start | bytes 1474568 | tf_op jit(solution)/shard_map/ppermute | solution.py:61
  168.5 3.8 %copy-start.19 = (bf16[29,64,128]{2,1,0:T(8,128)(2,1)}, bf16[29,64,128]{2,1,0:T(8,128)(2,1)S(1)}, u32[]{:S(2)}) copy-start(bf16[29,64,128]{2,1,0:T(8,128)(2,1)S(1)} %collective-permute-done.27.refs_8_) | copy-start | bytes 1425412
  168.5 2.8 %collective-permute-start.28 = (bf16[29,64,128]{2,1,0:T(8,128)(2,1)S(1)}, bf16[29,64,128]{2,1,0:T(8,128)(2,1)S(1)}, u32[]{:S(2)}, u32[]{:S(2)}) collective-permute-start(bf16[29,64,128]{2,1,0:T(8,128)(2,1)S(1)} %collective-permute-done.27.refs_8_), channel_id=1, source_target_pairs={{0,16},{16,0},{32,48},{48,32},{64,80},{80,64},{96,112},{112,96},{1... | collective-permute-start | bytes 1425416 | tf_op jit(solution)/shard_map/ppermute | solution.py:61
  171.3 1.1 copy-start.20
  171.3 1.9 copy-start.15
  171.3 1.0 copy-start.16
  172.4 0.8 copy-start.18
where the time goes:
time: 189 us; the launch traced here: 188 us
  waiting for transfers between devices  91.9 us (49%)
  starting transfers between devices  53.8 us (28%)
  Pallas kernels  29.8 us (16%)
  local copies, waits for them, and re-layouts  8.19 us (4%)
  other arithmetic  3.52 us (2%)
    ppermute x16, waiting for transfers between devices, sent_col(): return lax.ppermute(array, 'col', order)  51.5 us
    ppermute x13, waiting for transfers between devices, sent_row(): return lax.ppermute(array, 'row', order)  40.4 us
    ppermute x13, starting transfers between devices, sent_row(): return lax.ppermute(array, 'row', order)  29.2 us
    ppermute x16, starting transfers between devices, sent_col(): return lax.ppermute(array, 'col', order)  24.5 us
    pallas_call x1, Pallas kernels, second_product(): pl.pallas_call(body, in_specs=[in_smem] * 3 + [anywhere] * len(operands)...  15 us
    pallas_call x1, Pallas kernels, first_product(): pl.pallas_call(body, in_specs=in_specs, out_specs=[in_vmem] * len(out_sha...  14.5 us
    unnamed x49, local copies, waits for them, and re-layouts  3.9 us
  transfers between devices with their start and end apart: 29, of which 14 were waited for; matrix products, arithmetic and copies ran while one was open for 3% of the time, Pallas kernels for 0%

commit v1 on v0

--- a/solution.py
+++ b/solution.py
@@ -99,6 +99,19 @@
         slab.append((piece, turn * CORES, ranges))
         other = nearest[2] if turn == 0 else sent_row(piece, 0, 1)
         slab.append((other, turn * CORES + 1, ranges))
+    return slab
+
+
+def halves_slab(low, high, strips):
+    ahead_low, behind_high = sent_row(low, 1, 0), sent_row(high, -1, 0)
+    ahead_high, behind_low = sent_row(high, 1, 0), sent_row(low, -1, 0)
+    far = (sent_row(ahead_low, 1, 0), sent_row(behind_high, -1, 0))
+    slab = []
+    chips = [(low, high), (behind_low, behind_high), (ahead_low, ahead_high), far]
+    for turn, pair in enumerate(chips):
+        for x, (start, size) in zip(pair, strips):
+            slab.append((x, turn * CORES, [(0, start, size)]))
+            slab.append((sent_row(x, 0, 1), turn * CORES + 1, [(0, start, size)]))
     return slab
 
 
@@ -212,7 +225,7 @@
             table_ref = refs.pop(0)
         slab_refs = [refs.pop(0) for _ in slab]
         piece_refs = [[refs.pop(0) for _ in pieces] for pieces, _ in panels]
-        done_ref = refs.pop(0)
+        done_refs = [refs.pop(0) for _ in strips]
         if make:
             table_out, left_ref, left_sem, right_ref, right_sem, table_ref, extra_ref, extra_sem, table_sem = refs
         else:
@@ -253,14 +266,15 @@
             for copy in copies:
                 copy.start()
 
-        def finish(member, at, sums):
-            done_ref[at] = (sums * scale).astype(done_ref.dtype)
-
-        run = block_sums(table_ref, left_ref, right_ref, spans, finish)
         for copies, first, at, size in runs:
             for copy in copies:
                 copy.wait()
-            run(first, at, size)
+            strip = max(i for i, start in enumerate(starts) if start <= at)
+
+            def finish(member, at, sums, done_ref=done_refs[strip], start=starts[strip]):
+                done_ref[at - start] = (sums * scale).astype(done_ref.dtype)
+
+            block_sums(table_ref, left_ref, right_ref, spans, finish)(first, at, size)
 
     anywhere = pl.BlockSpec(memory_space=pl.ANY)
     in_vmem = pl.BlockSpec(memory_space=pltpu.VMEM)
@@ -269,7 +283,7 @@
     flops = WEIGHT * count * block * lanes * groups * block
     cost = pl.CostEstimate(flops=flops, bytes_accessed=2 * sum(x.size for x in operands), transcendentals=0)
     in_specs = [in_smem, in_smem, in_vmem if make else in_smem] + [anywhere] * len(operands)
-    out_shape = [jax.ShapeDtypeStruct((count, block, lanes), jnp.bfloat16)]
+    out_shape = [jax.ShapeDtypeStruct((size, block, lanes), jnp.bfloat16) for _, size in strips]
     scratch = [
         pltpu.VMEM((positions, spans + 1, block, lanes), jnp.bfloat16),
         pltpu.SemaphoreType.DMA((left_moves,)),
@@ -293,7 +307,7 @@
         compiler_params=pltpu.CompilerParams(vmem_limit_bytes=60 * MIB),
         cost_estimate=cost,
     )(rows_at, groups_at, expected if make else table, *operands)
-    return out if make else (*out, table)
+    return (out[:-1], out[-1]) if make else (out, table)
 
 
 def second_product(table, rows_at, groups_at, slab, panels, strips, spans, scale, square, own):
@@ -403,11 +417,11 @@
     chips, _ = lax.optimization_barrier(((own, on_1, on_2, on_3), nearest))
     first_slab = swapped_slab(chips)
     panels = [(plane, axis) for axis, plane in enumerate(planes)]
-    square, table = first_product(
+    squares, table = first_product(
         None, expected, rows_at, groups_at, first_slab, panels, halves, spans, scale
     )
-    second_slab = row_slab(square, halves)
-    squares, all_strips = [square], [halves]
+    second_slab = halves_slab(*squares, halves)
+    all_strips = [[strip] for strip in halves]
     where = (table, rows_at, groups_at)
     return tuple(second_product(*where, second_slab, panels, all_strips, spans, scale, squares, own))
 

time: 189 us -> 183 us (0.968)
  waiting for transfers between devices: 91.9 us -> 77.7 us
  starting transfers between devices: 53.8 us -> 62.2 us
    ppermute x13 -> x18, waiting for transfers between devices: 40.4 us -> 26.4 us  [sent_row(): return lax.ppermute(array, 'row', order)]
    ppermute x13 -> x18, starting transfers between devices: 29.2 us -> 37.7 us  [sent_row(): return lax.ppermute(array, 'row', order)]
    unnamed x49 -> x59, local copies, waits for them, and re-layouts: 3.9 us -> 3.67 us
  transfers between devices with their start and end apart: 29 -> 34, of which waited for: 14 -> 15; matrix products, arithmetic and copies ran while one was open for 3% -> 3% of each run, Pallas kernels for 0% -> 0%
where the time goes in v1:
time: 183 us; the launch traced here: 182 us
  waiting for transfers between devices  77.7 us (42%)
  starting transfers between devices  62.2 us (34%)
  Pallas kernels  29.7 us (16%)
  local copies, waits for them, and re-layouts  7.92 us (4%)
  other arithmetic  3.63 us (2%)
    ppermute x16, waiting for transfers between devices, sent_col(): return lax.ppermute(array, 'col', order)  51.3 us
    ppermute x18, starting transfers between devices, sent_row(): return lax.ppermute(array, 'row', order)  37.7 us
    ppermute x18, waiting for transfers between devices, sent_row(): return lax.ppermute(array, 'row', order)  26.4 us
    ppermute x16, starting transfers between devices, sent_col(): return lax.ppermute(array, 'col', order)  24.6 us
    pallas_call x1, Pallas kernels, second_product(): pl.pallas_call(body, in_specs=[in_smem] * 3 + [anywhere] * len(operands)...  15 us
    pallas_call x1, Pallas kernels, first_product(): pl.pallas_call(body, in_specs=in_specs, out_specs=[in_vmem] * len(out_sha...  14.3 us
    unnamed x59, local copies, waits for them, and re-layouts  3.67 us
  transfers between devices with their start and end apart: 34, of which 15 were waited for; matrix products, arithmetic and copies ran while one was open for 3% of the time, Pallas kernels for 0%

profile of v1, /device:TPU:1, one launch (start us, length us, event | category | flops | bytes accessed | tf_op | source)
XLA Modules:
  0.0 182.4 jit_solution(18003002867764732103)
XLA Ops:
  0.6 0.8 dynamic-slice_bitcast_fusion
  1.4 1.2 copy-done
  2.6 0.4 shard_map.41
  3.0 3.6 %collective-permute-start.5 = (bf16[29,64,128]{2,1,0:T(8,128)(2,1)S(1)}, bf16[29,64,128]{2,1,0:T(8,128)(2,1)S(1)}, u32[]{:S(2)}, u32[]{:S(2)}) collective-permute-start(bf16[29,64,128]{2,1,0:T(8,128)(2,1)S(1)} %get-tuple-element.29), channel_id=1, source_target_pairs={{0,3},{1,0},{2,1},{3,2},{4,7},{5,4},{6,5},{7,6},{8,11},{9,8},{10,9... | collective-permute-start | bytes 1425416 | tf_op jit(solution)/shard_map/ppermute | solution.py:71
  6.6 2.5 %collective-permute-start.8 = (bf16[59,64,128]{2,1,0:T(8,128)(2,1)S(1)}, bf16[59,64,128]{2,1,0:T(8,128)(2,1)S(1)}, u32[]{:S(2)}, u32[]{:S(2)}) collective-permute-start(bf16[59,64,128]{2,1,0:T(8,128)(2,1)S(1)} %get-tuple-element.33.refs_1_.refs_28_), channel_id=1, source_target_pairs={{0,96},{16,112},{32,0},{48,16},{64,32},{80,48},{96,64},{112,80},{1... | collective-permute-start | bytes 2899976 | tf_op jit(solution)/shard_map/ppermute | solution.py:61
  9.1 3.8 %collective-permute-start.1 = (bf16[31,64,128]{2,1,0:T(8,128)(2,1)S(1)}, bf16[31,64,128]{2,1,0:T(8,128)(2,1)S(1)}, u32[]{:S(2)}, u32[]{:S(2)}) collective-permute-start(bf16[31,64,128]{2,1,0:T(8,128)(2,1)S(1)} %get-tuple-element.25), channel_id=1, source_target_pairs={{0,12},{1,13},{2,14},{3,15},{4,0},{5,1},{6,2},{7,3},{8,4},{9,5},{1... | collective-permute-start | bytes 1523720 | tf_op jit(solution)/shard_map/ppermute | solution.py:71
  12.9 3.3 %collective-permute-done.5 = bf16[29,64,128]{2,1,0:T(8,128)(2,1)S(1)} collective-permute-done((bf16[29,64,128]{2,1,0:T(8,128)(2,1)S(1)}, bf16[29,64,128]{2,1,0:T(8,128)(2,1)S(1)}, u32[]{:S(2)}, u32[]{:S(2)}) %collective-permute-start.5) | collective-permute-done | bytes 475168 | tf_op jit(solution)/shard_map/ppermute | solution.py:71
  16.2 3.5 %collective-permute-start.6 = (bf16[15,64,128]{2,1,0:T(8,128)(2,1)S(1)}, bf16[15,64,128]{2,1,0:T(8,128)(2,1)S(1)}, u32[]{:S(2)}, u32[]{:S(2)}) collective-permute-start(bf16[15,64,128]{2,1,0:T(8,128)(2,1)S(1)} %slice.34), channel_id=1, source_target_pairs={{0,3},{1,0},{2,1},{3,2},{4,7},{5,4},{6,5},{7,6},{8,11},{9,8},{10,9... | collective-permute-start | bytes 737288 | tf_op jit(solution)/shard_map/ppermute | solution.py:71
  19.7 1.8 collective-permute-done.4
  21.5 0.1 collective-permute-start.7
  21.6 0.9 collective-permute-done.1
  22.5 3.5 %collective-permute-start.2 = (bf16[16,64,128]{2,1,0:T(8,128)(2,1)S(1)}, bf16[16,64,128]{2,1,0:T(8,128)(2,1)S(1)}, u32[]{:S(2)}, u32[]{:S(2)}) collective-permute-start(bf16[16,64,128]{2,1,0:T(8,128)(2,1)S(1)} %slice.32), channel_id=1, source_target_pairs={{0,12},{1,13},{2,14},{3,15},{4,0},{5,1},{6,2},{7,3},{8,4},{9,5},{1... | collective-permute-start | bytes 786440 | tf_op jit(solution)/shard_map/ppermute | solution.py:71
  26.0 0.1 collective-permute-start.3
  26.1 1.6 collective-permute-done.7
  27.7 4.6 %collective-permute-done.3 = bf16[15,64,128]{2,1,0:T(8,128)(2,1)S(1)} collective-permute-done((bf16[15,64,128]{2,1,0:T(8,128)(2,1)S(1)}, bf16[15,64,128]{2,1,0:T(8,128)(2,1)S(1)}, u32[]{:S(2)}, u32[]{:S(2)}) %collective-permute-start.3) | collective-permute-done | bytes 245792 | tf_op jit(solution)/shard_map/ppermute | solution.py:71
  32.6 0.1 constant_dynamic-update-slice_fusion.1
  32.7 0.1 collective-permute-start.11
  32.8 2.7 %collective-permute-start.12 = (bf16[124,64,128]{2,1,0:T(8,128)(2,1)S(1)}, bf16[124,64,128]{2,1,0:T(8,128)(2,1)S(1)}, u32[]{:S(2)}, u32[]{:S(2)}) collective-permute-start(bf16[124,64,128]{2,1,0:T(8,128)(2,1)S(1)} %constant_dynamic-update-slice_fusion.refs_9_.refs_16_), channel_id=1, source_target_pairs={{0,3},{1,0},{2,1},{3,2},{4,7},{5,4},{6,5},{7,6},{8,11},{9,8},{10,9... | collective-permute-start | bytes 6094856 | tf_op jit(solution)/shard_map/ppermute | solution.py:71
  35.5 0.9 collective-permute-start.9
  36.6 0.7 collective-permute-start.13
  37.3 2.2 %collective-permute-start.14 = (bf16[116,64,128]{2,1,0:T(8,128)(2,1)S(1)}, bf16[116,64,128]{2,1,0:T(8,128)(2,1)S(1)}, u32[]{:S(2)}, u32[]{:S(2)}) collective-permute-start(bf16[116,64,128]{2,1,0:T(8,128)(2,1)S(1)} %constant_dynamic-update-slice_fusion.4.refs_14_.refs_21_), channel_id=1, source_target_pairs={{0,12},{1,13},{2,14},{3,15},{4,0},{5,1},{6,2},{7,3},{8,4},{9,5},{1... | collective-permute-start | bytes 5701640 | tf_op jit(solution)/shard_map/ppermute | solution.py:71
  39.5 14.8 %collective-permute-done.9.refs_5_ = bf16[59,64,128]{2,1,0:T(8,128)(2,1)S(1)} collective-permute-done((bf16[59,64,128]{2,1,0:T(8,128)(2,1)S(1)}, bf16[59,64,128]{2,1,0:T(8,128)(2,1)S(1)}, u32[]{:S(2)}, u32[]{:S(2)}) %collective-permute-start.9) | collective-permute-done | bytes 966688 | tf_op jit(solution)/shard_map/ppermute | solution.py:61
  54.3 2.4 %collective-permute-start.10 = (bf16[59,64,128]{2,1,0:T(8,128)(2,1)S(1)}, bf16[59,64,128]{2,1,0:T(8,128)(2,1)S(1)}, u32[]{:S(2)}, u32[]{:S(2)}) collective-permute-start(bf16[59,64,128]{2,1,0:T(8,128)(2,1)S(1)} %collective-permute-done.9.refs_5_), channel_id=1, source_target_pairs={{0,96},{16,112},{32,0},{48,16},{64,32},{80,48},{96,64},{112,80},{1... | collective-permute-start | bytes 2899976 | tf_op jit(solution)/shard_map/ppermute | solution.py:61
  56.7 20.2 %collective-permute-done.13.refs_15_.refs_22_ = bf16[116,64,128]{2,1,0:T(8,128)(2,1)S(1)} collective-permute-done((bf16[116,64,128]{2,1,0:T(8,128)(2,1)S(1)}, bf16[116,64,128]{2,1,0:T(8,128)(2,1)S(1)}, u32[]{:S(2)}, u32[]{:S(2)}) %collective-permute-start.13) | collective-permute-done | bytes 1900576 | tf_op jit(solution)/shard_map/ppermute | solution.py:71
  76.9 0.2 collective-permute-done.14.refs_16_.refs_23_
  77.1 2.6 %pad_maximum_fusion = bf16[236,64,128]{2,1,0:T(8,128)(2,1)} fusion(bf16[59,64,128]{2,1,0:T(8,128)(2,1)S(1)} %collective-permute-done.10.refs_7_, bf16[59,64,128]{2,1,0:T(8,128)(2,1)S(1)} %collective-permute-done.9.refs_5_, bf16[59,64,128]{2,1,0:T(8,128)(2,1)S(1)} %collective-permute-done.8.refs_3_, bf16[59,64,128]{2,1,0:T(8,128)(2,1)S(1)} %get-tuple-element.33.refs_1_.refs_28_), kind=kLoop, calls=%fused_computation | loop fusion | flops 5799936 | bytes 7733248 | tf_op jit(solution)/shard_map/concatenate | solution.py:120
  79.7 4.8 %collective-permute-start.15 = (bf16[236,64,128]{2,1,0:T(8,128)(2,1)}, bf16[236,64,128]{2,1,0:T(8,128)(2,1)}, u32[]{:S(2)}, u32[]{:S(2)}) collective-permute-start(bf16[236,64,128]{2,1,0:T(8,128)(2,1)} %pad_maximum_fusion), channel_id=1, source_target_pairs={{0,16},{16,0},{32,48},{48,32},{64,80},{80,64},{96,112},{112,96},{1... | collective-permute-start | bytes 11599880 | tf_op jit(solution)/shard_map/ppermute | solution.py:61
  84.6 1.6 collective-permute-start.16
  86.2 0.1 collective-permute-start.17
  86.4 2.7 %collective-permute-start.18 = (bf16[58,64,128]{2,1,0:T(8,128)(2,1)S(1)}, bf16[58,64,128]{2,1,0:T(8,128)(2,1)}, u32[]{:S(2)}, u32[]{:S(2)}) collective-permute-start(bf16[58,64,128]{2,1,0:T(8,128)(2,1)S(1)} %slice.38), channel_id=1, source_target_pairs={{0,12},{1,13},{2,14},{3,15},{4,0},{5,1},{6,2},{7,3},{8,4},{9,5},{1... | collective-permute-start | bytes 2850824 | tf_op jit(solution)/shard_map/ppermute | solution.py:71
  89.1 1.0 slice.39
  90.1 0.6 broadcast.35
  90.7 0.7 reduce.3
  91.4 0.1 eq.68
  91.5 0.1 copy.4
  91.6 0.2 select_reduce_fusion
  91.8 0.1 broadcast_add_fusion
  91.9 0.6 pad.8.refs_0_
  92.5 0.6 stack.86.rows_ref
  93.1 0.7 stack.103.groups_ref
  93.8 14.2 %collective-permute-done.18.refs_17_.refs_24_ = bf16[58,64,128]{2,1,0:T(8,128)(2,1)} collective-permute-done((bf16[58,64,128]{2,1,0:T(8,128)(2,1)S(1)}, bf16[58,64,128]{2,1,0:T(8,128)(2,1)}, u32[]{:S(2)}, u32[]{:S(2)}) %collective-permute-start.18) | collective-permute-done | bytes 950304 | tf_op jit(solution)/shard_map/ppermute | solution.py:71
  108.0 4.5 %collective-permute-done.19.refs_18_.refs_25_ = bf16[58,64,128]{2,1,0:T(8,128)(2,1)} collective-permute-done((bf16[58,64,128]{2,1,0:T(8,128)(2,1)}, bf16[58,64,128]{2,1,0:T(8,128)(2,1)}, u32[]{:S(2)}, u32[]{:S(2)}) %collective-permute-start.19) | collective-permute-done | bytes 950304 | tf_op jit(solution)/shard_map/ppermute | solution.py:71
  112.5 14.3 %shard_map.42 = (bf16[30,64,128]{2,1,0:T(8,128)(2,1)}, bf16[29,64,128]{2,1,0:T(8,128)(2,1)}, s32[16,128]{1,0:T(8,128)}) custom-call(s32[8]{0:T(128)} %stack.86.rows_ref, s32[16]{0:T(128)} %stack.103.groups_ref, s32[16,128]{1,0:T(8,128)} %pad.8.refs_0_, bf16[59,64,128]{2,1,0:T(8,128)(2,1)} %copy-done.1, ...), custom_call_target="tpu_custom_call" | custom-call | flops 23756537856 | bytes 35061760 | tf_op jit(solution)/shard_map/pallas_call | solution.py:301
  126.8 1.3 collective-permute-start.26
  128.1 0.2 collective-permute-start.24
  128.3 2.4 %collective-permute-start.28 = (bf16[29,64,128]{2,1,0:T(8,128)(2,1)}, bf16[29,64,128]{2,1,0:T(8,128)(2,1)S(1)}, u32[]{:S(2)}, u32[]{:S(2)}) collective-permute-start(bf16[29,64,128]{2,1,0:T(8,128)(2,1)} %get-tuple-element.39.refs_2_.refs_27_), channel_id=1, source_target_pairs={{0,96},{16,112},{32,0},{48,16},{64,32},{80,48},{96,64},{112,80},{1... | collective-permute-start | bytes 1425416 | tf_op jit(solution)/shard_map/ppermute | solution.py:61
  130.8 3.6 %collective-permute-start.21 = (bf16[29,64,128]{2,1,0:T(8,128)(2,1)}, bf16[29,64,128]{2,1,0:T(8,128)(2,1)S(1)}, u32[]{:S(2)}, u32[]{:S(2)}) collective-permute-start(bf16[29,64,128]{2,1,0:T(8,128)(2,1)} %get-tuple-element.39.refs_2_.refs_27_), channel_id=1, source_target_pairs={{0,16},{16,0},{32,48},{48,32},{64,80},{80,64},{96,112},{112,96},{1... | collective-permute-start | bytes 1425416 | tf_op jit(solution)/shard_map/ppermute | solution.py:61
  134.3 4.6 %collective-permute-done.24.refs_6_ = bf16[29,64,128]{2,1,0:T(8,128)(2,1)S(1)} collective-permute-done((bf16[29,64,128]{2,1,0:T(8,128)(2,1)}, bf16[29,64,128]{2,1,0:T(8,128)(2,1)S(1)}, u32[]{:S(2)}, u32[]{:S(2)}) %collective-permute-start.24) | collective-permute-done | bytes 475168 | tf_op jit(solution)/shard_map/ppermute | solution.py:61
  138.9 7.4 %collective-permute-start.20 = (bf16[30,64,128]{2,1,0:T(8,128)(2,1)}, bf16[30,64,128]{2,1,0:T(8,128)(2,1)S(1)}, u32[]{:S(2)}, u32[]{:S(2)}) collective-permute-start(bf16[30,64,128]{2,1,0:T(8,128)(2,1)} %get-tuple-element.38.refs_0_.refs_26_), channel_id=1, source_target_pairs={{0,16},{16,0},{32,48},{48,32},{64,80},{80,64},{96,112},{112,96},{1... | collective-permute-start | bytes 1474568 | tf_op jit(solution)/shard_map/ppermute | solution.py:61
  146.3 1.0 collective-permute-done.28.refs_10_
  147.3 0.5 collective-permute-start.32
  147.8 6.7 %collective-permute-start.25 = (bf16[29,64,128]{2,1,0:T(8,128)(2,1)S(1)}, bf16[29,64,128]{2,1,0:T(8,128)(2,1)S(1)}, u32[]{:S(2)}, u32[]{:S(2)}) collective-permute-start(bf16[29,64,128]{2,1,0:T(8,128)(2,1)S(1)} %collective-permute-done.24.refs_6_), channel_id=1, source_target_pairs={{0,16},{16,0},{32,48},{48,32},{64,80},{80,64},{96,112},{112,96},{1... | collective-permute-start | bytes 1425416 | tf_op jit(solution)/shard_map/ppermute | solution.py:61
  154.5 0.8 collective-permute-start.23
  155.2 0.1 collective-permute-start.27
  155.3 4.3 %collective-permute-done.30.refs_12_ = bf16[30,64,128]{2,1,0:T(8,128)(2,1)S(1)} collective-permute-done((bf16[30,64,128]{2,1,0:T(8,128)(2,1)S(1)}, bf16[30,64,128]{2,1,0:T(8,128)(2,1)S(1)}, u32[]{:S(2)}, u32[]{:S(2)}) %collective-permute-start.30) | collective-permute-done | bytes 491552 | tf_op jit(solution)/shard_map/ppermute | solution.py:61
  159.6 1.8 collective-permute-start.31
  161.4 2.1 %collective-permute-start.29 = (bf16[29,64,128]{2,1,0:T(8,128)(2,1)S(1)}, bf16[29,64,128]{2,1,0:T(8,128)(2,1)S(1)}, u32[]{:S(2)}, u32[]{:S(2)}) collective-permute-start(bf16[29,64,128]{2,1,0:T(8,128)(2,1)S(1)} %collective-permute-done.28.refs_10_), channel_id=1, source_target_pairs={{0,16},{16,0},{32,48},{48,32},{64,80},{80,64},{96,112},{112,96},{1... | collective-permute-start | bytes 1425416 | tf_op jit(solution)/shard_map/ppermute | solution.py:61
  163.5 0.3 collective-permute-start.33
  163.8 1.1 collective-permute-done.29.refs_11_
  165.0 0.7 collective-permute-done.33.refs_15_
  165.7 0.1 copy-done.24
  165.8 0.7 copy-done.25
  166.5 0.7 copy-done.18
  167.2 15.0 %shard_map.43 = (bf16[64,7552]{1,0:T(8,128)(2,1)}, bf16[64,7552]{1,0:T(8,128)(2,1)}) custom-call(s32[16,128]{1,0:T(8,128)} %get-tuple-element.37.table_ref, s32[8]{0:T(128)} %stack.86.rows_ref, s32[16]{0:T(128)} %stack.103.groups_ref, bf16[30,64,128]{2,1,0:T(8,128)(2,1)} %get-tuple-element.38.refs_0_.refs_26_, bf16[30,64,128]{2,1,0:T(8,128)(2,1)} %copy-done.14, ...), custom_call_target="tpu_custom_call" | custom-call | flops 23756537856 | bytes 23461888 | tf_op jit(solution)/shard_map/pallas_call | solution.py:364
  (90 shorter events, 0.9 us)
Async XLA Ops:
  1.4 1.2 copy-start
  3.0 74.1 %copy-start.1 = (bf16[59,64,128]{2,1,0:T(8,128)(2,1)}, bf16[59,64,128]{2,1,0:T(8,128)(2,1)S(1)}, u32[]{:S(2)}) copy-start(bf16[59,64,128]{2,1,0:T(8,128)(2,1)S(1)} %get-tuple-element.33.refs_1_.refs_28_) | copy-start | bytes 2899972
  3.0 13.2 %collective-permute-start.5 = (bf16[29,64,128]{2,1,0:T(8,128)(2,1)S(1)}, bf16[29,64,128]{2,1,0:T(8,128)(2,1)S(1)}, u32[]{:S(2)}, u32[]{:S(2)}) collective-permute-start(bf16[29,64,128]{2,1,0:T(8,128)(2,1)S(1)} %get-tuple-element.29), channel_id=1, source_target_pairs={{0,3},{1,0},{2,1},{3,2},{4,7},{5,4},{6,5},{7,6},{8,11},{9,8},{10,9... | collective-permute-start | bytes 1425416 | tf_op jit(solution)/shard_map/ppermute | solution.py:71
  6.6 25.8 %collective-permute-start.8 = (bf16[59,64,128]{2,1,0:T(8,128)(2,1)S(1)}, bf16[59,64,128]{2,1,0:T(8,128)(2,1)S(1)}, u32[]{:S(2)}, u32[]{:S(2)}) collective-permute-start(bf16[59,64,128]{2,1,0:T(8,128)(2,1)S(1)} %get-tuple-element.33.refs_1_.refs_28_), channel_id=1, source_target_pairs={{0,96},{16,112},{32,0},{48,16},{64,32},{80,48},{96,64},{112,80},{1... | collective-permute-start | bytes 2899976 | tf_op jit(solution)/shard_map/ppermute | solution.py:61
  9.1 12.3 %collective-permute-start.4 = (bf16[29,64,128]{2,1,0:T(8,128)(2,1)S(1)}, bf16[29,64,128]{2,1,0:T(8,128)(2,1)S(1)}, u32[]{:S(2)}, u32[]{:S(2)}) collective-permute-start(bf16[29,64,128]{2,1,0:T(8,128)(2,1)S(1)} %get-tuple-element.29), channel_id=1, source_target_pairs={{0,1},{1,2},{2,3},{3,0},{4,5},{5,6},{6,7},{7,4},{8,9},{9,10},{10,1... | collective-permute-start | bytes 1425416 | tf_op jit(solution)/shard_map/ppermute | solution.py:71
  9.1 13.4 %collective-permute-start.1 = (bf16[31,64,128]{2,1,0:T(8,128)(2,1)S(1)}, bf16[31,64,128]{2,1,0:T(8,128)(2,1)S(1)}, u32[]{:S(2)}, u32[]{:S(2)}) collective-permute-start(bf16[31,64,128]{2,1,0:T(8,128)(2,1)S(1)} %get-tuple-element.25), channel_id=1, source_target_pairs={{0,12},{1,13},{2,14},{3,15},{4,0},{5,1},{6,2},{7,3},{8,4},{9,5},{1... | collective-permute-start | bytes 1523720 | tf_op jit(solution)/shard_map/ppermute | solution.py:71
  12.9 13.1 %collective-permute-start = (bf16[31,64,128]{2,1,0:T(8,128)(2,1)S(1)}, bf16[31,64,128]{2,1,0:T(8,128)(2,1)S(1)}, u32[]{:S(2)}, u32[]{:S(2)}) collective-permute-start(bf16[31,64,128]{2,1,0:T(8,128)(2,1)S(1)} %get-tuple-element.25), channel_id=1, source_target_pairs={{0,4},{1,5},{2,6},{3,7},{4,8},{5,9},{6,10},{7,11},{8,12},{9,13},{1... | collective-permute-start | bytes 1523720 | tf_op jit(solution)/shard_map/ppermute | solution.py:71
  16.2 11.5 %collective-permute-start.6 = (bf16[15,64,128]{2,1,0:T(8,128)(2,1)S(1)}, bf16[15,64,128]{2,1,0:T(8,128)(2,1)S(1)}, u32[]{:S(2)}, u32[]{:S(2)}) collective-permute-start(bf16[15,64,128]{2,1,0:T(8,128)(2,1)S(1)} %slice.34), channel_id=1, source_target_pairs={{0,3},{1,0},{2,1},{3,2},{4,7},{5,4},{6,5},{7,6},{8,11},{9,8},{10,9... | collective-permute-start | bytes 737288 | tf_op jit(solution)/shard_map/ppermute | solution.py:71
  21.5 6.2 %collective-permute-start.7 = (bf16[14,64,128]{2,1,0:T(8,128)(2,1)S(1)}, bf16[14,64,128]{2,1,0:T(8,128)(2,1)S(1)}, u32[]{:S(2)}, u32[]{:S(2)}) collective-permute-start(bf16[14,64,128]{2,1,0:T(8,128)(2,1)S(1)} %slice.35), channel_id=1, source_target_pairs={{0,1},{1,2},{2,3},{3,0},{4,5},{5,6},{6,7},{7,4},{8,9},{9,10},{10,1... | collective-permute-start | bytes 688136 | tf_op jit(solution)/shard_map/ppermute | solution.py:71
  22.5 9.8 %collective-permute-start.2 = (bf16[16,64,128]{2,1,0:T(8,128)(2,1)S(1)}, bf16[16,64,128]{2,1,0:T(8,128)(2,1)S(1)}, u32[]{:S(2)}, u32[]{:S(2)}) collective-permute-start(bf16[16,64,128]{2,1,0:T(8,128)(2,1)S(1)} %slice.32), channel_id=1, source_target_pairs={{0,12},{1,13},{2,14},{3,15},{4,0},{5,1},{6,2},{7,3},{8,4},{9,5},{1... | collective-permute-start | bytes 786440 | tf_op jit(solution)/shard_map/ppermute | solution.py:71
  26.0 6.3 %collective-permute-start.3 = (bf16[15,64,128]{2,1,0:T(8,128)(2,1)S(1)}, bf16[15,64,128]{2,1,0:T(8,128)(2,1)S(1)}, u32[]{:S(2)}, u32[]{:S(2)}) collective-permute-start(bf16[15,64,128]{2,1,0:T(8,128)(2,1)S(1)} %slice.33), channel_id=1, source_target_pairs={{0,4},{1,5},{2,6},{3,7},{4,8},{5,9},{6,10},{7,11},{8,12},{9,13},{1... | collective-permute-start | bytes 737288 | tf_op jit(solution)/shard_map/ppermute | solution.py:71
  32.4 44.7 %copy-start.2 = (bf16[59,64,128]{2,1,0:T(8,128)(2,1)}, bf16[59,64,128]{2,1,0:T(8,128)(2,1)S(1)}, u32[]{:S(2)}) copy-start(bf16[59,64,128]{2,1,0:T(8,128)(2,1)S(1)} %collective-permute-done.8.refs_3_) | copy-start | bytes 2899972
  32.7 44.3 %copy-start.9 = (bf16[124,64,128]{2,1,0:T(8,128)(2,1)}, bf16[124,64,128]{2,1,0:T(8,128)(2,1)S(1)}, u32[]{:S(2)}) copy-start(bf16[124,64,128]{2,1,0:T(8,128)(2,1)S(1)} %constant_dynamic-update-slice_fusion.refs_9_.refs_16_) | copy-start | bytes 6094852
  32.7 44.3 %collective-permute-start.11 = (bf16[124,64,128]{2,1,0:T(8,128)(2,1)S(1)}, bf16[124,64,128]{2,1,0:T(8,128)(2,1)S(1)}, u32[]{:S(2)}, u32[]{:S(2)}) collective-permute-start(bf16[124,64,128]{2,1,0:T(8,128)(2,1)S(1)} %constant_dynamic-update-slice_fusion.refs_9_.refs_16_), channel_id=1, source_target_pairs={{0,1},{1,2},{2,3},{3,0},{4,5},{5,6},{6,7},{7,4},{8,9},{9,10},{10,1... | collective-permute-start | bytes 6094856 | tf_op jit(solution)/shard_map/ppermute | solution.py:71
  32.8 44.3 %collective-permute-start.12 = (bf16[124,64,128]{2,1,0:T(8,128)(2,1)S(1)}, bf16[124,64,128]{2,1,0:T(8,128)(2,1)S(1)}, u32[]{:S(2)}, u32[]{:S(2)}) collective-permute-start(bf16[124,64,128]{2,1,0:T(8,128)(2,1)S(1)} %constant_dynamic-update-slice_fusion.refs_9_.refs_16_), channel_id=1, source_target_pairs={{0,3},{1,0},{2,1},{3,2},{4,7},{5,4},{6,5},{7,6},{8,11},{9,8},{10,9... | collective-permute-start | bytes 6094856 | tf_op jit(solution)/shard_map/ppermute | solution.py:71
  35.5 18.8 %collective-permute-start.9 = (bf16[59,64,128]{2,1,0:T(8,128)(2,1)S(1)}, bf16[59,64,128]{2,1,0:T(8,128)(2,1)S(1)}, u32[]{:S(2)}, u32[]{:S(2)}) collective-permute-start(bf16[59,64,128]{2,1,0:T(8,128)(2,1)S(1)} %collective-permute-done.8.refs_3_), channel_id=1, source_target_pairs={{0,96},{16,112},{32,0},{48,16},{64,32},{80,48},{96,64},{112,80},{1... | collective-permute-start | bytes 2899976 | tf_op jit(solution)/shard_map/ppermute | solution.py:61
  36.6 40.4 %copy-start.10 = (bf16[116,64,128]{2,1,0:T(8,128)(2,1)}, bf16[116,64,128]{2,1,0:T(8,128)(2,1)S(1)}, u32[]{:S(2)}) copy-start(bf16[116,64,128]{2,1,0:T(8,128)(2,1)S(1)} %constant_dynamic-update-slice_fusion.4.refs_14_.refs_21_) | copy-start | bytes 5701636
  36.6 40.2 %collective-permute-start.13 = (bf16[116,64,128]{2,1,0:T(8,128)(2,1)S(1)}, bf16[116,64,128]{2,1,0:T(8,128)(2,1)S(1)}, u32[]{:S(2)}, u32[]{:S(2)}) collective-permute-start(bf16[116,64,128]{2,1,0:T(8,128)(2,1)S(1)} %constant_dynamic-update-slice_fusion.4.refs_14_.refs_21_), channel_id=1, source_target_pairs={{0,4},{1,5},{2,6},{3,7},{4,8},{5,9},{6,10},{7,11},{8,12},{9,13},{1... | collective-permute-start | bytes 5701640 | tf_op jit(solution)/shard_map/ppermute | solution.py:71
  37.3 39.7 %collective-permute-start.14 = (bf16[116,64,128]{2,1,0:T(8,128)(2,1)S(1)}, bf16[116,64,128]{2,1,0:T(8,128)(2,1)S(1)}, u32[]{:S(2)}, u32[]{:S(2)}) collective-permute-start(bf16[116,64,128]{2,1,0:T(8,128)(2,1)S(1)} %constant_dynamic-update-slice_fusion.4.refs_14_.refs_21_), channel_id=1, source_target_pairs={{0,12},{1,13},{2,14},{3,15},{4,0},{5,1},{6,2},{7,3},{8,4},{9,5},{1... | collective-permute-start | bytes 5701640 | tf_op jit(solution)/shard_map/ppermute | solution.py:71
  54.3 25.4 %copy-start.3 = (bf16[59,64,128]{2,1,0:T(8,128)(2,1)}, bf16[59,64,128]{2,1,0:T(8,128)(2,1)S(1)}, u32[]{:S(2)}) copy-start(bf16[59,64,128]{2,1,0:T(8,128)(2,1)S(1)} %collective-permute-done.9.refs_5_) | copy-start | bytes 2899972
  54.3 22.7 %collective-permute-start.10 = (bf16[59,64,128]{2,1,0:T(8,128)(2,1)S(1)}, bf16[59,64,128]{2,1,0:T(8,128)(2,1)S(1)}, u32[]{:S(2)}, u32[]{:S(2)}) collective-permute-start(bf16[59,64,128]{2,1,0:T(8,128)(2,1)S(1)} %collective-permute-done.9.refs_5_), channel_id=1, source_target_pairs={{0,96},{16,112},{32,0},{48,16},{64,32},{80,48},{96,64},{112,80},{1... | collective-permute-start | bytes 2899976 | tf_op jit(solution)/shard_map/ppermute | solution.py:61
  76.9 12.3 %copy-start.7 = (bf16[116,64,128]{2,1,0:T(8,128)(2,1)}, bf16[116,64,128]{2,1,0:T(8,128)(2,1)S(1)}, u32[]{:S(2)}) copy-start(bf16[116,64,128]{2,1,0:T(8,128)(2,1)S(1)} %collective-permute-done.13.refs_15_.refs_22_) | copy-start | bytes 5701636
  77.0 9.4 %copy-start.8 = (bf16[116,64,128]{2,1,0:T(8,128)(2,1)}, bf16[116,64,128]{2,1,0:T(8,128)(2,1)S(1)}, u32[]{:S(2)}) copy-start(bf16[116,64,128]{2,1,0:T(8,128)(2,1)S(1)} %collective-permute-done.14.refs_16_.refs_23_) | copy-start | bytes 5701636
  77.0 2.7 %copy-start.4 = (bf16[59,64,128]{2,1,0:T(8,128)(2,1)}, bf16[59,64,128]{2,1,0:T(8,128)(2,1)S(1)}, u32[]{:S(2)}) copy-start(bf16[59,64,128]{2,1,0:T(8,128)(2,1)S(1)} %collective-permute-done.10.refs_7_) | copy-start | bytes 2899972
  77.1 9.1 %copy-start.5 = (bf16[124,64,128]{2,1,0:T(8,128)(2,1)}, bf16[124,64,128]{2,1,0:T(8,128)(2,1)S(1)}, u32[]{:S(2)}) copy-start(bf16[124,64,128]{2,1,0:T(8,128)(2,1)S(1)} %collective-permute-done.11.refs_10_.refs_17_) | copy-start | bytes 6094852
  77.1 7.4 %copy-start.6 = (bf16[124,64,128]{2,1,0:T(8,128)(2,1)}, bf16[124,64,128]{2,1,0:T(8,128)(2,1)S(1)}, u32[]{:S(2)}) copy-start(bf16[124,64,128]{2,1,0:T(8,128)(2,1)S(1)} %collective-permute-done.12.refs_11_.refs_18_) | copy-start | bytes 6094852
  79.7 32.7 %collective-permute-start.15 = (bf16[236,64,128]{2,1,0:T(8,128)(2,1)}, bf16[236,64,128]{2,1,0:T(8,128)(2,1)}, u32[]{:S(2)}, u32[]{:S(2)}) collective-permute-start(bf16[236,64,128]{2,1,0:T(8,128)(2,1)} %pad_maximum_fusion), channel_id=1, source_target_pairs={{0,16},{16,0},{32,48},{48,32},{64,80},{80,64},{96,112},{112,96},{1... | collective-permute-start | bytes 11599880 | tf_op jit(solution)/shard_map/ppermute | solution.py:61
  84.6 27.9 %collective-permute-start.16 = (bf16[62,64,128]{2,1,0:T(8,128)(2,1)S(1)}, bf16[62,64,128]{2,1,0:T(8,128)(2,1)}, u32[]{:S(2)}, u32[]{:S(2)}) collective-permute-start(bf16[62,64,128]{2,1,0:T(8,128)(2,1)S(1)} %slice.36), channel_id=1, source_target_pairs={{0,3},{1,0},{2,1},{3,2},{4,7},{5,4},{6,5},{7,6},{8,11},{9,8},{10,9... | collective-permute-start | bytes 3047432 | tf_op jit(solution)/shard_map/ppermute | solution.py:71
  86.2 4.5 %copy-start.11 = (s32[944,1]{0,1:T(1,128)S(1)}, s32[944,1]{0,1:T(1,128)}, u32[]{:S(2)}) copy-start(s32[944,1]{0,1:T(1,128)} %param.3) | copy-start | bytes 11332
  86.2 26.2 %collective-permute-start.17 = (bf16[62,64,128]{2,1,0:T(8,128)(2,1)S(1)}, bf16[62,64,128]{2,1,0:T(8,128)(2,1)}, u32[]{:S(2)}, u32[]{:S(2)}) collective-permute-start(bf16[62,64,128]{2,1,0:T(8,128)(2,1)S(1)} %slice.37), channel_id=1, source_target_pairs={{0,1},{1,2},{2,3},{3,0},{4,5},{5,6},{6,7},{7,4},{8,9},{9,10},{10,1... | collective-permute-start | bytes 3047432 | tf_op jit(solution)/shard_map/ppermute | solution.py:71
  86.4 21.6 %collective-permute-start.18 = (bf16[58,64,128]{2,1,0:T(8,128)(2,1)S(1)}, bf16[58,64,128]{2,1,0:T(8,128)(2,1)}, u32[]{:S(2)}, u32[]{:S(2)}) collective-permute-start(bf16[58,64,128]{2,1,0:T(8,128)(2,1)S(1)} %slice.38), channel_id=1, source_target_pairs={{0,12},{1,13},{2,14},{3,15},{4,0},{5,1},{6,2},{7,3},{8,4},{9,5},{1... | collective-permute-start | bytes 2850824 | tf_op jit(solution)/shard_map/ppermute | solution.py:71
  90.1 22.3 %collective-permute-start.19 = (bf16[58,64,128]{2,1,0:T(8,128)(2,1)}, bf16[58,64,128]{2,1,0:T(8,128)(2,1)}, u32[]{:S(2)}, u32[]{:S(2)}) collective-permute-start(bf16[58,64,128]{2,1,0:T(8,128)(2,1)} %slice.39), channel_id=1, source_target_pairs={{0,4},{1,5},{2,6},{3,7},{4,8},{5,9},{6,10},{7,11},{8,12},{9,13},{1... | collective-permute-start | bytes 2850824 | tf_op jit(solution)/shard_map/ppermute | solution.py:71
  126.8 19.5 %collective-permute-start.26 = (bf16[30,64,128]{2,1,0:T(8,128)(2,1)}, bf16[30,64,128]{2,1,0:T(8,128)(2,1)S(1)}, u32[]{:S(2)}, u32[]{:S(2)}) collective-permute-start(bf16[30,64,128]{2,1,0:T(8,128)(2,1)} %get-tuple-element.38.refs_0_.refs_26_), channel_id=1, source_target_pairs={{0,96},{16,112},{32,0},{48,16},{64,32},{80,48},{96,64},{112,80},{1... | collective-permute-start | bytes 1474568 | tf_op jit(solution)/shard_map/ppermute | solution.py:61
  128.1 10.8 %collective-permute-start.24 = (bf16[29,64,128]{2,1,0:T(8,128)(2,1)}, bf16[29,64,128]{2,1,0:T(8,128)(2,1)S(1)}, u32[]{:S(2)}, u32[]{:S(2)}) collective-permute-start(bf16[29,64,128]{2,1,0:T(8,128)(2,1)} %get-tuple-element.39.refs_2_.refs_27_), channel_id=1, source_target_pairs={{0,32},{16,48},{32,64},{48,80},{64,96},{80,112},{96,0},{112,16},{1... | collective-permute-start | bytes 1425416 | tf_op jit(solution)/shard_map/ppermute | solution.py:61
  128.3 19.0 %collective-permute-start.28 = (bf16[29,64,128]{2,1,0:T(8,128)(2,1)}, bf16[29,64,128]{2,1,0:T(8,128)(2,1)S(1)}, u32[]{:S(2)}, u32[]{:S(2)}) collective-permute-start(bf16[29,64,128]{2,1,0:T(8,128)(2,1)} %get-tuple-element.39.refs_2_.refs_27_), channel_id=1, source_target_pairs={{0,96},{16,112},{32,0},{48,16},{64,32},{80,48},{96,64},{112,80},{1... | collective-permute-start | bytes 1425416 | tf_op jit(solution)/shard_map/ppermute | solution.py:61
  130.8 17.0 %collective-permute-start.21 = (bf16[29,64,128]{2,1,0:T(8,128)(2,1)}, bf16[29,64,128]{2,1,0:T(8,128)(2,1)S(1)}, u32[]{:S(2)}, u32[]{:S(2)}) collective-permute-start(bf16[29,64,128]{2,1,0:T(8,128)(2,1)} %get-tuple-element.39.refs_2_.refs_27_), channel_id=1, source_target_pairs={{0,16},{16,0},{32,48},{48,32},{64,80},{80,64},{96,112},{112,96},{1... | collective-permute-start | bytes 1425416 | tf_op jit(solution)/shard_map/ppermute | solution.py:61
  134.3 20.2 %collective-permute-start.22 = (bf16[30,64,128]{2,1,0:T(8,128)(2,1)}, bf16[30,64,128]{2,1,0:T(8,128)(2,1)S(1)}, u32[]{:S(2)}, u32[]{:S(2)}) collective-permute-start(bf16[30,64,128]{2,1,0:T(8,128)(2,1)} %get-tuple-element.38.refs_0_.refs_26_), channel_id=1, source_target_pairs={{0,32},{16,48},{32,64},{48,80},{64,96},{80,112},{96,0},{112,16},{1... | collective-permute-start | bytes 1474568 | tf_op jit(solution)/shard_map/ppermute | solution.py:61
  138.9 27.6 %copy-start.19 = (bf16[29,64,128]{2,1,0:T(8,128)(2,1)}, bf16[29,64,128]{2,1,0:T(8,128)(2,1)S(1)}, u32[]{:S(2)}) copy-start(bf16[29,64,128]{2,1,0:T(8,128)(2,1)S(1)} %collective-permute-done.24.refs_6_) | copy-start | bytes 1425412
  138.9 16.4 %collective-permute-start.20 = (bf16[30,64,128]{2,1,0:T(8,128)(2,1)}, bf16[30,64,128]{2,1,0:T(8,128)(2,1)S(1)}, u32[]{:S(2)}, u32[]{:S(2)}) collective-permute-start(bf16[30,64,128]{2,1,0:T(8,128)(2,1)} %get-tuple-element.38.refs_0_.refs_26_), channel_id=1, source_target_pairs={{0,16},{16,0},{32,48},{48,32},{64,80},{80,64},{96,112},{112,96},{1... | collective-permute-start | bytes 1474568 | tf_op jit(solution)/shard_map/ppermute | solution.py:61
  146.3 20.1 %copy-start.12 = (bf16[30,64,128]{2,1,0:T(8,128)(2,1)}, bf16[30,64,128]{2,1,0:T(8,128)(2,1)S(1)}, u32[]{:S(2)}) copy-start(bf16[30,64,128]{2,1,0:T(8,128)(2,1)S(1)} %collective-permute-done.26.refs_8_) | copy-start | bytes 1474564
  146.3 13.3 %collective-permute-start.30 = (bf16[30,64,128]{2,1,0:T(8,128)(2,1)S(1)}, bf16[30,64,128]{2,1,0:T(8,128)(2,1)S(1)}, u32[]{:S(2)}, u32[]{:S(2)}) collective-permute-start(bf16[30,64,128]{2,1,0:T(8,128)(2,1)S(1)} %collective-permute-done.26.refs_8_), channel_id=1, source_target_pairs={{0,96},{16,112},{32,0},{48,16},{64,32},{80,48},{96,64},{112,80},{1... | collective-permute-start | bytes 1474568 | tf_op jit(solution)/shard_map/ppermute | solution.py:61
  147.3 18.4 %copy-start.20 = (bf16[29,64,128]{2,1,0:T(8,128)(2,1)}, bf16[29,64,128]{2,1,0:T(8,128)(2,1)S(1)}, u32[]{:S(2)}) copy-start(bf16[29,64,128]{2,1,0:T(8,128)(2,1)S(1)} %collective-permute-done.28.refs_10_) | copy-start | bytes 1425412
  147.3 14.1 %collective-permute-start.32 = (bf16[29,64,128]{2,1,0:T(8,128)(2,1)S(1)}, bf16[29,64,128]{2,1,0:T(8,128)(2,1)S(1)}, u32[]{:S(2)}, u32[]{:S(2)}) collective-permute-start(bf16[29,64,128]{2,1,0:T(8,128)(2,1)S(1)} %collective-permute-done.24.refs_6_), channel_id=1, source_target_pairs={{0,32},{16,48},{32,64},{48,80},{64,96},{80,112},{96,0},{112,16},{1... | collective-permute-start | bytes 1425416 | tf_op jit(solution)/shard_map/ppermute | solution.py:61
  147.8 6.7 %copy-start.21 = (bf16[29,64,128]{2,1,0:T(8,128)(2,1)}, bf16[29,64,128]{2,1,0:T(8,128)(2,1)S(1)}, u32[]{:S(2)}) copy-start(bf16[29,64,128]{2,1,0:T(8,128)(2,1)S(1)} %collective-permute-done.21.refs_3_) | copy-start | bytes 1425412
  147.8 15.7 %collective-permute-start.25 = (bf16[29,64,128]{2,1,0:T(8,128)(2,1)S(1)}, bf16[29,64,128]{2,1,0:T(8,128)(2,1)S(1)}, u32[]{:S(2)}, u32[]{:S(2)}) collective-permute-start(bf16[29,64,128]{2,1,0:T(8,128)(2,1)S(1)} %collective-permute-done.24.refs_6_), channel_id=1, source_target_pairs={{0,16},{16,0},{32,48},{48,32},{64,80},{80,64},{96,112},{112,96},{1... | collective-permute-start | bytes 1425416 | tf_op jit(solution)/shard_map/ppermute | solution.py:61
  154.5 12.0 %copy-start.13 = (bf16[30,64,128]{2,1,0:T(8,128)(2,1)}, bf16[30,64,128]{2,1,0:T(8,128)(2,1)S(1)}, u32[]{:S(2)}) copy-start(bf16[30,64,128]{2,1,0:T(8,128)(2,1)S(1)} %collective-permute-done.22.refs_4_) | copy-start | bytes 1474564
  154.5 10.5 %collective-permute-start.23 = (bf16[30,64,128]{2,1,0:T(8,128)(2,1)S(1)}, bf16[30,64,128]{2,1,0:T(8,128)(2,1)S(1)}, u32[]{:S(2)}, u32[]{:S(2)}) collective-permute-start(bf16[30,64,128]{2,1,0:T(8,128)(2,1)S(1)} %collective-permute-done.22.refs_4_), channel_id=1, source_target_pairs={{0,16},{16,0},{32,48},{48,32},{64,80},{80,64},{96,112},{112,96},{1... | collective-permute-start | bytes 1474568 | tf_op jit(solution)/shard_map/ppermute | solution.py:61
  155.2 11.2 %copy-start.14 = (bf16[30,64,128]{2,1,0:T(8,128)(2,1)}, bf16[30,64,128]{2,1,0:T(8,128)(2,1)S(1)}, u32[]{:S(2)}) copy-start(bf16[30,64,128]{2,1,0:T(8,128)(2,1)S(1)} %collective-permute-done.20.refs_1_) | copy-start | bytes 1474564
  155.2 9.7 %collective-permute-start.27 = (bf16[30,64,128]{2,1,0:T(8,128)(2,1)S(1)}, bf16[30,64,128]{2,1,0:T(8,128)(2,1)S(1)}, u32[]{:S(2)}, u32[]{:S(2)}) collective-permute-start(bf16[30,64,128]{2,1,0:T(8,128)(2,1)S(1)} %collective-permute-done.26.refs_8_), channel_id=1, source_target_pairs={{0,16},{16,0},{32,48},{48,32},{64,80},{80,64},{96,112},{112,96},{1... | collective-permute-start | bytes 1474568 | tf_op jit(solution)/shard_map/ppermute | solution.py:61
  159.6 6.8 %copy-start.15 = (bf16[30,64,128]{2,1,0:T(8,128)(2,1)}, bf16[30,64,128]{2,1,0:T(8,128)(2,1)S(1)}, u32[]{:S(2)}) copy-start(bf16[30,64,128]{2,1,0:T(8,128)(2,1)S(1)} %collective-permute-done.30.refs_12_) | copy-start | bytes 1474564
  159.6 6.0 %collective-permute-start.31 = (bf16[30,64,128]{2,1,0:T(8,128)(2,1)S(1)}, bf16[30,64,128]{2,1,0:T(8,128)(2,1)S(1)}, u32[]{:S(2)}, u32[]{:S(2)}) collective-permute-start(bf16[30,64,128]{2,1,0:T(8,128)(2,1)S(1)} %collective-permute-done.30.refs_12_), channel_id=1, source_target_pairs={{0,16},{16,0},{32,48},{48,32},{64,80},{80,64},{96,112},{112,96},{1... | collective-permute-start | bytes 1474568 | tf_op jit(solution)/shard_map/ppermute | solution.py:61
  161.4 4.2 %copy-start.22 = (bf16[29,64,128]{2,1,0:T(8,128)(2,1)}, bf16[29,64,128]{2,1,0:T(8,128)(2,1)S(1)}, u32[]{:S(2)}) copy-start(bf16[29,64,128]{2,1,0:T(8,128)(2,1)S(1)} %collective-permute-done.32.refs_14_) | copy-start | bytes 1425412
  161.4 3.6 %collective-permute-start.29 = (bf16[29,64,128]{2,1,0:T(8,128)(2,1)S(1)}, bf16[29,64,128]{2,1,0:T(8,128)(2,1)S(1)}, u32[]{:S(2)}, u32[]{:S(2)}) collective-permute-start(bf16[29,64,128]{2,1,0:T(8,128)(2,1)S(1)} %collective-permute-done.28.refs_10_), channel_id=1, source_target_pairs={{0,16},{16,0},{32,48},{48,32},{64,80},{80,64},{96,112},{112,96},{1... | collective-permute-start | bytes 1425416 | tf_op jit(solution)/shard_map/ppermute | solution.py:61
  163.5 2.2 %copy-start.23 = (bf16[29,64,128]{2,1,0:T(8,128)(2,1)}, bf16[29,64,128]{2,1,0:T(8,128)(2,1)S(1)}, u32[]{:S(2)}) copy-start(bf16[29,64,128]{2,1,0:T(8,128)(2,1)S(1)} %collective-permute-done.25.refs_7_) | copy-start | bytes 1425412
  163.5 2.1 %collective-permute-start.33 = (bf16[29,64,128]{2,1,0:T(8,128)(2,1)S(1)}, bf16[29,64,128]{2,1,0:T(8,128)(2,1)S(1)}, u32[]{:S(2)}, u32[]{:S(2)}) collective-permute-start(bf16[29,64,128]{2,1,0:T(8,128)(2,1)S(1)} %collective-permute-done.32.refs_14_), channel_id=1, source_target_pairs={{0,16},{16,0},{32,48},{48,32},{64,80},{80,64},{96,112},{112,96},{1... | collective-permute-start | bytes 1425416 | tf_op jit(solution)/shard_map/ppermute | solution.py:61
  165.0 0.8 copy-start.24
  165.0 1.5 copy-start.16
  165.0 1.5 copy-start.17
  165.7 0.8 copy-start.25
  166.4 0.8 copy-start.18

commit v2 on v1

--- a/solution.py
+++ b/solution.py
@@ -225,7 +225,12 @@
             table_ref = refs.pop(0)
         slab_refs = [refs.pop(0) for _ in slab]
         piece_refs = [[refs.pop(0) for _ in pieces] for pieces, _ in panels]
-        done_refs = [refs.pop(0) for _ in strips]
+        out_refs = [refs.pop(0) for _ in strips]
+        done_refs, done_sem = [refs.pop() for _ in strips][::-1], refs.pop()
+        out_copies = [
+            pltpu.make_async_copy(ref, out, done_sem.at[i])
+            for i, (ref, out) in enumerate(zip(done_refs, out_refs))
+        ]
         if make:
             table_out, left_ref, left_sem, right_ref, right_sem, table_ref, extra_ref, extra_sem, table_sem = refs
         else:
@@ -275,6 +280,10 @@
                 done_ref[at - start] = (sums * scale).astype(done_ref.dtype)
 
             block_sums(table_ref, left_ref, right_ref, spans, finish)(first, at, size)
+            if at + size == starts[strip] + strips[strip][1]:
+                out_copies[strip].start()
+        for copy in out_copies:
+            copy.wait()
 
     anywhere = pl.BlockSpec(memory_space=pl.ANY)
     in_vmem = pl.BlockSpec(memory_space=pltpu.VMEM)
@@ -298,10 +307,12 @@
             pltpu.SemaphoreType.DMA((groups,)),
             pltpu.SemaphoreType.DMA,
         ]
+    scratch.append(pltpu.SemaphoreType.DMA((len(strips),)))
+    scratch += [pltpu.VMEM((size, block, lanes), jnp.bfloat16) for _, size in strips]
     out = pl.pallas_call(
         body,
         in_specs=in_specs,
-        out_specs=[in_vmem] * len(out_shape),
+        out_specs=[anywhere] * len(strips) + [in_vmem] * int(make),
         out_shape=out_shape,
         scratch_shapes=scratch,
         compiler_params=pltpu.CompilerParams(vmem_limit_bytes=60 * MIB),
@@ -330,13 +341,16 @@
         slab_refs = [refs.pop(0) for _ in slab]
         piece_refs = [[refs.pop(0) for _ in pieces] for pieces, _ in panels]
         square_refs = [refs.pop(0) for _ in square]
-        own_ref, square_ref, flat_ref, left_ref, left_sem, right_ref, right_sem, done_ref = refs
+        own_ref, square_out, flat_ref, left_ref, left_sem, right_ref, right_sem, done_ref = refs[:8]
+        square_ref, square_sem = refs[8:]
+        square_copy = pltpu.make_async_copy(square_ref, square_out, square_sem)
         left_copies = slab_copies(slab_refs, slab, rows_ref, left_ref, left_sem)
         runs = panel_copies(piece_refs, panels, starts, flat_strips, 1, groups_ref, right_ref, right_sem)
         for copy in left_copies + runs[0][0]:
             copy.start()
         left_ref[:, spans] = jnp.zeros((positions, block, lanes), left_ref.dtype)
         join_columns(lambda m: square_refs[members[m][0]][members[m][1]], square_ref, spans, block)
+        square_copy.start()
         for copy in left_copies:
             copy.wait()
         for copies, _, _, _ in runs[1:]:
@@ -353,6 +367,7 @@
                 copy.wait()
             run(first, at, size)
         join_columns(lambda m: done_ref[members[m][2]], flat_ref, spans, block)
+        square_copy.wait()
 
     anywhere = pl.BlockSpec(memory_space=pl.ANY)
     in_vmem = pl.BlockSpec(memory_space=pltpu.VMEM)
@@ -364,7 +379,7 @@
     return pl.pallas_call(
         body,
         in_specs=[in_smem] * 3 + [anywhere] * len(operands) + [in_vmem] * (len(square) + 1),
-        out_specs=[in_vmem] * 2,
+        out_specs=[anywhere, in_vmem],
         out_shape=[flat] * 2,
         scratch_shapes=[
             pltpu.VMEM((positions, spans + 1, block, lanes), jnp.bfloat16),
@@ -372,6 +387,8 @@
             pltpu.VMEM((groups, spans, block, lanes), jnp.bfloat16),
             pltpu.SemaphoreType.DMA((panel_moves(flat_strips),)),
             pltpu.VMEM((spans, block, lanes), jnp.bfloat16),
+            pltpu.VMEM((block, spans * lanes), jnp.bfloat16),
+            pltpu.SemaphoreType.DMA,
         ],
         compiler_params=pltpu.CompilerParams(vmem_limit_bytes=60 * MIB),
         cost_estimate=cost,
@@ -388,7 +405,7 @@
     column = pattern[:, 0]
     scale = 1.0 / math.sqrt(groups * block)
 
-    split = (spans + 1) // 2
+    split = (spans + 1) // 2 + 1
     halves = [(0, split), (split, spans - split)]
     own_links = lax.dynamic_slice_in_dim(column, mine * rows_here, rows_here, 0)
     own, *pieces = pair_columns(values, own_links, spans, halves)

time: 183 us -> 184 us (level)
  waiting for transfers between devices: 77.7 us -> 88 us
  starting transfers between devices: 62.2 us -> 52.5 us
    ppermute x18, starting transfers between devices: 37.7 us -> 29.1 us  [sent_row(): return lax.ppermute(array, 'row', order)]
    ppermute x18, waiting for transfers between devices: 26.4 us -> 34.4 us  [sent_row(): return lax.ppermute(array, 'row', order)]
    ppermute x16, waiting for transfers between devices: 51.3 us -> 53.6 us  [sent_col(): return lax.ppermute(array, 'col', order)]
  transfers between devices with their start and end apart: 34 -> 34, of which waited for: 15 -> 16; matrix products, arithmetic and copies ran while one was open for 3% -> 3% of each run, Pallas kernels for 0% -> 0%
where the time goes in v2:
time: 184 us
  waiting for transfers between devices  88 us (48%)
  starting transfers between devices  52.5 us (29%)
  Pallas kernels  30.9 us (17%)
  local copies, waits for them, and re-layouts  7.84 us (4%)
  other arithmetic  3.4 us (2%)
    ppermute x16, waiting for transfers between devices, sent_col(): return lax.ppermute(array, 'col', order)  53.6 us
    ppermute x18, waiting for transfers between devices, sent_row(): return lax.ppermute(array, 'row', order)  34.4 us
    ppermute x18, starting transfers between devices, sent_row(): return lax.ppermute(array, 'row', order)  29.1 us
    ppermute x16, starting transfers between devices, sent_col(): return lax.ppermute(array, 'col', order)  23.4 us
    pallas_call x1, Pallas kernels, second_product(): pl.pallas_call(body, in_specs=[in_smem] * 3 + [anywhere] * len(operands)...  15.3 us
    pallas_call x1, Pallas kernels, first_product(): pl.pallas_call(body, in_specs=in_specs, out_specs=[anywhere] * len(strips...  15.2 us
  transfers between devices with their start and end apart: 34, of which 16 were waited for; matrix products, arithmetic and copies ran while one was open for 3% of the time, Pallas kernels for 0%

profile of v2, /device:TPU:1, one launch (start us, length us, event | category | flops | bytes accessed | tf_op | source)
XLA Modules:
  0.0 183.8 jit_solution(16482302944115986406)
XLA Ops:
  0.6 0.8 dynamic-slice_bitcast_fusion
  1.4 1.2 copy-done
  2.6 0.4 shard_map.41
  3.0 3.4 %collective-permute-start.8 = (bf16[59,64,128]{2,1,0:T(8,128)(2,1)S(1)}, bf16[59,64,128]{2,1,0:T(8,128)(2,1)S(1)}, u32[]{:S(2)}, u32[]{:S(2)}) collective-permute-start(bf16[59,64,128]{2,1,0:T(8,128)(2,1)S(1)} %get-tuple-element.33.refs_1_.refs_28_), channel_id=1, source_target_pairs={{0,96},{16,112},{32,0},{48,16},{64,32},{80,48},{96,64},{112,80},{1... | collective-permute-start | bytes 2899976 | tf_op jit(solution)/shard_map/ppermute | solution.py:61
  6.4 2.7 %collective-permute-start.5 = (bf16[28,64,128]{2,1,0:T(8,128)(2,1)S(1)}, bf16[28,64,128]{2,1,0:T(8,128)(2,1)S(1)}, u32[]{:S(2)}, u32[]{:S(2)}) collective-permute-start(bf16[28,64,128]{2,1,0:T(8,128)(2,1)S(1)} %get-tuple-element.29), channel_id=1, source_target_pairs={{0,3},{1,0},{2,1},{3,2},{4,7},{5,4},{6,5},{7,6},{8,11},{9,8},{10,9... | collective-permute-start | bytes 1376264 | tf_op jit(solution)/shard_map/ppermute | solution.py:71
  9.1 3.8 %collective-permute-start.1 = (bf16[32,64,128]{2,1,0:T(8,128)(2,1)S(1)}, bf16[32,64,128]{2,1,0:T(8,128)(2,1)S(1)}, u32[]{:S(2)}, u32[]{:S(2)}) collective-permute-start(bf16[32,64,128]{2,1,0:T(8,128)(2,1)S(1)} %get-tuple-element.25), channel_id=1, source_target_pairs={{0,12},{1,13},{2,14},{3,15},{4,0},{5,1},{6,2},{7,3},{8,4},{9,5},{1... | collective-permute-start | bytes 1572872 | tf_op jit(solution)/shard_map/ppermute | solution.py:71
  12.9 5.1 %collective-permute-done.5 = bf16[28,64,128]{2,1,0:T(8,128)(2,1)S(1)} collective-permute-done((bf16[28,64,128]{2,1,0:T(8,128)(2,1)S(1)}, bf16[28,64,128]{2,1,0:T(8,128)(2,1)S(1)}, u32[]{:S(2)}, u32[]{:S(2)}) %collective-permute-start.5) | collective-permute-done | bytes 458784 | tf_op jit(solution)/shard_map/ppermute | solution.py:71
  18.0 3.5 %collective-permute-start.6 = (bf16[14,64,128]{2,1,0:T(8,128)(2,1)S(1)}, bf16[14,64,128]{2,1,0:T(8,128)(2,1)S(1)}, u32[]{:S(2)}, u32[]{:S(2)}) collective-permute-start(bf16[14,64,128]{2,1,0:T(8,128)(2,1)S(1)} %slice.34), channel_id=1, source_target_pairs={{0,3},{1,0},{2,1},{3,2},{4,7},{5,4},{6,5},{7,6},{8,11},{9,8},{10,9... | collective-permute-start | bytes 688136 | tf_op jit(solution)/shard_map/ppermute | solution.py:71
  21.5 0.1 collective-permute-start.7
  21.6 1.3 collective-permute-done.1
  22.9 3.5 %collective-permute-start.2 = (bf16[16,64,128]{2,1,0:T(8,128)(2,1)S(1)}, bf16[16,64,128]{2,1,0:T(8,128)(2,1)S(1)}, u32[]{:S(2)}, u32[]{:S(2)}) collective-permute-start(bf16[16,64,128]{2,1,0:T(8,128)(2,1)S(1)} %slice.32), channel_id=1, source_target_pairs={{0,12},{1,13},{2,14},{3,15},{4,0},{5,1},{6,2},{7,3},{8,4},{9,5},{1... | collective-permute-start | bytes 786440 | tf_op jit(solution)/shard_map/ppermute | solution.py:71
  26.4 0.1 collective-permute-start.3
  26.5 1.5 collective-permute-done.7
  28.0 1.7 collective-permute-done.2
  29.7 3.2 %collective-permute-done.3 = bf16[16,64,128]{2,1,0:T(8,128)(2,1)S(1)} collective-permute-done((bf16[16,64,128]{2,1,0:T(8,128)(2,1)S(1)}, bf16[16,64,128]{2,1,0:T(8,128)(2,1)S(1)}, u32[]{:S(2)}, u32[]{:S(2)}) %collective-permute-start.3) | collective-permute-done | bytes 262176 | tf_op jit(solution)/shard_map/ppermute | solution.py:71
  33.3 0.1 collective-permute-start.11
  33.3 2.7 %collective-permute-start.12 = (bf16[128,64,128]{2,1,0:T(8,128)(2,1)S(1)}, bf16[128,64,128]{2,1,0:T(8,128)(2,1)S(1)}, u32[]{:S(2)}, u32[]{:S(2)}) collective-permute-start(bf16[128,64,128]{2,1,0:T(8,128)(2,1)S(1)} %constant_dynamic-update-slice_fusion.refs_9_.refs_16_), channel_id=1, source_target_pairs={{0,3},{1,0},{2,1},{3,2},{4,7},{5,4},{6,5},{7,6},{8,11},{9,8},{10,9... | collective-permute-start | bytes 6291464 | tf_op jit(solution)/shard_map/ppermute | solution.py:71
  36.0 0.6 collective-permute-start.9
  36.9 0.1 collective-permute-start.13
  37.0 2.7 %collective-permute-start.14 = (bf16[112,64,128]{2,1,0:T(8,128)(2,1)S(1)}, bf16[112,64,128]{2,1,0:T(8,128)(2,1)S(1)}, u32[]{:S(2)}, u32[]{:S(2)}) collective-permute-start(bf16[112,64,128]{2,1,0:T(8,128)(2,1)S(1)} %constant_dynamic-update-slice_fusion.4.refs_14_.refs_21_), channel_id=1, source_target_pairs={{0,12},{1,13},{2,14},{3,15},{4,0},{5,1},{6,2},{7,3},{8,4},{9,5},{1... | collective-permute-start | bytes 5505032 | tf_op jit(solution)/shard_map/ppermute | solution.py:71
  39.6 15.2 %collective-permute-done.9.refs_5_ = bf16[59,64,128]{2,1,0:T(8,128)(2,1)S(1)} collective-permute-done((bf16[59,64,128]{2,1,0:T(8,128)(2,1)S(1)}, bf16[59,64,128]{2,1,0:T(8,128)(2,1)S(1)}, u32[]{:S(2)}, u32[]{:S(2)}) %collective-permute-start.9) | collective-permute-done | bytes 966688 | tf_op jit(solution)/shard_map/ppermute | solution.py:61
  54.9 1.8 collective-permute-start.10
  56.6 18.6 %collective-permute-done.13.refs_15_.refs_22_ = bf16[112,64,128]{2,1,0:T(8,128)(2,1)S(1)} collective-permute-done((bf16[112,64,128]{2,1,0:T(8,128)(2,1)S(1)}, bf16[112,64,128]{2,1,0:T(8,128)(2,1)S(1)}, u32[]{:S(2)}, u32[]{:S(2)}) %collective-permute-start.13) | collective-permute-done | bytes 1835040 | tf_op jit(solution)/shard_map/ppermute | solution.py:71
  75.2 2.8 %collective-permute-done.11.refs_10_.refs_17_ = bf16[128,64,128]{2,1,0:T(8,128)(2,1)S(1)} collective-permute-done((bf16[128,64,128]{2,1,0:T(8,128)(2,1)S(1)}, bf16[128,64,128]{2,1,0:T(8,128)(2,1)S(1)}, u32[]{:S(2)}, u32[]{:S(2)}) %collective-permute-start.11) | collective-permute-done | bytes 2097184 | tf_op jit(solution)/shard_map/ppermute | solution.py:71
  78.1 2.4 %pad_maximum_fusion = bf16[236,64,128]{2,1,0:T(8,128)(2,1)} fusion(bf16[59,64,128]{2,1,0:T(8,128)(2,1)S(1)} %collective-permute-done.10.refs_7_, bf16[59,64,128]{2,1,0:T(8,128)(2,1)S(1)} %collective-permute-done.9.refs_5_, bf16[59,64,128]{2,1,0:T(8,128)(2,1)S(1)} %collective-permute-done.8.refs_3_, bf16[59,64,128]{2,1,0:T(8,128)(2,1)S(1)} %get-tuple-element.33.refs_1_.refs_28_), kind=kLoop, calls=%fused_computation | loop fusion | flops 5799936 | bytes 7733248 | tf_op jit(solution)/shard_map/concatenate | solution.py:120
  80.5 4.5 %collective-permute-start.15 = (bf16[236,64,128]{2,1,0:T(8,128)(2,1)}, bf16[236,64,128]{2,1,0:T(8,128)(2,1)}, u32[]{:S(2)}, u32[]{:S(2)}) collective-permute-start(bf16[236,64,128]{2,1,0:T(8,128)(2,1)} %pad_maximum_fusion), channel_id=1, source_target_pairs={{0,16},{16,0},{32,48},{48,32},{64,80},{80,64},{96,112},{112,96},{1... | collective-permute-start | bytes 11599880 | tf_op jit(solution)/shard_map/ppermute | solution.py:61
  85.1 2.7 %collective-permute-start.16 = (bf16[64,64,128]{2,1,0:T(8,128)(2,1)S(1)}, bf16[64,64,128]{2,1,0:T(8,128)(2,1)}, u32[]{:S(2)}, u32[]{:S(2)}) collective-permute-start(bf16[64,64,128]{2,1,0:T(8,128)(2,1)S(1)} %slice.36), channel_id=1, source_target_pairs={{0,3},{1,0},{2,1},{3,2},{4,7},{5,4},{6,5},{7,6},{8,11},{9,8},{10,9... | collective-permute-start | bytes 3145736 | tf_op jit(solution)/shard_map/ppermute | solution.py:71
  87.9 0.1 collective-permute-start.17
  88.0 0.7 collective-permute-start.18
  88.7 1.0 slice.39
  89.7 0.9 collective-permute-start.19
  90.6 0.5 broadcast.35
  91.1 0.6 reduce.3
  91.8 0.1 eq.68
  91.9 0.1 copy.4
  92.0 0.2 select_reduce_fusion
  92.2 0.1 broadcast_add_fusion
  92.2 0.6 pad.8.refs_0_
  92.8 0.6 stack.86.rows_ref
  93.4 0.7 stack.103.groups_ref
  94.1 15.5 %collective-permute-done.18.refs_17_.refs_24_ = bf16[56,64,128]{2,1,0:T(8,128)(2,1)} collective-permute-done((bf16[56,64,128]{2,1,0:T(8,128)(2,1)S(1)}, bf16[56,64,128]{2,1,0:T(8,128)(2,1)}, u32[]{:S(2)}, u32[]{:S(2)}) %collective-permute-start.18) | collective-permute-done | bytes 917536 | tf_op jit(solution)/shard_map/ppermute | solution.py:71
  109.6 2.6 %collective-permute-done.19.refs_18_.refs_25_ = bf16[56,64,128]{2,1,0:T(8,128)(2,1)} collective-permute-done((bf16[56,64,128]{2,1,0:T(8,128)(2,1)}, bf16[56,64,128]{2,1,0:T(8,128)(2,1)}, u32[]{:S(2)}, u32[]{:S(2)}) %collective-permute-start.19) | collective-permute-done | bytes 917536 | tf_op jit(solution)/shard_map/ppermute | solution.py:71
  112.2 1.3 collective-permute-done.17.refs_13_.refs_20_
  113.5 15.2 %shard_map.42 = (bf16[31,64,128]{2,1,0:T(8,128)(2,1)}, bf16[28,64,128]{2,1,0:T(8,128)(2,1)}, s32[16,128]{1,0:T(8,128)}) custom-call(s32[8]{0:T(128)} %stack.86.rows_ref, s32[16]{0:T(128)} %stack.103.groups_ref, s32[16,128]{1,0:T(8,128)} %pad.8.refs_0_, bf16[59,64,128]{2,1,0:T(8,128)(2,1)} %copy-done.1, ...), custom_call_target="tpu_custom_call" | custom-call | flops 23756537856 | bytes 35061760 | tf_op jit(solution)/shard_map/pallas_call | solution.py:312
  128.7 0.6 collective-permute-start.26
  129.3 0.9 collective-permute-start.24
  130.2 1.8 collective-permute-start.28
  132.0 2.2 %collective-permute-start.21 = (bf16[28,64,128]{2,1,0:T(8,128)(2,1)}, bf16[28,64,128]{2,1,0:T(8,128)(2,1)S(1)}, u32[]{:S(2)}, u32[]{:S(2)}) collective-permute-start(bf16[28,64,128]{2,1,0:T(8,128)(2,1)} %get-tuple-element.39.refs_2_.refs_27_), channel_id=1, source_target_pairs={{0,16},{16,0},{32,48},{48,32},{64,80},{80,64},{96,112},{112,96},{1... | collective-permute-start | bytes 1376264 | tf_op jit(solution)/shard_map/ppermute | solution.py:61
  134.2 6.9 %collective-permute-done.24.refs_6_ = bf16[28,64,128]{2,1,0:T(8,128)(2,1)S(1)} collective-permute-done((bf16[28,64,128]{2,1,0:T(8,128)(2,1)}, bf16[28,64,128]{2,1,0:T(8,128)(2,1)S(1)}, u32[]{:S(2)}, u32[]{:S(2)}) %collective-permute-start.24) | collective-permute-done | bytes 458784 | tf_op jit(solution)/shard_map/ppermute | solution.py:61
  141.1 4.7 %collective-permute-start.20 = (bf16[31,64,128]{2,1,0:T(8,128)(2,1)}, bf16[31,64,128]{2,1,0:T(8,128)(2,1)S(1)}, u32[]{:S(2)}, u32[]{:S(2)}) collective-permute-start(bf16[31,64,128]{2,1,0:T(8,128)(2,1)} %get-tuple-element.38.refs_0_.refs_26_), channel_id=1, source_target_pairs={{0,16},{16,0},{32,48},{48,32},{64,80},{80,64},{96,112},{112,96},{1... | collective-permute-start | bytes 1523720 | tf_op jit(solution)/shard_map/ppermute | solution.py:61
  145.8 4.7 %collective-permute-done.28.refs_10_ = bf16[28,64,128]{2,1,0:T(8,128)(2,1)S(1)} collective-permute-done((bf16[28,64,128]{2,1,0:T(8,128)(2,1)}, bf16[28,64,128]{2,1,0:T(8,128)(2,1)S(1)}, u32[]{:S(2)}, u32[]{:S(2)}) %collective-permute-start.28) | collective-permute-done | bytes 458784 | tf_op jit(solution)/shard_map/ppermute | solution.py:61
  150.5 4.2 %collective-permute-start.25 = (bf16[28,64,128]{2,1,0:T(8,128)(2,1)S(1)}, bf16[28,64,128]{2,1,0:T(8,128)(2,1)S(1)}, u32[]{:S(2)}, u32[]{:S(2)}) collective-permute-start(bf16[28,64,128]{2,1,0:T(8,128)(2,1)S(1)} %collective-permute-done.24.refs_6_), channel_id=1, source_target_pairs={{0,16},{16,0},{32,48},{48,32},{64,80},{80,64},{96,112},{112,96},{1... | collective-permute-start | bytes 1376264 | tf_op jit(solution)/shard_map/ppermute | solution.py:61
  154.7 0.7 collective-permute-start.23
  155.5 0.1 collective-permute-start.27
  155.6 5.8 %collective-permute-done.30.refs_12_ = bf16[31,64,128]{2,1,0:T(8,128)(2,1)S(1)} collective-permute-done((bf16[31,64,128]{2,1,0:T(8,128)(2,1)S(1)}, bf16[31,64,128]{2,1,0:T(8,128)(2,1)S(1)}, u32[]{:S(2)}, u32[]{:S(2)}) %collective-permute-start.30) | collective-permute-done | bytes 507936 | tf_op jit(solution)/shard_map/ppermute | solution.py:61
  161.4 2.3 %collective-permute-start.31 = (bf16[31,64,128]{2,1,0:T(8,128)(2,1)S(1)}, bf16[31,64,128]{2,1,0:T(8,128)(2,1)S(1)}, u32[]{:S(2)}, u32[]{:S(2)}) collective-permute-start(bf16[31,64,128]{2,1,0:T(8,128)(2,1)S(1)} %collective-permute-done.30.refs_12_), channel_id=1, source_target_pairs={{0,16},{16,0},{32,48},{48,32},{64,80},{80,64},{96,112},{112,96},{1... | collective-permute-start | bytes 1523720 | tf_op jit(solution)/shard_map/ppermute | solution.py:61
  163.7 1.0 collective-permute-start.29
  164.6 0.3 collective-permute-start.33
  165.0 1.1 collective-permute-done.29.refs_11_
  166.1 0.6 collective-permute-done.33.refs_15_
  166.8 0.1 copy-done.24
  166.9 0.6 copy-done.25
  167.6 0.7 copy-done.18
  168.3 15.3 %shard_map.43 = (bf16[64,7552]{1,0:T(8,128)(2,1)}, bf16[64,7552]{1,0:T(8,128)(2,1)}) custom-call(s32[16,128]{1,0:T(8,128)} %get-tuple-element.37.table_ref, s32[8]{0:T(128)} %stack.86.rows_ref, s32[16]{0:T(128)} %stack.103.groups_ref, bf16[31,64,128]{2,1,0:T(8,128)(2,1)} %get-tuple-element.38.refs_0_.refs_26_, bf16[31,64,128]{2,1,0:T(8,128)(2,1)} %copy-done.14, ...), custom_call_target="tpu_custom_call" | custom-call | flops 23756537856 | bytes 23461888 | tf_op jit(solution)/shard_map/pallas_call | solution.py:379
  (90 shorter events, 1.0 us)
Async XLA Ops:
  1.4 1.2 copy-start
  3.0 75.1 %copy-start.1 = (bf16[59,64,128]{2,1,0:T(8,128)(2,1)}, bf16[59,64,128]{2,1,0:T(8,128)(2,1)S(1)}, u32[]{:S(2)}) copy-start(bf16[59,64,128]{2,1,0:T(8,128)(2,1)S(1)} %get-tuple-element.33.refs_1_.refs_28_) | copy-start | bytes 2899972
  3.0 29.9 %collective-permute-start.8 = (bf16[59,64,128]{2,1,0:T(8,128)(2,1)S(1)}, bf16[59,64,128]{2,1,0:T(8,128)(2,1)S(1)}, u32[]{:S(2)}, u32[]{:S(2)}) collective-permute-start(bf16[59,64,128]{2,1,0:T(8,128)(2,1)S(1)} %get-tuple-element.33.refs_1_.refs_28_), channel_id=1, source_target_pairs={{0,96},{16,112},{32,0},{48,16},{64,32},{80,48},{96,64},{112,80},{1... | collective-permute-start | bytes 2899976 | tf_op jit(solution)/shard_map/ppermute | solution.py:61
  6.4 11.6 %collective-permute-start.5 = (bf16[28,64,128]{2,1,0:T(8,128)(2,1)S(1)}, bf16[28,64,128]{2,1,0:T(8,128)(2,1)S(1)}, u32[]{:S(2)}, u32[]{:S(2)}) collective-permute-start(bf16[28,64,128]{2,1,0:T(8,128)(2,1)S(1)} %get-tuple-element.29), channel_id=1, source_target_pairs={{0,3},{1,0},{2,1},{3,2},{4,7},{5,4},{6,5},{7,6},{8,11},{9,8},{10,9... | collective-permute-start | bytes 1376264 | tf_op jit(solution)/shard_map/ppermute | solution.py:71
  9.1 12.4 %collective-permute-start.4 = (bf16[28,64,128]{2,1,0:T(8,128)(2,1)S(1)}, bf16[28,64,128]{2,1,0:T(8,128)(2,1)S(1)}, u32[]{:S(2)}, u32[]{:S(2)}) collective-permute-start(bf16[28,64,128]{2,1,0:T(8,128)(2,1)S(1)} %get-tuple-element.29), channel_id=1, source_target_pairs={{0,1},{1,2},{2,3},{3,0},{4,5},{5,6},{6,7},{7,4},{8,9},{9,10},{10,1... | collective-permute-start | bytes 1376264 | tf_op jit(solution)/shard_map/ppermute | solution.py:71
  9.1 13.7 %collective-permute-start.1 = (bf16[32,64,128]{2,1,0:T(8,128)(2,1)S(1)}, bf16[32,64,128]{2,1,0:T(8,128)(2,1)S(1)}, u32[]{:S(2)}, u32[]{:S(2)}) collective-permute-start(bf16[32,64,128]{2,1,0:T(8,128)(2,1)S(1)} %get-tuple-element.25), channel_id=1, source_target_pairs={{0,12},{1,13},{2,14},{3,15},{4,0},{5,1},{6,2},{7,3},{8,4},{9,5},{1... | collective-permute-start | bytes 1572872 | tf_op jit(solution)/shard_map/ppermute | solution.py:71
  12.9 13.5 %collective-permute-start = (bf16[32,64,128]{2,1,0:T(8,128)(2,1)S(1)}, bf16[32,64,128]{2,1,0:T(8,128)(2,1)S(1)}, u32[]{:S(2)}, u32[]{:S(2)}) collective-permute-start(bf16[32,64,128]{2,1,0:T(8,128)(2,1)S(1)} %get-tuple-element.25), channel_id=1, source_target_pairs={{0,4},{1,5},{2,6},{3,7},{4,8},{5,9},{6,10},{7,11},{8,12},{9,13},{1... | collective-permute-start | bytes 1572872 | tf_op jit(solution)/shard_map/ppermute | solution.py:71
  18.0 8.5 %collective-permute-start.6 = (bf16[14,64,128]{2,1,0:T(8,128)(2,1)S(1)}, bf16[14,64,128]{2,1,0:T(8,128)(2,1)S(1)}, u32[]{:S(2)}, u32[]{:S(2)}) collective-permute-start(bf16[14,64,128]{2,1,0:T(8,128)(2,1)S(1)} %slice.34), channel_id=1, source_target_pairs={{0,3},{1,0},{2,1},{3,2},{4,7},{5,4},{6,5},{7,6},{8,11},{9,8},{10,9... | collective-permute-start | bytes 688136 | tf_op jit(solution)/shard_map/ppermute | solution.py:71
  21.5 6.4 %collective-permute-start.7 = (bf16[14,64,128]{2,1,0:T(8,128)(2,1)S(1)}, bf16[14,64,128]{2,1,0:T(8,128)(2,1)S(1)}, u32[]{:S(2)}, u32[]{:S(2)}) collective-permute-start(bf16[14,64,128]{2,1,0:T(8,128)(2,1)S(1)} %slice.35), channel_id=1, source_target_pairs={{0,1},{1,2},{2,3},{3,0},{4,5},{5,6},{6,7},{7,4},{8,9},{9,10},{10,1... | collective-permute-start | bytes 688136 | tf_op jit(solution)/shard_map/ppermute | solution.py:71
  22.9 6.8 %collective-permute-start.2 = (bf16[16,64,128]{2,1,0:T(8,128)(2,1)S(1)}, bf16[16,64,128]{2,1,0:T(8,128)(2,1)S(1)}, u32[]{:S(2)}, u32[]{:S(2)}) collective-permute-start(bf16[16,64,128]{2,1,0:T(8,128)(2,1)S(1)} %slice.32), channel_id=1, source_target_pairs={{0,12},{1,13},{2,14},{3,15},{4,0},{5,1},{6,2},{7,3},{8,4},{9,5},{1... | collective-permute-start | bytes 786440 | tf_op jit(solution)/shard_map/ppermute | solution.py:71
  26.4 6.5 %collective-permute-start.3 = (bf16[16,64,128]{2,1,0:T(8,128)(2,1)S(1)}, bf16[16,64,128]{2,1,0:T(8,128)(2,1)S(1)}, u32[]{:S(2)}, u32[]{:S(2)}) collective-permute-start(bf16[16,64,128]{2,1,0:T(8,128)(2,1)S(1)} %slice.33), channel_id=1, source_target_pairs={{0,4},{1,5},{2,6},{3,7},{4,8},{5,9},{6,10},{7,11},{8,12},{9,13},{1... | collective-permute-start | bytes 786440 | tf_op jit(solution)/shard_map/ppermute | solution.py:71
  33.0 45.1 %copy-start.2 = (bf16[59,64,128]{2,1,0:T(8,128)(2,1)}, bf16[59,64,128]{2,1,0:T(8,128)(2,1)S(1)}, u32[]{:S(2)}) copy-start(bf16[59,64,128]{2,1,0:T(8,128)(2,1)S(1)} %collective-permute-done.8.refs_3_) | copy-start | bytes 2899972
  33.2 44.8 %copy-start.9 = (bf16[128,64,128]{2,1,0:T(8,128)(2,1)}, bf16[128,64,128]{2,1,0:T(8,128)(2,1)S(1)}, u32[]{:S(2)}) copy-start(bf16[128,64,128]{2,1,0:T(8,128)(2,1)S(1)} %constant_dynamic-update-slice_fusion.refs_9_.refs_16_) | copy-start | bytes 6291460
  33.3 44.8 %collective-permute-start.11 = (bf16[128,64,128]{2,1,0:T(8,128)(2,1)S(1)}, bf16[128,64,128]{2,1,0:T(8,128)(2,1)S(1)}, u32[]{:S(2)}, u32[]{:S(2)}) collective-permute-start(bf16[128,64,128]{2,1,0:T(8,128)(2,1)S(1)} %constant_dynamic-update-slice_fusion.refs_9_.refs_16_), channel_id=1, source_target_pairs={{0,1},{1,2},{2,3},{3,0},{4,5},{5,6},{6,7},{7,4},{8,9},{9,10},{10,1... | collective-permute-start | bytes 6291464 | tf_op jit(solution)/shard_map/ppermute | solution.py:71
  33.3 44.7 %collective-permute-start.12 = (bf16[128,64,128]{2,1,0:T(8,128)(2,1)S(1)}, bf16[128,64,128]{2,1,0:T(8,128)(2,1)S(1)}, u32[]{:S(2)}, u32[]{:S(2)}) collective-permute-start(bf16[128,64,128]{2,1,0:T(8,128)(2,1)S(1)} %constant_dynamic-update-slice_fusion.refs_9_.refs_16_), channel_id=1, source_target_pairs={{0,3},{1,0},{2,1},{3,2},{4,7},{5,4},{6,5},{7,6},{8,11},{9,8},{10,9... | collective-permute-start | bytes 6291464 | tf_op jit(solution)/shard_map/ppermute | solution.py:71
  36.0 18.8 %collective-permute-start.9 = (bf16[59,64,128]{2,1,0:T(8,128)(2,1)S(1)}, bf16[59,64,128]{2,1,0:T(8,128)(2,1)S(1)}, u32[]{:S(2)}, u32[]{:S(2)}) collective-permute-start(bf16[59,64,128]{2,1,0:T(8,128)(2,1)S(1)} %collective-permute-done.8.refs_3_), channel_id=1, source_target_pairs={{0,96},{16,112},{32,0},{48,16},{64,32},{80,48},{96,64},{112,80},{1... | collective-permute-start | bytes 2899976 | tf_op jit(solution)/shard_map/ppermute | solution.py:61
  36.9 41.2 %copy-start.10 = (bf16[112,64,128]{2,1,0:T(8,128)(2,1)}, bf16[112,64,128]{2,1,0:T(8,128)(2,1)S(1)}, u32[]{:S(2)}) copy-start(bf16[112,64,128]{2,1,0:T(8,128)(2,1)S(1)} %constant_dynamic-update-slice_fusion.4.refs_14_.refs_21_) | copy-start | bytes 5505028
  36.9 38.4 %collective-permute-start.13 = (bf16[112,64,128]{2,1,0:T(8,128)(2,1)S(1)}, bf16[112,64,128]{2,1,0:T(8,128)(2,1)S(1)}, u32[]{:S(2)}, u32[]{:S(2)}) collective-permute-start(bf16[112,64,128]{2,1,0:T(8,128)(2,1)S(1)} %constant_dynamic-update-slice_fusion.4.refs_14_.refs_21_), channel_id=1, source_target_pairs={{0,4},{1,5},{2,6},{3,7},{4,8},{5,9},{6,10},{7,11},{8,12},{9,13},{1... | collective-permute-start | bytes 5505032 | tf_op jit(solution)/shard_map/ppermute | solution.py:71
  37.0 38.3 %collective-permute-start.14 = (bf16[112,64,128]{2,1,0:T(8,128)(2,1)S(1)}, bf16[112,64,128]{2,1,0:T(8,128)(2,1)S(1)}, u32[]{:S(2)}, u32[]{:S(2)}) collective-permute-start(bf16[112,64,128]{2,1,0:T(8,128)(2,1)S(1)} %constant_dynamic-update-slice_fusion.4.refs_14_.refs_21_), channel_id=1, source_target_pairs={{0,12},{1,13},{2,14},{3,15},{4,0},{5,1},{6,2},{7,3},{8,4},{9,5},{1... | collective-permute-start | bytes 5505032 | tf_op jit(solution)/shard_map/ppermute | solution.py:71
  54.9 25.7 %copy-start.3 = (bf16[59,64,128]{2,1,0:T(8,128)(2,1)}, bf16[59,64,128]{2,1,0:T(8,128)(2,1)S(1)}, u32[]{:S(2)}) copy-start(bf16[59,64,128]{2,1,0:T(8,128)(2,1)S(1)} %collective-permute-done.9.refs_5_) | copy-start | bytes 2899972
  54.9 20.4 %collective-permute-start.10 = (bf16[59,64,128]{2,1,0:T(8,128)(2,1)S(1)}, bf16[59,64,128]{2,1,0:T(8,128)(2,1)S(1)}, u32[]{:S(2)}, u32[]{:S(2)}) collective-permute-start(bf16[59,64,128]{2,1,0:T(8,128)(2,1)S(1)} %collective-permute-done.9.refs_5_), channel_id=1, source_target_pairs={{0,96},{16,112},{32,0},{48,16},{64,32},{80,48},{96,64},{112,80},{1... | collective-permute-start | bytes 2899976 | tf_op jit(solution)/shard_map/ppermute | solution.py:61
  75.2 13.5 %copy-start.7 = (bf16[112,64,128]{2,1,0:T(8,128)(2,1)}, bf16[112,64,128]{2,1,0:T(8,128)(2,1)S(1)}, u32[]{:S(2)}) copy-start(bf16[112,64,128]{2,1,0:T(8,128)(2,1)S(1)} %collective-permute-done.13.refs_15_.refs_22_) | copy-start | bytes 5505028
  75.2 12.8 %copy-start.8 = (bf16[112,64,128]{2,1,0:T(8,128)(2,1)}, bf16[112,64,128]{2,1,0:T(8,128)(2,1)S(1)}, u32[]{:S(2)}) copy-start(bf16[112,64,128]{2,1,0:T(8,128)(2,1)S(1)} %collective-permute-done.14.refs_16_.refs_23_) | copy-start | bytes 5505028
  75.2 5.3 %copy-start.4 = (bf16[59,64,128]{2,1,0:T(8,128)(2,1)}, bf16[59,64,128]{2,1,0:T(8,128)(2,1)S(1)}, u32[]{:S(2)}) copy-start(bf16[59,64,128]{2,1,0:T(8,128)(2,1)S(1)} %collective-permute-done.10.refs_7_) | copy-start | bytes 2899972
  78.1 9.7 %copy-start.5 = (bf16[128,64,128]{2,1,0:T(8,128)(2,1)}, bf16[128,64,128]{2,1,0:T(8,128)(2,1)S(1)}, u32[]{:S(2)}) copy-start(bf16[128,64,128]{2,1,0:T(8,128)(2,1)S(1)} %collective-permute-done.11.refs_10_.refs_17_) | copy-start | bytes 6291460
  78.1 6.9 %copy-start.6 = (bf16[128,64,128]{2,1,0:T(8,128)(2,1)}, bf16[128,64,128]{2,1,0:T(8,128)(2,1)S(1)}, u32[]{:S(2)}) copy-start(bf16[128,64,128]{2,1,0:T(8,128)(2,1)S(1)} %collective-permute-done.12.refs_11_.refs_18_) | copy-start | bytes 6291460
  80.5 33.0 %collective-permute-start.15 = (bf16[236,64,128]{2,1,0:T(8,128)(2,1)}, bf16[236,64,128]{2,1,0:T(8,128)(2,1)}, u32[]{:S(2)}, u32[]{:S(2)}) collective-permute-start(bf16[236,64,128]{2,1,0:T(8,128)(2,1)} %pad_maximum_fusion), channel_id=1, source_target_pairs={{0,16},{16,0},{32,48},{48,32},{64,80},{80,64},{96,112},{112,96},{1... | collective-permute-start | bytes 11599880 | tf_op jit(solution)/shard_map/ppermute | solution.py:61
  85.1 27.1 %collective-permute-start.16 = (bf16[64,64,128]{2,1,0:T(8,128)(2,1)S(1)}, bf16[64,64,128]{2,1,0:T(8,128)(2,1)}, u32[]{:S(2)}, u32[]{:S(2)}) collective-permute-start(bf16[64,64,128]{2,1,0:T(8,128)(2,1)S(1)} %slice.36), channel_id=1, source_target_pairs={{0,3},{1,0},{2,1},{3,2},{4,7},{5,4},{6,5},{7,6},{8,11},{9,8},{10,9... | collective-permute-start | bytes 3145736 | tf_op jit(solution)/shard_map/ppermute | solution.py:71
  87.9 3.3 %copy-start.11 = (s32[944,1]{0,1:T(1,128)S(1)}, s32[944,1]{0,1:T(1,128)}, u32[]{:S(2)}) copy-start(s32[944,1]{0,1:T(1,128)} %param.3) | copy-start | bytes 11332
  87.9 25.6 %collective-permute-start.17 = (bf16[64,64,128]{2,1,0:T(8,128)(2,1)S(1)}, bf16[64,64,128]{2,1,0:T(8,128)(2,1)}, u32[]{:S(2)}, u32[]{:S(2)}) collective-permute-start(bf16[64,64,128]{2,1,0:T(8,128)(2,1)S(1)} %slice.37), channel_id=1, source_target_pairs={{0,1},{1,2},{2,3},{3,0},{4,5},{5,6},{6,7},{7,4},{8,9},{9,10},{10,1... | collective-permute-start | bytes 3145736 | tf_op jit(solution)/shard_map/ppermute | solution.py:71
  88.0 21.6 %collective-permute-start.18 = (bf16[56,64,128]{2,1,0:T(8,128)(2,1)S(1)}, bf16[56,64,128]{2,1,0:T(8,128)(2,1)}, u32[]{:S(2)}, u32[]{:S(2)}) collective-permute-start(bf16[56,64,128]{2,1,0:T(8,128)(2,1)S(1)} %slice.38), channel_id=1, source_target_pairs={{0,12},{1,13},{2,14},{3,15},{4,0},{5,1},{6,2},{7,3},{8,4},{9,5},{1... | collective-permute-start | bytes 2752520 | tf_op jit(solution)/shard_map/ppermute | solution.py:71
  89.7 22.5 %collective-permute-start.19 = (bf16[56,64,128]{2,1,0:T(8,128)(2,1)}, bf16[56,64,128]{2,1,0:T(8,128)(2,1)}, u32[]{:S(2)}, u32[]{:S(2)}) collective-permute-start(bf16[56,64,128]{2,1,0:T(8,128)(2,1)} %slice.39), channel_id=1, source_target_pairs={{0,4},{1,5},{2,6},{3,7},{4,8},{5,9},{6,10},{7,11},{8,12},{9,13},{1... | collective-permute-start | bytes 2752520 | tf_op jit(solution)/shard_map/ppermute | solution.py:71
  128.7 17.1 %collective-permute-start.26 = (bf16[31,64,128]{2,1,0:T(8,128)(2,1)}, bf16[31,64,128]{2,1,0:T(8,128)(2,1)S(1)}, u32[]{:S(2)}, u32[]{:S(2)}) collective-permute-start(bf16[31,64,128]{2,1,0:T(8,128)(2,1)} %get-tuple-element.38.refs_0_.refs_26_), channel_id=1, source_target_pairs={{0,96},{16,112},{32,0},{48,16},{64,32},{80,48},{96,64},{112,80},{1... | collective-permute-start | bytes 1523720 | tf_op jit(solution)/shard_map/ppermute | solution.py:61
  129.3 11.8 %collective-permute-start.24 = (bf16[28,64,128]{2,1,0:T(8,128)(2,1)}, bf16[28,64,128]{2,1,0:T(8,128)(2,1)S(1)}, u32[]{:S(2)}, u32[]{:S(2)}) collective-permute-start(bf16[28,64,128]{2,1,0:T(8,128)(2,1)} %get-tuple-element.39.refs_2_.refs_27_), channel_id=1, source_target_pairs={{0,32},{16,48},{32,64},{48,80},{64,96},{80,112},{96,0},{112,16},{1... | collective-permute-start | bytes 1376264 | tf_op jit(solution)/shard_map/ppermute | solution.py:61
  130.2 20.3 %collective-permute-start.28 = (bf16[28,64,128]{2,1,0:T(8,128)(2,1)}, bf16[28,64,128]{2,1,0:T(8,128)(2,1)S(1)}, u32[]{:S(2)}, u32[]{:S(2)}) collective-permute-start(bf16[28,64,128]{2,1,0:T(8,128)(2,1)} %get-tuple-element.39.refs_2_.refs_27_), channel_id=1, source_target_pairs={{0,96},{16,112},{32,0},{48,16},{64,32},{80,48},{96,64},{112,80},{1... | collective-permute-start | bytes 1376264 | tf_op jit(solution)/shard_map/ppermute | solution.py:61
  132.0 18.5 %collective-permute-start.21 = (bf16[28,64,128]{2,1,0:T(8,128)(2,1)}, bf16[28,64,128]{2,1,0:T(8,128)(2,1)S(1)}, u32[]{:S(2)}, u32[]{:S(2)}) collective-permute-start(bf16[28,64,128]{2,1,0:T(8,128)(2,1)} %get-tuple-element.39.refs_2_.refs_27_), channel_id=1, source_target_pairs={{0,16},{16,0},{32,48},{48,32},{64,80},{80,64},{96,112},{112,96},{1... | collective-permute-start | bytes 1376264 | tf_op jit(solution)/shard_map/ppermute | solution.py:61
  134.2 20.6 %collective-permute-start.22 = (bf16[31,64,128]{2,1,0:T(8,128)(2,1)}, bf16[31,64,128]{2,1,0:T(8,128)(2,1)S(1)}, u32[]{:S(2)}, u32[]{:S(2)}) collective-permute-start(bf16[31,64,128]{2,1,0:T(8,128)(2,1)} %get-tuple-element.38.refs_0_.refs_26_), channel_id=1, source_target_pairs={{0,32},{16,48},{32,64},{48,80},{64,96},{80,112},{96,0},{112,16},{1... | collective-permute-start | bytes 1523720 | tf_op jit(solution)/shard_map/ppermute | solution.py:61
  141.1 26.4 %copy-start.19 = (bf16[28,64,128]{2,1,0:T(8,128)(2,1)}, bf16[28,64,128]{2,1,0:T(8,128)(2,1)S(1)}, u32[]{:S(2)}) copy-start(bf16[28,64,128]{2,1,0:T(8,128)(2,1)S(1)} %collective-permute-done.24.refs_6_) | copy-start | bytes 1376260
  141.1 14.4 %collective-permute-start.20 = (bf16[31,64,128]{2,1,0:T(8,128)(2,1)}, bf16[31,64,128]{2,1,0:T(8,128)(2,1)S(1)}, u32[]{:S(2)}, u32[]{:S(2)}) collective-permute-start(bf16[31,64,128]{2,1,0:T(8,128)(2,1)} %get-tuple-element.38.refs_0_.refs_26_), channel_id=1, source_target_pairs={{0,16},{16,0},{32,48},{48,32},{64,80},{80,64},{96,112},{112,96},{1... | collective-permute-start | bytes 1523720 | tf_op jit(solution)/shard_map/ppermute | solution.py:61
  145.8 21.7 %copy-start.12 = (bf16[31,64,128]{2,1,0:T(8,128)(2,1)}, bf16[31,64,128]{2,1,0:T(8,128)(2,1)S(1)}, u32[]{:S(2)}) copy-start(bf16[31,64,128]{2,1,0:T(8,128)(2,1)S(1)} %collective-permute-done.26.refs_8_) | copy-start | bytes 1523716
  145.8 15.6 %collective-permute-start.30 = (bf16[31,64,128]{2,1,0:T(8,128)(2,1)S(1)}, bf16[31,64,128]{2,1,0:T(8,128)(2,1)S(1)}, u32[]{:S(2)}, u32[]{:S(2)}) collective-permute-start(bf16[31,64,128]{2,1,0:T(8,128)(2,1)S(1)} %collective-permute-done.26.refs_8_), channel_id=1, source_target_pairs={{0,96},{16,112},{32,0},{48,16},{64,32},{80,48},{96,64},{112,80},{1... | collective-permute-start | bytes 1523720 | tf_op jit(solution)/shard_map/ppermute | solution.py:61
  150.5 16.3 %copy-start.20 = (bf16[28,64,128]{2,1,0:T(8,128)(2,1)}, bf16[28,64,128]{2,1,0:T(8,128)(2,1)S(1)}, u32[]{:S(2)}) copy-start(bf16[28,64,128]{2,1,0:T(8,128)(2,1)S(1)} %collective-permute-done.28.refs_10_) | copy-start | bytes 1376260
  150.5 13.2 %collective-permute-start.32 = (bf16[28,64,128]{2,1,0:T(8,128)(2,1)S(1)}, bf16[28,64,128]{2,1,0:T(8,128)(2,1)S(1)}, u32[]{:S(2)}, u32[]{:S(2)}) collective-permute-start(bf16[28,64,128]{2,1,0:T(8,128)(2,1)S(1)} %collective-permute-done.24.refs_6_), channel_id=1, source_target_pairs={{0,32},{16,48},{32,64},{48,80},{64,96},{80,112},{96,0},{112,16},{1... | collective-permute-start | bytes 1376264 | tf_op jit(solution)/shard_map/ppermute | solution.py:61
  150.5 4.2 %copy-start.21 = (bf16[28,64,128]{2,1,0:T(8,128)(2,1)}, bf16[28,64,128]{2,1,0:T(8,128)(2,1)S(1)}, u32[]{:S(2)}) copy-start(bf16[28,64,128]{2,1,0:T(8,128)(2,1)S(1)} %collective-permute-done.21.refs_3_) | copy-start | bytes 1376260
  150.5 14.1 %collective-permute-start.25 = (bf16[28,64,128]{2,1,0:T(8,128)(2,1)S(1)}, bf16[28,64,128]{2,1,0:T(8,128)(2,1)S(1)}, u32[]{:S(2)}, u32[]{:S(2)}) collective-permute-start(bf16[28,64,128]{2,1,0:T(8,128)(2,1)S(1)} %collective-permute-done.24.refs_6_), channel_id=1, source_target_pairs={{0,16},{16,0},{32,48},{48,32},{64,80},{80,64},{96,112},{112,96},{1... | collective-permute-start | bytes 1376264 | tf_op jit(solution)/shard_map/ppermute | solution.py:61
  154.7 12.8 %copy-start.13 = (bf16[31,64,128]{2,1,0:T(8,128)(2,1)}, bf16[31,64,128]{2,1,0:T(8,128)(2,1)S(1)}, u32[]{:S(2)}) copy-start(bf16[31,64,128]{2,1,0:T(8,128)(2,1)S(1)} %collective-permute-done.22.refs_4_) | copy-start | bytes 1523716
  154.7 11.3 %collective-permute-start.23 = (bf16[31,64,128]{2,1,0:T(8,128)(2,1)S(1)}, bf16[31,64,128]{2,1,0:T(8,128)(2,1)S(1)}, u32[]{:S(2)}, u32[]{:S(2)}) collective-permute-start(bf16[31,64,128]{2,1,0:T(8,128)(2,1)S(1)} %collective-permute-done.22.refs_4_), channel_id=1, source_target_pairs={{0,16},{16,0},{32,48},{48,32},{64,80},{80,64},{96,112},{112,96},{1... | collective-permute-start | bytes 1523720 | tf_op jit(solution)/shard_map/ppermute | solution.py:61
  155.5 12.1 %copy-start.14 = (bf16[31,64,128]{2,1,0:T(8,128)(2,1)}, bf16[31,64,128]{2,1,0:T(8,128)(2,1)S(1)}, u32[]{:S(2)}) copy-start(bf16[31,64,128]{2,1,0:T(8,128)(2,1)S(1)} %collective-permute-done.20.refs_1_) | copy-start | bytes 1523716
  155.5 10.6 %collective-permute-start.27 = (bf16[31,64,128]{2,1,0:T(8,128)(2,1)S(1)}, bf16[31,64,128]{2,1,0:T(8,128)(2,1)S(1)}, u32[]{:S(2)}, u32[]{:S(2)}) collective-permute-start(bf16[31,64,128]{2,1,0:T(8,128)(2,1)S(1)} %collective-permute-done.26.refs_8_), channel_id=1, source_target_pairs={{0,16},{16,0},{32,48},{48,32},{64,80},{80,64},{96,112},{112,96},{1... | collective-permute-start | bytes 1523720 | tf_op jit(solution)/shard_map/ppermute | solution.py:61
  161.4 6.2 %copy-start.15 = (bf16[31,64,128]{2,1,0:T(8,128)(2,1)}, bf16[31,64,128]{2,1,0:T(8,128)(2,1)S(1)}, u32[]{:S(2)}) copy-start(bf16[31,64,128]{2,1,0:T(8,128)(2,1)S(1)} %collective-permute-done.30.refs_12_) | copy-start | bytes 1523716
  161.4 5.4 %collective-permute-start.31 = (bf16[31,64,128]{2,1,0:T(8,128)(2,1)S(1)}, bf16[31,64,128]{2,1,0:T(8,128)(2,1)S(1)}, u32[]{:S(2)}, u32[]{:S(2)}) collective-permute-start(bf16[31,64,128]{2,1,0:T(8,128)(2,1)S(1)} %collective-permute-done.30.refs_12_), channel_id=1, source_target_pairs={{0,16},{16,0},{32,48},{48,32},{64,80},{80,64},{96,112},{112,96},{1... | collective-permute-start | bytes 1523720 | tf_op jit(solution)/shard_map/ppermute | solution.py:61
  163.7 3.1 %copy-start.22 = (bf16[28,64,128]{2,1,0:T(8,128)(2,1)}, bf16[28,64,128]{2,1,0:T(8,128)(2,1)S(1)}, u32[]{:S(2)}) copy-start(bf16[28,64,128]{2,1,0:T(8,128)(2,1)S(1)} %collective-permute-done.32.refs_14_) | copy-start | bytes 1376260
  163.7 2.4 %collective-permute-start.29 = (bf16[28,64,128]{2,1,0:T(8,128)(2,1)S(1)}, bf16[28,64,128]{2,1,0:T(8,128)(2,1)S(1)}, u32[]{:S(2)}, u32[]{:S(2)}) collective-permute-start(bf16[28,64,128]{2,1,0:T(8,128)(2,1)S(1)} %collective-permute-done.28.refs_10_), channel_id=1, source_target_pairs={{0,16},{16,0},{32,48},{48,32},{64,80},{80,64},{96,112},{112,96},{1... | collective-permute-start | bytes 1376264 | tf_op jit(solution)/shard_map/ppermute | solution.py:61
  164.6 2.1 %copy-start.23 = (bf16[28,64,128]{2,1,0:T(8,128)(2,1)}, bf16[28,64,128]{2,1,0:T(8,128)(2,1)S(1)}, u32[]{:S(2)}) copy-start(bf16[28,64,128]{2,1,0:T(8,128)(2,1)S(1)} %collective-permute-done.25.refs_7_) | copy-start | bytes 1376260
  164.6 2.1 %collective-permute-start.33 = (bf16[28,64,128]{2,1,0:T(8,128)(2,1)S(1)}, bf16[28,64,128]{2,1,0:T(8,128)(2,1)S(1)}, u32[]{:S(2)}, u32[]{:S(2)}) collective-permute-start(bf16[28,64,128]{2,1,0:T(8,128)(2,1)S(1)} %collective-permute-done.32.refs_14_), channel_id=1, source_target_pairs={{0,16},{16,0},{32,48},{48,32},{64,80},{80,64},{96,112},{112,96},{1... | collective-permute-start | bytes 1376264 | tf_op jit(solution)/shard_map/ppermute | solution.py:61
  166.1 0.8 copy-start.24
  166.1 1.4 copy-start.16
  166.1 1.5 copy-start.17
  166.7 0.8 copy-start.25
  167.5 0.8 copy-start.18

commit v3 on v1

--- a/solution.py
+++ b/solution.py
@@ -71,17 +71,20 @@
     return lax.ppermute(array, "col", order)
 
 
-def ring(array, sent, nearest=None):
+def ring(array, sent, nearest=None, marks=None):
     size = array.shape[0]
     half = (size + 1) // 2
     behind, ahead = nearest or (sent(array, -1), sent(array, 1))
-    low = sent(lax.slice_in_dim(ahead, 0, half, axis=0), 1)
-    high = sent(lax.slice_in_dim(behind, half, size, axis=0), -1)
+    low = lax.slice_in_dim(ahead, 0, half, axis=0)
+    high = lax.slice_in_dim(behind, half, size, axis=0)
+    if marks is not None:
+        marks += [low, high]
+    low, high = sent(low, 1), sent(high, -1)
     return [(array, 0, 0), (behind, 1, 0), (ahead, 2, 0), (low, 3, 0), (high, 3, half)]
 
 
-def col_ring(array, axis):
-    return ring(array, lambda x, turn: sent_col(x, turn, axis))
+def col_ring(array, axis, marks=None):
+    return ring(array, lambda x, turn: sent_col(x, turn, axis), marks=marks)
 
 
 def row_slab(array, strips):
@@ -412,9 +415,9 @@
     expected = expected + spans * jnp.arange(groups, dtype=jnp.int32)[:, None]
     expected = jnp.pad(expected, ((0, 0), (0, 2 * block - rows_here)), constant_values=-1)
 
-    planes = [col_ring(jnp.concatenate(line, axis=0), 1 - axis) for axis, line in enumerate(lines)]
-    nearest = [x for plane in planes for x, place, _ in plane if place in (1, 2)]
-    chips, _ = lax.optimization_barrier(((own, on_1, on_2, on_3), nearest))
+    marks = []
+    planes = [col_ring(jnp.concatenate(line, axis=0), 1 - axis, marks) for axis, line in enumerate(lines)]
+    chips, _ = lax.optimization_barrier(((own, on_1, on_2, on_3), marks))
     first_slab = swapped_slab(chips)
     panels = [(plane, axis) for axis, plane in enumerate(planes)]
     squares, table = first_product(

time: 183 us -> 185 us (1.011)
  waiting for transfers between devices: 77.7 us -> 90.6 us
  starting transfers between devices: 62.2 us -> 49.4 us
  local copies, waits for them, and re-layouts: 7.92 us -> 10.9 us
    ppermute x18, starting transfers between devices: 37.7 us -> 27.1 us  [sent_row(): return lax.ppermute(array, 'row', order)]
    ppermute x18, waiting for transfers between devices: 26.4 us -> 36 us  [sent_row(): return lax.ppermute(array, 'row', order)]
    ppermute x16, waiting for transfers between devices: 51.3 us -> 54.6 us  [sent_col(): return lax.ppermute(array, 'col', order)]
    ppermute x16, starting transfers between devices: 24.6 us -> 22.3 us  [sent_col(): return lax.ppermute(array, 'col', order)]
    unnamed x59, local copies, waits for them, and re-layouts: 3.67 us -> 5.54 us
  transfers between devices with their start and end apart: 34 -> 34, of which waited for: 15 -> 16; matrix products, arithmetic and copies ran while one was open for 3% -> 3% of each run, Pallas kernels for 0% -> 0%
where the time goes in v3:
time: 185 us
  waiting for transfers between devices  90.6 us (49%)
  starting transfers between devices  49.4 us (27%)
  Pallas kernels  29.7 us (16%)
  local copies, waits for them, and re-layouts  10.9 us (6%)
  other arithmetic  3.28 us (2%)
    ppermute x16, waiting for transfers between devices, sent_col(): return lax.ppermute(array, 'col', order)  54.6 us
    ppermute x18, waiting for transfers between devices, sent_row(): return lax.ppermute(array, 'row', order)  36 us
    ppermute x18, starting transfers between devices, sent_row(): return lax.ppermute(array, 'row', order)  27.1 us
    ppermute x16, starting transfers between devices, sent_col(): return lax.ppermute(array, 'col', order)  22.3 us
    pallas_call x1, Pallas kernels, second_product(): pl.pallas_call(body, in_specs=[in_smem] * 3 + [anywhere] * len(operands)...  15 us
    pallas_call x1, Pallas kernels, first_product(): pl.pallas_call(body, in_specs=in_specs, out_specs=[in_vmem] * len(out_sha...  14.3 us
    unnamed x59, local copies, waits for them, and re-layouts  5.54 us
  transfers between devices with their start and end apart: 34, of which 16 were waited for; matrix products, arithmetic and copies ran while one was open for 3% of the time, Pallas kernels for 0%

profile of v3, /device:TPU:1, one launch (start us, length us, event | category | flops | bytes accessed | tf_op | source)
XLA Modules:
  0.0 185.1 jit_solution(3917975844099996009)
XLA Ops:
  0.6 0.8 dynamic-slice_bitcast_fusion
  1.4 1.2 copy-done
  2.6 0.4 shard_map.41
  3.0 3.6 %collective-permute-start.5 = (bf16[29,64,128]{2,1,0:T(8,128)(2,1)S(1)}, bf16[29,64,128]{2,1,0:T(8,128)(2,1)S(1)}, u32[]{:S(2)}, u32[]{:S(2)}) collective-permute-start(bf16[29,64,128]{2,1,0:T(8,128)(2,1)S(1)} %get-tuple-element.29), channel_id=1, source_target_pairs={{0,3},{1,0},{2,1},{3,2},{4,7},{5,4},{6,5},{7,6},{8,11},{9,8},{10,9... | collective-permute-start | bytes 1425416 | tf_op jit(solution)/shard_map/ppermute | solution.py:71
  6.6 2.5 %collective-permute-start.8 = (bf16[59,64,128]{2,1,0:T(8,128)(2,1)S(1)}, bf16[59,64,128]{2,1,0:T(8,128)(2,1)S(1)}, u32[]{:S(2)}, u32[]{:S(2)}) collective-permute-start(bf16[59,64,128]{2,1,0:T(8,128)(2,1)S(1)} %get-tuple-element.33.refs_1_.refs_28_), channel_id=1, source_target_pairs={{0,96},{16,112},{32,0},{48,16},{64,32},{80,48},{96,64},{112,80},{1... | collective-permute-start | bytes 2899976 | tf_op jit(solution)/shard_map/ppermute | solution.py:61
  9.1 3.8 %collective-permute-start.1 = (bf16[31,64,128]{2,1,0:T(8,128)(2,1)S(1)}, bf16[31,64,128]{2,1,0:T(8,128)(2,1)S(1)}, u32[]{:S(2)}, u32[]{:S(2)}) collective-permute-start(bf16[31,64,128]{2,1,0:T(8,128)(2,1)S(1)} %get-tuple-element.25), channel_id=1, source_target_pairs={{0,12},{1,13},{2,14},{3,15},{4,0},{5,1},{6,2},{7,3},{8,4},{9,5},{1... | collective-permute-start | bytes 1523720 | tf_op jit(solution)/shard_map/ppermute | solution.py:71
  12.9 3.3 %collective-permute-done.5 = bf16[29,64,128]{2,1,0:T(8,128)(2,1)S(1)} collective-permute-done((bf16[29,64,128]{2,1,0:T(8,128)(2,1)S(1)}, bf16[29,64,128]{2,1,0:T(8,128)(2,1)S(1)}, u32[]{:S(2)}, u32[]{:S(2)}) %collective-permute-start.5) | collective-permute-done | bytes 475168 | tf_op jit(solution)/shard_map/ppermute | solution.py:71
  16.2 3.5 %collective-permute-start.6 = (bf16[15,64,128]{2,1,0:T(8,128)(2,1)S(1)}, bf16[15,64,128]{2,1,0:T(8,128)(2,1)S(1)}, u32[]{:S(2)}, u32[]{:S(2)}) collective-permute-start(bf16[15,64,128]{2,1,0:T(8,128)(2,1)S(1)} %slice.34), channel_id=1, source_target_pairs={{0,3},{1,0},{2,1},{3,2},{4,7},{5,4},{6,5},{7,6},{8,11},{9,8},{10,9... | collective-permute-start | bytes 737288 | tf_op jit(solution)/shard_map/ppermute | solution.py:71
  19.7 1.8 collective-permute-done.4
  21.5 0.1 collective-permute-start.7
  21.6 0.9 collective-permute-done.1
  22.5 3.5 %collective-permute-start.2 = (bf16[16,64,128]{2,1,0:T(8,128)(2,1)S(1)}, bf16[16,64,128]{2,1,0:T(8,128)(2,1)S(1)}, u32[]{:S(2)}, u32[]{:S(2)}) collective-permute-start(bf16[16,64,128]{2,1,0:T(8,128)(2,1)S(1)} %slice.32), channel_id=1, source_target_pairs={{0,12},{1,13},{2,14},{3,15},{4,0},{5,1},{6,2},{7,3},{8,4},{9,5},{1... | collective-permute-start | bytes 786440 | tf_op jit(solution)/shard_map/ppermute | solution.py:71
  26.0 0.1 collective-permute-start.3
  26.1 1.6 collective-permute-done.7
  27.7 4.6 %collective-permute-done.3 = bf16[15,64,128]{2,1,0:T(8,128)(2,1)S(1)} collective-permute-done((bf16[15,64,128]{2,1,0:T(8,128)(2,1)S(1)}, bf16[15,64,128]{2,1,0:T(8,128)(2,1)S(1)}, u32[]{:S(2)}, u32[]{:S(2)}) %collective-permute-start.3) | collective-permute-done | bytes 245792 | tf_op jit(solution)/shard_map/ppermute | solution.py:71
  32.7 2.5 %collective-permute-start.11 = (bf16[124,64,128]{2,1,0:T(8,128)(2,1)S(1)}, bf16[124,64,128]{2,1,0:T(8,128)(2,1)S(1)}, u32[]{:S(2)}, u32[]{:S(2)}) collective-permute-start(bf16[124,64,128]{2,1,0:T(8,128)(2,1)S(1)} %constant_dynamic-update-slice_fusion.refs_9_.refs_16_), channel_id=1, source_target_pairs={{0,3},{1,0},{2,1},{3,2},{4,7},{5,4},{6,5},{7,6},{8,11},{9,8},{10,9... | collective-permute-start | bytes 6094856 | tf_op jit(solution)/shard_map/ppermute | solution.py:71
  35.2 0.6 collective-permute-start.9
  36.1 2.2 %collective-permute-start.13 = (bf16[116,64,128]{2,1,0:T(8,128)(2,1)S(1)}, bf16[116,64,128]{2,1,0:T(8,128)(2,1)S(1)}, u32[]{:S(2)}, u32[]{:S(2)}) collective-permute-start(bf16[116,64,128]{2,1,0:T(8,128)(2,1)S(1)} %constant_dynamic-update-slice_fusion.4.refs_14_.refs_21_), channel_id=1, source_target_pairs={{0,12},{1,13},{2,14},{3,15},{4,0},{5,1},{6,2},{7,3},{8,4},{9,5},{1... | collective-permute-start | bytes 5701640 | tf_op jit(solution)/shard_map/ppermute | solution.py:71
  38.3 15.8 %collective-permute-done.9.refs_5_ = bf16[59,64,128]{2,1,0:T(8,128)(2,1)S(1)} collective-permute-done((bf16[59,64,128]{2,1,0:T(8,128)(2,1)S(1)}, bf16[59,64,128]{2,1,0:T(8,128)(2,1)S(1)}, u32[]{:S(2)}, u32[]{:S(2)}) %collective-permute-start.9) | collective-permute-done | bytes 966688 | tf_op jit(solution)/shard_map/ppermute | solution.py:61
  54.0 1.8 collective-permute-start.10
  55.8 20.5 %collective-permute-done.13.refs_16_.refs_23_ = bf16[116,64,128]{2,1,0:T(8,128)(2,1)S(1)} collective-permute-done((bf16[116,64,128]{2,1,0:T(8,128)(2,1)S(1)}, bf16[116,64,128]{2,1,0:T(8,128)(2,1)S(1)}, u32[]{:S(2)}, u32[]{:S(2)}) %collective-permute-start.13) | collective-permute-done | bytes 1900576 | tf_op jit(solution)/shard_map/ppermute | solution.py:71
  76.3 1.1 slice.38
  77.3 2.1 %collective-permute-done.14.refs_15_.refs_22_ = bf16[116,64,128]{2,1,0:T(8,128)(2,1)S(1)} collective-permute-done((bf16[116,64,128]{2,1,0:T(8,128)(2,1)S(1)}, bf16[116,64,128]{2,1,0:T(8,128)(2,1)S(1)}, u32[]{:S(2)}, u32[]{:S(2)}) %collective-permute-start.14) | collective-permute-done | bytes 1900576 | tf_op jit(solution)/shard_map/ppermute | solution.py:71
  79.4 1.1 slice.39
  80.6 1.9 %copy-done.6 = bf16[124,64,128]{2,1,0:T(8,128)(2,1)} copy-done((bf16[124,64,128]{2,1,0:T(8,128)(2,1)}, bf16[124,64,128]{2,1,0:T(8,128)(2,1)S(1)}, u32[]{:S(2)}) %copy-start.6) | copy-done | bytes 2031640
  82.6 2.2 %pad_maximum_fusion = bf16[236,64,128]{2,1,0:T(8,128)(2,1)} fusion(bf16[59,64,128]{2,1,0:T(8,128)(2,1)S(1)} %collective-permute-done.10.refs_7_, bf16[59,64,128]{2,1,0:T(8,128)(2,1)S(1)} %collective-permute-done.9.refs_5_, bf16[59,64,128]{2,1,0:T(8,128)(2,1)S(1)} %collective-permute-done.8.refs_3_, bf16[59,64,128]{2,1,0:T(8,128)(2,1)S(1)} %get-tuple-element.33.refs_1_.refs_28_), kind=kLoop, calls=%fused_computation | loop fusion | flops 5799936 | bytes 7733248 | tf_op jit(solution)/shard_map/concatenate | solution.py:123
  84.8 3.9 %collective-permute-start.15 = (bf16[236,64,128]{2,1,0:T(8,128)(2,1)}, bf16[236,64,128]{2,1,0:T(8,128)(2,1)}, u32[]{:S(2)}, u32[]{:S(2)}) collective-permute-start(bf16[236,64,128]{2,1,0:T(8,128)(2,1)} %pad_maximum_fusion), channel_id=1, source_target_pairs={{0,16},{16,0},{32,48},{48,32},{64,80},{80,64},{96,112},{112,96},{1... | collective-permute-start | bytes 11599880 | tf_op jit(solution)/shard_map/ppermute | solution.py:61
  88.7 1.7 collective-permute-start.16
  90.4 1.1 collective-permute-start.18
  91.5 0.4 collective-permute-start.19
  91.9 0.6 broadcast.35
  92.5 0.7 reduce.3
  93.1 0.1 eq.68
  93.2 0.1 copy.4
  93.3 0.2 select_reduce_fusion
  93.5 0.1 broadcast_add_fusion
  93.6 0.6 pad.8.refs_0_
  94.2 0.7 stack.86.rows_ref
  94.9 0.7 stack.103.groups_ref
  95.6 17.3 %collective-permute-done.18.refs_17_.refs_24_ = bf16[58,64,128]{2,1,0:T(8,128)(2,1)} collective-permute-done((bf16[58,64,128]{2,1,0:T(8,128)(2,1)}, bf16[58,64,128]{2,1,0:T(8,128)(2,1)}, u32[]{:S(2)}, u32[]{:S(2)}) %collective-permute-start.18) | collective-permute-done | bytes 950304 | tf_op jit(solution)/shard_map/ppermute | solution.py:71
  112.9 2.0 %collective-permute-done.19.refs_18_.refs_25_ = bf16[58,64,128]{2,1,0:T(8,128)(2,1)} collective-permute-done((bf16[58,64,128]{2,1,0:T(8,128)(2,1)}, bf16[58,64,128]{2,1,0:T(8,128)(2,1)}, u32[]{:S(2)}, u32[]{:S(2)}) %collective-permute-start.19) | collective-permute-done | bytes 950304 | tf_op jit(solution)/shard_map/ppermute | solution.py:71
  114.9 0.5 collective-permute-done.17.refs_13_.refs_20_
  115.4 14.3 %shard_map.42 = (bf16[30,64,128]{2,1,0:T(8,128)(2,1)}, bf16[29,64,128]{2,1,0:T(8,128)(2,1)}, s32[16,128]{1,0:T(8,128)}) custom-call(s32[8]{0:T(128)} %stack.86.rows_ref, s32[16]{0:T(128)} %stack.103.groups_ref, s32[16,128]{1,0:T(8,128)} %pad.8.refs_0_, bf16[59,64,128]{2,1,0:T(8,128)(2,1)} %copy-done.1, ...), custom_call_target="tpu_custom_call" | custom-call | flops 23756537856 | bytes 35061760 | tf_op jit(solution)/shard_map/pallas_call | solution.py:304
  129.7 0.1 collective-permute-start.26
  129.8 1.5 collective-permute-start.24
  131.3 1.3 collective-permute-start.28
  132.5 2.0 %collective-permute-start.21 = (bf16[29,64,128]{2,1,0:T(8,128)(2,1)}, bf16[29,64,128]{2,1,0:T(8,128)(2,1)S(1)}, u32[]{:S(2)}, u32[]{:S(2)}) collective-permute-start(bf16[29,64,128]{2,1,0:T(8,128)(2,1)} %get-tuple-element.39.refs_2_.refs_27_), channel_id=1, source_target_pairs={{0,16},{16,0},{32,48},{48,32},{64,80},{80,64},{96,112},{112,96},{1... | collective-permute-start | bytes 1425416 | tf_op jit(solution)/shard_map/ppermute | solution.py:61
  134.5 0.2 collective-permute-start.22
  134.7 7.5 %collective-permute-done.24.refs_6_ = bf16[29,64,128]{2,1,0:T(8,128)(2,1)S(1)} collective-permute-done((bf16[29,64,128]{2,1,0:T(8,128)(2,1)}, bf16[29,64,128]{2,1,0:T(8,128)(2,1)S(1)}, u32[]{:S(2)}, u32[]{:S(2)}) %collective-permute-start.24) | collective-permute-done | bytes 475168 | tf_op jit(solution)/shard_map/ppermute | solution.py:61
  142.2 4.3 %collective-permute-start.20 = (bf16[30,64,128]{2,1,0:T(8,128)(2,1)}, bf16[30,64,128]{2,1,0:T(8,128)(2,1)S(1)}, u32[]{:S(2)}, u32[]{:S(2)}) collective-permute-start(bf16[30,64,128]{2,1,0:T(8,128)(2,1)} %get-tuple-element.38.refs_0_.refs_26_), channel_id=1, source_target_pairs={{0,16},{16,0},{32,48},{48,32},{64,80},{80,64},{96,112},{112,96},{1... | collective-permute-start | bytes 1474568 | tf_op jit(solution)/shard_map/ppermute | solution.py:61
  146.5 5.2 %collective-permute-done.28.refs_10_ = bf16[29,64,128]{2,1,0:T(8,128)(2,1)S(1)} collective-permute-done((bf16[29,64,128]{2,1,0:T(8,128)(2,1)}, bf16[29,64,128]{2,1,0:T(8,128)(2,1)S(1)}, u32[]{:S(2)}, u32[]{:S(2)}) %collective-permute-start.28) | collective-permute-done | bytes 475168 | tf_op jit(solution)/shard_map/ppermute | solution.py:61
  151.8 3.9 %collective-permute-start.25 = (bf16[29,64,128]{2,1,0:T(8,128)(2,1)S(1)}, bf16[29,64,128]{2,1,0:T(8,128)(2,1)S(1)}, u32[]{:S(2)}, u32[]{:S(2)}) collective-permute-start(bf16[29,64,128]{2,1,0:T(8,128)(2,1)S(1)} %collective-permute-done.24.refs_6_), channel_id=1, source_target_pairs={{0,16},{16,0},{32,48},{48,32},{64,80},{80,64},{96,112},{112,96},{1... | collective-permute-start | bytes 1425416 | tf_op jit(solution)/shard_map/ppermute | solution.py:61
  155.7 0.8 collective-permute-start.23
  156.5 0.1 collective-permute-start.27
  156.6 5.7 %collective-permute-done.30.refs_12_ = bf16[30,64,128]{2,1,0:T(8,128)(2,1)S(1)} collective-permute-done((bf16[30,64,128]{2,1,0:T(8,128)(2,1)S(1)}, bf16[30,64,128]{2,1,0:T(8,128)(2,1)S(1)}, u32[]{:S(2)}, u32[]{:S(2)}) %collective-permute-start.30) | collective-permute-done | bytes 491552 | tf_op jit(solution)/shard_map/ppermute | solution.py:61
  162.3 2.1 %collective-permute-start.31 = (bf16[30,64,128]{2,1,0:T(8,128)(2,1)S(1)}, bf16[30,64,128]{2,1,0:T(8,128)(2,1)S(1)}, u32[]{:S(2)}, u32[]{:S(2)}) collective-permute-start(bf16[30,64,128]{2,1,0:T(8,128)(2,1)S(1)} %collective-permute-done.30.refs_12_), channel_id=1, source_target_pairs={{0,16},{16,0},{32,48},{48,32},{64,80},{80,64},{96,112},{112,96},{1... | collective-permute-start | bytes 1474568 | tf_op jit(solution)/shard_map/ppermute | solution.py:61
  164.4 1.9 %collective-permute-start.29 = (bf16[29,64,128]{2,1,0:T(8,128)(2,1)S(1)}, bf16[29,64,128]{2,1,0:T(8,128)(2,1)S(1)}, u32[]{:S(2)}, u32[]{:S(2)}) collective-permute-start(bf16[29,64,128]{2,1,0:T(8,128)(2,1)S(1)} %collective-permute-done.28.refs_10_), channel_id=1, source_target_pairs={{0,16},{16,0},{32,48},{48,32},{64,80},{80,64},{96,112},{112,96},{1... | collective-permute-start | bytes 1425416 | tf_op jit(solution)/shard_map/ppermute | solution.py:61
  166.2 0.3 collective-permute-start.33
  166.6 1.1 collective-permute-done.29.refs_11_
  167.7 0.7 collective-permute-done.33.refs_15_
  168.4 0.1 copy-done.24
  168.5 0.7 copy-done.25
  169.2 0.7 copy-done.18
  169.9 15.0 %shard_map.43 = (bf16[64,7552]{1,0:T(8,128)(2,1)}, bf16[64,7552]{1,0:T(8,128)(2,1)}) custom-call(s32[16,128]{1,0:T(8,128)} %get-tuple-element.37.table_ref, s32[8]{0:T(128)} %stack.86.rows_ref, s32[16]{0:T(128)} %stack.103.groups_ref, bf16[30,64,128]{2,1,0:T(8,128)(2,1)} %get-tuple-element.38.refs_0_.refs_26_, bf16[30,64,128]{2,1,0:T(8,128)(2,1)} %copy-done.14, ...), custom_call_target="tpu_custom_call" | custom-call | flops 23756537856 | bytes 23461888 | tf_op jit(solution)/shard_map/pallas_call | solution.py:367
  (90 shorter events, 0.9 us)
Async XLA Ops:
  1.4 1.2 copy-start
  3.0 79.5 %copy-start.1 = (bf16[59,64,128]{2,1,0:T(8,128)(2,1)}, bf16[59,64,128]{2,1,0:T(8,128)(2,1)S(1)}, u32[]{:S(2)}) copy-start(bf16[59,64,128]{2,1,0:T(8,128)(2,1)S(1)} %get-tuple-element.33.refs_1_.refs_28_) | copy-start | bytes 2899972
  3.0 13.2 %collective-permute-start.5 = (bf16[29,64,128]{2,1,0:T(8,128)(2,1)S(1)}, bf16[29,64,128]{2,1,0:T(8,128)(2,1)S(1)}, u32[]{:S(2)}, u32[]{:S(2)}) collective-permute-start(bf16[29,64,128]{2,1,0:T(8,128)(2,1)S(1)} %get-tuple-element.29), channel_id=1, source_target_pairs={{0,3},{1,0},{2,1},{3,2},{4,7},{5,4},{6,5},{7,6},{8,11},{9,8},{10,9... | collective-permute-start | bytes 1425416 | tf_op jit(solution)/shard_map/ppermute | solution.py:71
  6.6 25.8 %collective-permute-start.8 = (bf16[59,64,128]{2,1,0:T(8,128)(2,1)S(1)}, bf16[59,64,128]{2,1,0:T(8,128)(2,1)S(1)}, u32[]{:S(2)}, u32[]{:S(2)}) collective-permute-start(bf16[59,64,128]{2,1,0:T(8,128)(2,1)S(1)} %get-tuple-element.33.refs_1_.refs_28_), channel_id=1, source_target_pairs={{0,96},{16,112},{32,0},{48,16},{64,32},{80,48},{96,64},{112,80},{1... | collective-permute-start | bytes 2899976 | tf_op jit(solution)/shard_map/ppermute | solution.py:61
  9.1 12.3 %collective-permute-start.4 = (bf16[29,64,128]{2,1,0:T(8,128)(2,1)S(1)}, bf16[29,64,128]{2,1,0:T(8,128)(2,1)S(1)}, u32[]{:S(2)}, u32[]{:S(2)}) collective-permute-start(bf16[29,64,128]{2,1,0:T(8,128)(2,1)S(1)} %get-tuple-element.29), channel_id=1, source_target_pairs={{0,1},{1,2},{2,3},{3,0},{4,5},{5,6},{6,7},{7,4},{8,9},{9,10},{10,1... | collective-permute-start | bytes 1425416 | tf_op jit(solution)/shard_map/ppermute | solution.py:71
  9.1 13.4 %collective-permute-start.1 = (bf16[31,64,128]{2,1,0:T(8,128)(2,1)S(1)}, bf16[31,64,128]{2,1,0:T(8,128)(2,1)S(1)}, u32[]{:S(2)}, u32[]{:S(2)}) collective-permute-start(bf16[31,64,128]{2,1,0:T(8,128)(2,1)S(1)} %get-tuple-element.25), channel_id=1, source_target_pairs={{0,12},{1,13},{2,14},{3,15},{4,0},{5,1},{6,2},{7,3},{8,4},{9,5},{1... | collective-permute-start | bytes 1523720 | tf_op jit(solution)/shard_map/ppermute | solution.py:71
  12.9 13.1 %collective-permute-start = (bf16[31,64,128]{2,1,0:T(8,128)(2,1)S(1)}, bf16[31,64,128]{2,1,0:T(8,128)(2,1)S(1)}, u32[]{:S(2)}, u32[]{:S(2)}) collective-permute-start(bf16[31,64,128]{2,1,0:T(8,128)(2,1)S(1)} %get-tuple-element.25), channel_id=1, source_target_pairs={{0,4},{1,5},{2,6},{3,7},{4,8},{5,9},{6,10},{7,11},{8,12},{9,13},{1... | collective-permute-start | bytes 1523720 | tf_op jit(solution)/shard_map/ppermute | solution.py:71
  16.2 11.5 %collective-permute-start.6 = (bf16[15,64,128]{2,1,0:T(8,128)(2,1)S(1)}, bf16[15,64,128]{2,1,0:T(8,128)(2,1)S(1)}, u32[]{:S(2)}, u32[]{:S(2)}) collective-permute-start(bf16[15,64,128]{2,1,0:T(8,128)(2,1)S(1)} %slice.34), channel_id=1, source_target_pairs={{0,3},{1,0},{2,1},{3,2},{4,7},{5,4},{6,5},{7,6},{8,11},{9,8},{10,9... | collective-permute-start | bytes 737288 | tf_op jit(solution)/shard_map/ppermute | solution.py:71
  21.5 6.2 %collective-permute-start.7 = (bf16[14,64,128]{2,1,0:T(8,128)(2,1)S(1)}, bf16[14,64,128]{2,1,0:T(8,128)(2,1)S(1)}, u32[]{:S(2)}, u32[]{:S(2)}) collective-permute-start(bf16[14,64,128]{2,1,0:T(8,128)(2,1)S(1)} %slice.35), channel_id=1, source_target_pairs={{0,1},{1,2},{2,3},{3,0},{4,5},{5,6},{6,7},{7,4},{8,9},{9,10},{10,1... | collective-permute-start | bytes 688136 | tf_op jit(solution)/shard_map/ppermute | solution.py:71
  22.5 9.8 %collective-permute-start.2 = (bf16[16,64,128]{2,1,0:T(8,128)(2,1)S(1)}, bf16[16,64,128]{2,1,0:T(8,128)(2,1)S(1)}, u32[]{:S(2)}, u32[]{:S(2)}) collective-permute-start(bf16[16,64,128]{2,1,0:T(8,128)(2,1)S(1)} %slice.32), channel_id=1, source_target_pairs={{0,12},{1,13},{2,14},{3,15},{4,0},{5,1},{6,2},{7,3},{8,4},{9,5},{1... | collective-permute-start | bytes 786440 | tf_op jit(solution)/shard_map/ppermute | solution.py:71
  26.0 6.3 %collective-permute-start.3 = (bf16[15,64,128]{2,1,0:T(8,128)(2,1)S(1)}, bf16[15,64,128]{2,1,0:T(8,128)(2,1)S(1)}, u32[]{:S(2)}, u32[]{:S(2)}) collective-permute-start(bf16[15,64,128]{2,1,0:T(8,128)(2,1)S(1)} %slice.33), channel_id=1, source_target_pairs={{0,4},{1,5},{2,6},{3,7},{4,8},{5,9},{6,10},{7,11},{8,12},{9,13},{1... | collective-permute-start | bytes 737288 | tf_op jit(solution)/shard_map/ppermute | solution.py:71
  32.4 50.1 %copy-start.2 = (bf16[59,64,128]{2,1,0:T(8,128)(2,1)}, bf16[59,64,128]{2,1,0:T(8,128)(2,1)S(1)}, u32[]{:S(2)}) copy-start(bf16[59,64,128]{2,1,0:T(8,128)(2,1)S(1)} %collective-permute-done.8.refs_3_) | copy-start | bytes 2899972
  32.7 44.6 %copy-start.9 = (bf16[124,64,128]{2,1,0:T(8,128)(2,1)}, bf16[124,64,128]{2,1,0:T(8,128)(2,1)S(1)}, u32[]{:S(2)}) copy-start(bf16[124,64,128]{2,1,0:T(8,128)(2,1)S(1)} %constant_dynamic-update-slice_fusion.refs_9_.refs_16_) | copy-start | bytes 6094852
  32.7 47.7 %collective-permute-start.11 = (bf16[124,64,128]{2,1,0:T(8,128)(2,1)S(1)}, bf16[124,64,128]{2,1,0:T(8,128)(2,1)S(1)}, u32[]{:S(2)}, u32[]{:S(2)}) collective-permute-start(bf16[124,64,128]{2,1,0:T(8,128)(2,1)S(1)} %constant_dynamic-update-slice_fusion.refs_9_.refs_16_), channel_id=1, source_target_pairs={{0,3},{1,0},{2,1},{3,2},{4,7},{5,4},{6,5},{7,6},{8,11},{9,8},{10,9... | collective-permute-start | bytes 6094856 | tf_op jit(solution)/shard_map/ppermute | solution.py:71
  35.2 45.4 %collective-permute-start.12 = (bf16[124,64,128]{2,1,0:T(8,128)(2,1)S(1)}, bf16[124,64,128]{2,1,0:T(8,128)(2,1)S(1)}, u32[]{:S(2)}, u32[]{:S(2)}) collective-permute-start(bf16[124,64,128]{2,1,0:T(8,128)(2,1)S(1)} %constant_dynamic-update-slice_fusion.refs_9_.refs_16_), channel_id=1, source_target_pairs={{0,1},{1,2},{2,3},{3,0},{4,5},{5,6},{6,7},{7,4},{8,9},{9,10},{10,1... | collective-permute-start | bytes 6094856 | tf_op jit(solution)/shard_map/ppermute | solution.py:71
  35.2 18.8 %collective-permute-start.9 = (bf16[59,64,128]{2,1,0:T(8,128)(2,1)S(1)}, bf16[59,64,128]{2,1,0:T(8,128)(2,1)S(1)}, u32[]{:S(2)}, u32[]{:S(2)}) collective-permute-start(bf16[59,64,128]{2,1,0:T(8,128)(2,1)S(1)} %collective-permute-done.8.refs_3_), channel_id=1, source_target_pairs={{0,96},{16,112},{32,0},{48,16},{64,32},{80,48},{96,64},{112,80},{1... | collective-permute-start | bytes 2899976 | tf_op jit(solution)/shard_map/ppermute | solution.py:61
  36.1 48.8 %copy-start.10 = (bf16[116,64,128]{2,1,0:T(8,128)(2,1)}, bf16[116,64,128]{2,1,0:T(8,128)(2,1)S(1)}, u32[]{:S(2)}) copy-start(bf16[116,64,128]{2,1,0:T(8,128)(2,1)S(1)} %constant_dynamic-update-slice_fusion.4.refs_14_.refs_21_) | copy-start | bytes 5701636
  36.1 40.2 %collective-permute-start.13 = (bf16[116,64,128]{2,1,0:T(8,128)(2,1)S(1)}, bf16[116,64,128]{2,1,0:T(8,128)(2,1)S(1)}, u32[]{:S(2)}, u32[]{:S(2)}) collective-permute-start(bf16[116,64,128]{2,1,0:T(8,128)(2,1)S(1)} %constant_dynamic-update-slice_fusion.4.refs_14_.refs_21_), channel_id=1, source_target_pairs={{0,12},{1,13},{2,14},{3,15},{4,0},{5,1},{6,2},{7,3},{8,4},{9,5},{1... | collective-permute-start | bytes 5701640 | tf_op jit(solution)/shard_map/ppermute | solution.py:71
  38.3 41.1 %collective-permute-start.14 = (bf16[116,64,128]{2,1,0:T(8,128)(2,1)S(1)}, bf16[116,64,128]{2,1,0:T(8,128)(2,1)S(1)}, u32[]{:S(2)}, u32[]{:S(2)}) collective-permute-start(bf16[116,64,128]{2,1,0:T(8,128)(2,1)S(1)} %constant_dynamic-update-slice_fusion.4.refs_14_.refs_21_), channel_id=1, source_target_pairs={{0,4},{1,5},{2,6},{3,7},{4,8},{5,9},{6,10},{7,11},{8,12},{9,13},{1... | collective-permute-start | bytes 5701640 | tf_op jit(solution)/shard_map/ppermute | solution.py:71
  54.0 28.5 %copy-start.3 = (bf16[59,64,128]{2,1,0:T(8,128)(2,1)}, bf16[59,64,128]{2,1,0:T(8,128)(2,1)S(1)}, u32[]{:S(2)}) copy-start(bf16[59,64,128]{2,1,0:T(8,128)(2,1)S(1)} %collective-permute-done.9.refs_5_) | copy-start | bytes 2899972
  54.0 28.5 %collective-permute-start.10 = (bf16[59,64,128]{2,1,0:T(8,128)(2,1)S(1)}, bf16[59,64,128]{2,1,0:T(8,128)(2,1)S(1)}, u32[]{:S(2)}, u32[]{:S(2)}) collective-permute-start(bf16[59,64,128]{2,1,0:T(8,128)(2,1)S(1)} %collective-permute-done.9.refs_5_), channel_id=1, source_target_pairs={{0,96},{16,112},{32,0},{48,16},{64,32},{80,48},{96,64},{112,80},{1... | collective-permute-start | bytes 2899976 | tf_op jit(solution)/shard_map/ppermute | solution.py:61
  76.3 4.3 %copy-start.7 = (bf16[116,64,128]{2,1,0:T(8,128)(2,1)}, bf16[116,64,128]{2,1,0:T(8,128)(2,1)S(1)}, u32[]{:S(2)}) copy-start(bf16[116,64,128]{2,1,0:T(8,128)(2,1)S(1)} %collective-permute-done.13.refs_16_.refs_23_) | copy-start | bytes 5701636
  79.4 3.1 %copy-start.8 = (bf16[116,64,128]{2,1,0:T(8,128)(2,1)}, bf16[116,64,128]{2,1,0:T(8,128)(2,1)S(1)}, u32[]{:S(2)}) copy-start(bf16[116,64,128]{2,1,0:T(8,128)(2,1)S(1)} %collective-permute-done.14.refs_15_.refs_22_) | copy-start | bytes 5701636
  80.5 2.1 %copy-start.5 = (bf16[124,64,128]{2,1,0:T(8,128)(2,1)}, bf16[124,64,128]{2,1,0:T(8,128)(2,1)S(1)}, u32[]{:S(2)}) copy-start(bf16[124,64,128]{2,1,0:T(8,128)(2,1)S(1)} %collective-permute-done.11.refs_11_.refs_18_) | copy-start | bytes 6094852
  80.6 1.9 %copy-start.6 = (bf16[124,64,128]{2,1,0:T(8,128)(2,1)}, bf16[124,64,128]{2,1,0:T(8,128)(2,1)S(1)}, u32[]{:S(2)}) copy-start(bf16[124,64,128]{2,1,0:T(8,128)(2,1)S(1)} %collective-permute-done.12.refs_10_.refs_17_) | copy-start | bytes 6094852
  82.5 9.9 %copy-start.11 = (s32[944,1]{0,1:T(1,128)S(1)}, s32[944,1]{0,1:T(1,128)}, u32[]{:S(2)}) copy-start(s32[944,1]{0,1:T(1,128)} %param.3) | copy-start | bytes 11332
  82.6 2.2 %copy-start.4 = (bf16[59,64,128]{2,1,0:T(8,128)(2,1)}, bf16[59,64,128]{2,1,0:T(8,128)(2,1)S(1)}, u32[]{:S(2)}) copy-start(bf16[59,64,128]{2,1,0:T(8,128)(2,1)S(1)} %collective-permute-done.10.refs_7_) | copy-start | bytes 2899972
  84.8 30.6 %collective-permute-start.15 = (bf16[236,64,128]{2,1,0:T(8,128)(2,1)}, bf16[236,64,128]{2,1,0:T(8,128)(2,1)}, u32[]{:S(2)}, u32[]{:S(2)}) collective-permute-start(bf16[236,64,128]{2,1,0:T(8,128)(2,1)} %pad_maximum_fusion), channel_id=1, source_target_pairs={{0,16},{16,0},{32,48},{48,32},{64,80},{80,64},{96,112},{112,96},{1... | collective-permute-start | bytes 11599880 | tf_op jit(solution)/shard_map/ppermute | solution.py:61
  88.7 26.2 %collective-permute-start.16 = (bf16[62,64,128]{2,1,0:T(8,128)(2,1)S(1)}, bf16[62,64,128]{2,1,0:T(8,128)(2,1)}, u32[]{:S(2)}, u32[]{:S(2)}) collective-permute-start(bf16[62,64,128]{2,1,0:T(8,128)(2,1)S(1)} %slice.36), channel_id=1, source_target_pairs={{0,3},{1,0},{2,1},{3,2},{4,7},{5,4},{6,5},{7,6},{8,11},{9,8},{10,9... | collective-permute-start | bytes 3047432 | tf_op jit(solution)/shard_map/ppermute | solution.py:71
  90.4 25.0 %collective-permute-start.17 = (bf16[62,64,128]{2,1,0:T(8,128)(2,1)S(1)}, bf16[62,64,128]{2,1,0:T(8,128)(2,1)}, u32[]{:S(2)}, u32[]{:S(2)}) collective-permute-start(bf16[62,64,128]{2,1,0:T(8,128)(2,1)S(1)} %slice.37), channel_id=1, source_target_pairs={{0,1},{1,2},{2,3},{3,0},{4,5},{5,6},{6,7},{7,4},{8,9},{9,10},{10,1... | collective-permute-start | bytes 3047432 | tf_op jit(solution)/shard_map/ppermute | solution.py:71
  90.4 22.5 %collective-permute-start.18 = (bf16[58,64,128]{2,1,0:T(8,128)(2,1)}, bf16[58,64,128]{2,1,0:T(8,128)(2,1)}, u32[]{:S(2)}, u32[]{:S(2)}) collective-permute-start(bf16[58,64,128]{2,1,0:T(8,128)(2,1)} %slice.38), channel_id=1, source_target_pairs={{0,12},{1,13},{2,14},{3,15},{4,0},{5,1},{6,2},{7,3},{8,4},{9,5},{1... | collective-permute-start | bytes 2850824 | tf_op jit(solution)/shard_map/ppermute | solution.py:71
  91.5 23.4 %collective-permute-start.19 = (bf16[58,64,128]{2,1,0:T(8,128)(2,1)}, bf16[58,64,128]{2,1,0:T(8,128)(2,1)}, u32[]{:S(2)}, u32[]{:S(2)}) collective-permute-start(bf16[58,64,128]{2,1,0:T(8,128)(2,1)} %slice.39), channel_id=1, source_target_pairs={{0,4},{1,5},{2,6},{3,7},{4,8},{5,9},{6,10},{7,11},{8,12},{9,13},{1... | collective-permute-start | bytes 2850824 | tf_op jit(solution)/shard_map/ppermute | solution.py:71
  129.7 16.8 %collective-permute-start.26 = (bf16[30,64,128]{2,1,0:T(8,128)(2,1)}, bf16[30,64,128]{2,1,0:T(8,128)(2,1)S(1)}, u32[]{:S(2)}, u32[]{:S(2)}) collective-permute-start(bf16[30,64,128]{2,1,0:T(8,128)(2,1)} %get-tuple-element.38.refs_0_.refs_26_), channel_id=1, source_target_pairs={{0,96},{16,112},{32,0},{48,16},{64,32},{80,48},{96,64},{112,80},{1... | collective-permute-start | bytes 1474568 | tf_op jit(solution)/shard_map/ppermute | solution.py:61
  129.8 12.4 %collective-permute-start.24 = (bf16[29,64,128]{2,1,0:T(8,128)(2,1)}, bf16[29,64,128]{2,1,0:T(8,128)(2,1)S(1)}, u32[]{:S(2)}, u32[]{:S(2)}) collective-permute-start(bf16[29,64,128]{2,1,0:T(8,128)(2,1)} %get-tuple-element.39.refs_2_.refs_27_), channel_id=1, source_target_pairs={{0,32},{16,48},{32,64},{48,80},{64,96},{80,112},{96,0},{112,16},{1... | collective-permute-start | bytes 1425416 | tf_op jit(solution)/shard_map/ppermute | solution.py:61
  131.3 20.5 %collective-permute-start.28 = (bf16[29,64,128]{2,1,0:T(8,128)(2,1)}, bf16[29,64,128]{2,1,0:T(8,128)(2,1)S(1)}, u32[]{:S(2)}, u32[]{:S(2)}) collective-permute-start(bf16[29,64,128]{2,1,0:T(8,128)(2,1)} %get-tuple-element.39.refs_2_.refs_27_), channel_id=1, source_target_pairs={{0,96},{16,112},{32,0},{48,16},{64,32},{80,48},{96,64},{112,80},{1... | collective-permute-start | bytes 1425416 | tf_op jit(solution)/shard_map/ppermute | solution.py:61
  132.5 19.2 %collective-permute-start.21 = (bf16[29,64,128]{2,1,0:T(8,128)(2,1)}, bf16[29,64,128]{2,1,0:T(8,128)(2,1)S(1)}, u32[]{:S(2)}, u32[]{:S(2)}) collective-permute-start(bf16[29,64,128]{2,1,0:T(8,128)(2,1)} %get-tuple-element.39.refs_2_.refs_27_), channel_id=1, source_target_pairs={{0,16},{16,0},{32,48},{48,32},{64,80},{80,64},{96,112},{112,96},{1... | collective-permute-start | bytes 1425416 | tf_op jit(solution)/shard_map/ppermute | solution.py:61
  134.5 21.2 %collective-permute-start.22 = (bf16[30,64,128]{2,1,0:T(8,128)(2,1)}, bf16[30,64,128]{2,1,0:T(8,128)(2,1)S(1)}, u32[]{:S(2)}, u32[]{:S(2)}) collective-permute-start(bf16[30,64,128]{2,1,0:T(8,128)(2,1)} %get-tuple-element.38.refs_0_.refs_26_), channel_id=1, source_target_pairs={{0,32},{16,48},{32,64},{48,80},{64,96},{80,112},{96,0},{112,16},{1... | collective-permute-start | bytes 1474568 | tf_op jit(solution)/shard_map/ppermute | solution.py:61
  142.2 26.9 %copy-start.19 = (bf16[29,64,128]{2,1,0:T(8,128)(2,1)}, bf16[29,64,128]{2,1,0:T(8,128)(2,1)S(1)}, u32[]{:S(2)}) copy-start(bf16[29,64,128]{2,1,0:T(8,128)(2,1)S(1)} %collective-permute-done.24.refs_6_) | copy-start | bytes 1425412
  142.2 14.2 %collective-permute-start.20 = (bf16[30,64,128]{2,1,0:T(8,128)(2,1)}, bf16[30,64,128]{2,1,0:T(8,128)(2,1)S(1)}, u32[]{:S(2)}, u32[]{:S(2)}) collective-permute-start(bf16[30,64,128]{2,1,0:T(8,128)(2,1)} %get-tuple-element.38.refs_0_.refs_26_), channel_id=1, source_target_pairs={{0,16},{16,0},{32,48},{48,32},{64,80},{80,64},{96,112},{112,96},{1... | collective-permute-start | bytes 1474568 | tf_op jit(solution)/shard_map/ppermute | solution.py:61
  146.5 22.7 %copy-start.12 = (bf16[30,64,128]{2,1,0:T(8,128)(2,1)}, bf16[30,64,128]{2,1,0:T(8,128)(2,1)S(1)}, u32[]{:S(2)}) copy-start(bf16[30,64,128]{2,1,0:T(8,128)(2,1)S(1)} %collective-permute-done.26.refs_8_) | copy-start | bytes 1474564
  146.5 15.8 %collective-permute-start.30 = (bf16[30,64,128]{2,1,0:T(8,128)(2,1)S(1)}, bf16[30,64,128]{2,1,0:T(8,128)(2,1)S(1)}, u32[]{:S(2)}, u32[]{:S(2)}) collective-permute-start(bf16[30,64,128]{2,1,0:T(8,128)(2,1)S(1)} %collective-permute-done.26.refs_8_), channel_id=1, source_target_pairs={{0,96},{16,112},{32,0},{48,16},{64,32},{80,48},{96,64},{112,80},{1... | collective-permute-start | bytes 1474568 | tf_op jit(solution)/shard_map/ppermute | solution.py:61
  151.7 16.7 %copy-start.20 = (bf16[29,64,128]{2,1,0:T(8,128)(2,1)}, bf16[29,64,128]{2,1,0:T(8,128)(2,1)S(1)}, u32[]{:S(2)}) copy-start(bf16[29,64,128]{2,1,0:T(8,128)(2,1)S(1)} %collective-permute-done.28.refs_10_) | copy-start | bytes 1425412
  151.7 12.6 %collective-permute-start.32 = (bf16[29,64,128]{2,1,0:T(8,128)(2,1)S(1)}, bf16[29,64,128]{2,1,0:T(8,128)(2,1)S(1)}, u32[]{:S(2)}, u32[]{:S(2)}) collective-permute-start(bf16[29,64,128]{2,1,0:T(8,128)(2,1)S(1)} %collective-permute-done.24.refs_6_), channel_id=1, source_target_pairs={{0,32},{16,48},{32,64},{48,80},{64,96},{80,112},{96,0},{112,16},{1... | collective-permute-start | bytes 1425416 | tf_op jit(solution)/shard_map/ppermute | solution.py:61
  151.7 3.9 %copy-start.21 = (bf16[29,64,128]{2,1,0:T(8,128)(2,1)}, bf16[29,64,128]{2,1,0:T(8,128)(2,1)S(1)}, u32[]{:S(2)}) copy-start(bf16[29,64,128]{2,1,0:T(8,128)(2,1)S(1)} %collective-permute-done.21.refs_3_) | copy-start | bytes 1425412
  151.8 14.5 %collective-permute-start.25 = (bf16[29,64,128]{2,1,0:T(8,128)(2,1)S(1)}, bf16[29,64,128]{2,1,0:T(8,128)(2,1)S(1)}, u32[]{:S(2)}, u32[]{:S(2)}) collective-permute-start(bf16[29,64,128]{2,1,0:T(8,128)(2,1)S(1)} %collective-permute-done.24.refs_6_), channel_id=1, source_target_pairs={{0,16},{16,0},{32,48},{48,32},{64,80},{80,64},{96,112},{112,96},{1... | collective-permute-start | bytes 1425416 | tf_op jit(solution)/shard_map/ppermute | solution.py:61
  155.7 13.5 %copy-start.13 = (bf16[30,64,128]{2,1,0:T(8,128)(2,1)}, bf16[30,64,128]{2,1,0:T(8,128)(2,1)S(1)}, u32[]{:S(2)}) copy-start(bf16[30,64,128]{2,1,0:T(8,128)(2,1)S(1)} %collective-permute-done.22.refs_4_) | copy-start | bytes 1474564
  155.7 12.0 %collective-permute-start.23 = (bf16[30,64,128]{2,1,0:T(8,128)(2,1)S(1)}, bf16[30,64,128]{2,1,0:T(8,128)(2,1)S(1)}, u32[]{:S(2)}, u32[]{:S(2)}) collective-permute-start(bf16[30,64,128]{2,1,0:T(8,128)(2,1)S(1)} %collective-permute-done.22.refs_4_), channel_id=1, source_target_pairs={{0,16},{16,0},{32,48},{48,32},{64,80},{80,64},{96,112},{112,96},{1... | collective-permute-start | bytes 1474568 | tf_op jit(solution)/shard_map/ppermute | solution.py:61
  156.5 12.7 %copy-start.14 = (bf16[30,64,128]{2,1,0:T(8,128)(2,1)}, bf16[30,64,128]{2,1,0:T(8,128)(2,1)S(1)}, u32[]{:S(2)}) copy-start(bf16[30,64,128]{2,1,0:T(8,128)(2,1)S(1)} %collective-permute-done.20.refs_1_) | copy-start | bytes 1474564
  156.5 11.2 %collective-permute-start.27 = (bf16[30,64,128]{2,1,0:T(8,128)(2,1)S(1)}, bf16[30,64,128]{2,1,0:T(8,128)(2,1)S(1)}, u32[]{:S(2)}, u32[]{:S(2)}) collective-permute-start(bf16[30,64,128]{2,1,0:T(8,128)(2,1)S(1)} %collective-permute-done.26.refs_8_), channel_id=1, source_target_pairs={{0,16},{16,0},{32,48},{48,32},{64,80},{80,64},{96,112},{112,96},{1... | collective-permute-start | bytes 1474568 | tf_op jit(solution)/shard_map/ppermute | solution.py:61
  162.3 6.9 %copy-start.15 = (bf16[30,64,128]{2,1,0:T(8,128)(2,1)}, bf16[30,64,128]{2,1,0:T(8,128)(2,1)S(1)}, u32[]{:S(2)}) copy-start(bf16[30,64,128]{2,1,0:T(8,128)(2,1)S(1)} %collective-permute-done.30.refs_12_) | copy-start | bytes 1474564
  162.3 6.1 %collective-permute-start.31 = (bf16[30,64,128]{2,1,0:T(8,128)(2,1)S(1)}, bf16[30,64,128]{2,1,0:T(8,128)(2,1)S(1)}, u32[]{:S(2)}, u32[]{:S(2)}) collective-permute-start(bf16[30,64,128]{2,1,0:T(8,128)(2,1)S(1)} %collective-permute-done.30.refs_12_), channel_id=1, source_target_pairs={{0,16},{16,0},{32,48},{48,32},{64,80},{80,64},{96,112},{112,96},{1... | collective-permute-start | bytes 1474568 | tf_op jit(solution)/shard_map/ppermute | solution.py:61
  164.4 4.0 %copy-start.22 = (bf16[29,64,128]{2,1,0:T(8,128)(2,1)}, bf16[29,64,128]{2,1,0:T(8,128)(2,1)S(1)}, u32[]{:S(2)}) copy-start(bf16[29,64,128]{2,1,0:T(8,128)(2,1)S(1)} %collective-permute-done.32.refs_14_) | copy-start | bytes 1425412
  164.4 3.3 %collective-permute-start.29 = (bf16[29,64,128]{2,1,0:T(8,128)(2,1)S(1)}, bf16[29,64,128]{2,1,0:T(8,128)(2,1)S(1)}, u32[]{:S(2)}, u32[]{:S(2)}) collective-permute-start(bf16[29,64,128]{2,1,0:T(8,128)(2,1)S(1)} %collective-permute-done.28.refs_10_), channel_id=1, source_target_pairs={{0,16},{16,0},{32,48},{48,32},{64,80},{80,64},{96,112},{112,96},{1... | collective-permute-start | bytes 1425416 | tf_op jit(solution)/shard_map/ppermute | solution.py:61
  166.2 2.2 %copy-start.23 = (bf16[29,64,128]{2,1,0:T(8,128)(2,1)}, bf16[29,64,128]{2,1,0:T(8,128)(2,1)S(1)}, u32[]{:S(2)}) copy-start(bf16[29,64,128]{2,1,0:T(8,128)(2,1)S(1)} %collective-permute-done.25.refs_7_) | copy-start | bytes 1425412
  166.2 2.1 %collective-permute-start.33 = (bf16[29,64,128]{2,1,0:T(8,128)(2,1)S(1)}, bf16[29,64,128]{2,1,0:T(8,128)(2,1)S(1)}, u32[]{:S(2)}, u32[]{:S(2)}) collective-permute-start(bf16[29,64,128]{2,1,0:T(8,128)(2,1)S(1)} %collective-permute-done.32.refs_14_), channel_id=1, source_target_pairs={{0,16},{16,0},{32,48},{48,32},{64,80},{80,64},{96,112},{112,96},{1... | collective-permute-start | bytes 1425416 | tf_op jit(solution)/shard_map/ppermute | solution.py:61
  167.7 0.8 copy-start.24
  167.7 1.5 copy-start.16
  167.7 1.5 copy-start.17
  168.4 0.8 copy-start.25
  169.2 0.8 copy-start.18
